TPU v7x, 128 devices: a whole 4x4x4 slice. The times are simulated.
128 devices in a mesh: section: 2 (over x_hi), row: 8 (over y, core), col: 8 (over x_lo, z).
Axes of the slice: x: 4 (x_hi: 2, x_lo: 2; x = x_hi * 2 + x_lo), y: 4, z: 4, core: 2. Of those that a mesh axis runs over, the one named last changes fastest.
Arguments:
- tokens: bfloat16 [512, 12288], P(None, 'row'), may hold values from -36 to 36
- vectors: float32 [2, 12288], P('section', 'row'), may hold values from 0.5 to 1.5
- weights: bfloat16 [2, 12288, 24576], P('section', 'row', 'col'), may hold values from -0.0546875 to 0.0546875
- cotangent: bfloat16 [512, 12288], P('col', 'row'), may hold values from -6 to 6
Outputs:
- section_outputs: bfloat16 [2, 512, 12288], P('section', 'col', 'row')
- weight_grads: bfloat16 [2, 12288, 24576], P('section', 'row', 'col')
- vector_grads: float32 [2, 12288], P('section', 'row')
All inputs are finite; a program needn't handle non-finite values.
Results may differ from a plain program's by a relative error of at most 0.0064.
Values may be sent and summed in bfloat16 or wider, within the bound.
No kernel may reach another device: no remote copies, remote signals or barrier semaphores. Data moves between devices by JAX's collectives and lax.ppermute only.
A program may use at most 128 MiB of HBM per device.

v0:
```python
import jax
import jax.numpy as jnp
from jax import lax
from jax.sharding import PartitionSpec as P

D = 12288


def passed_along(block, axis, distance):
    devices = range(lax.axis_size(axis))
    route = [(i - distance, i) for i in devices if i - distance in devices]
    return lax.ppermute(block, axis, route)


def activation(values):
    return jax.nn.gelu(values, approximate=True)


def only_when(flag, compute, out_shape):

    def nothing():
        return jnp.zeros(out_shape, jnp.float32)

    return lax.cond(flag, compute, nothing)


def local(tokens, vectors, weights, cotangent):
    second = lax.axis_index("section") == 1
    first = jnp.logical_not(second)
    weight = weights[0]
    own_vector = vectors[0]
    total_rows = tokens.shape[0]
    feature_cols = weight.shape[0]
    hidden_cols = weight.shape[1]
    col_ranks = lax.axis_size("col")
    inputs = tokens.astype(jnp.float32)
    total, squares = lax.psum((jnp.sum(inputs, axis=1), jnp.sum(inputs * inputs, axis=1)), "row")
    mean = total / D
    inv_std = lax.rsqrt(squares / D - mean * mean + 1e-05)
    centered = (inputs - mean[:, None]) * inv_std[:, None]
    normed = (centered * own_vector).astype(jnp.bfloat16)
    partial_pre = only_when(
        first,
        lambda: jnp.dot(normed, weight, preferred_element_type=jnp.float32),
        (total_rows, hidden_cols),
    )
    preact = lax.psum_scatter(partial_pre, "row", scatter_dimension=1, tiled=True)
    hidden_share = activation(preact).astype(jnp.bfloat16)
    token_block = lax.all_to_all(hidden_share, "row", split_axis=0, concat_axis=1, tiled=True)
    arrived = passed_along(token_block, "section", 1)
    hidden_full = lax.all_gather(arrived, "row", axis=0, tiled=True)

    def compute():
        return lax.dot_general(
            hidden_full, weight, (((1,), (1,)), ((), ())), preferred_element_type=jnp.float32
        )

    summed = lax.psum_scatter(
        only_when(second, compute, (lax.axis_size("col") * cotangent.shape[0], feature_cols)),
        "col",
        scatter_dimension=0,
        tiled=True,
    )
    output = (summed + own_vector).astype(jnp.bfloat16)
    cot_full = lax.all_gather(cotangent, "col", axis=0, tiled=True)
    bias_grad = jnp.sum(cot_full.astype(jnp.float32), axis=0)

    def down_grad():
        return lax.dot_general(
            cot_full, hidden_full, (((0,), (0,)), ((), ())), preferred_element_type=jnp.float32
        )

    grad_down = only_when(second, down_grad, (feature_cols, hidden_cols)).astype(jnp.bfloat16)
    partial_grad = only_when(
        second,
        lambda: jnp.dot(cot_full, weight, preferred_element_type=jnp.float32),
        (total_rows, hidden_cols),
    )
    grad_hidden = lax.psum_scatter(partial_grad, "row", scatter_dimension=1, tiled=True).astype(
        jnp.bfloat16
    )
    returned = passed_along(grad_hidden, "section", -1)
    _, pullback = jax.vjp(activation, preact)
    grad_pre = pullback(returned.astype(jnp.float32))[0].astype(jnp.bfloat16)
    grad_pre_full = lax.all_gather(grad_pre, "row", axis=1, tiled=True)

    def up_grad():
        return lax.dot_general(
            normed, grad_pre_full, (((0,), (0,)), ((), ())), preferred_element_type=jnp.float32
        )

    grad_up = only_when(first, up_grad, (feature_cols, hidden_cols)).astype(jnp.bfloat16)
    block_rows = total_rows // col_ranks

    def compute():
        return lax.dot_general(
            grad_pre_full, weight, (((1,), (1,)), ((), ())), preferred_element_type=jnp.float32
        )

    grad_normed = lax.psum_scatter(
        only_when(first, compute, (lax.axis_size("col") * block_rows, feature_cols)),
        "col",
        scatter_dimension=0,
        tiled=True,
    )
    first_row = lax.axis_index("col") * block_rows
    centered_block = lax.dynamic_slice_in_dim(centered, first_row, block_rows, 0)
    inv_std_block = lax.dynamic_slice_in_dim(inv_std, first_row, block_rows, 0)
    grad_centered = grad_normed * own_vector
    mean_grad, slope_grad = lax.psum(
        (jnp.sum(grad_centered, axis=1), jnp.sum(grad_centered * centered_block, axis=1)), "row"
    )
    grad_inputs = (
        inv_std_block[:, None]
        * (grad_centered - mean_grad[:, None] / D - centered_block * (slope_grad[:, None] / D))
    ).astype(jnp.bfloat16)
    gain_grad = lax.psum(jnp.sum(grad_normed * centered_block, axis=0), "col")
    section_outputs = jnp.where(second, output, grad_inputs)[None]
    weight_grads = jnp.where(second, grad_down, grad_up)[None]
    vector_grads = jnp.where(second, bias_grad, gain_grad)[None]
    return (section_outputs, weight_grads, vector_grads)


def solution(mesh):
    in_specs = (P(None, "row"), P("section", "row"), P("section", "row", "col"), P("col", "row"))
    out_specs = (P("section", "col", "row"), P("section", "row", "col"), P("section", "row"))
    return jax.shard_map(local, mesh=mesh, in_specs=in_specs, out_specs=out_specs, check_vma=False)
```

profile of v0, /device:TPU:0, one launch (start us, length us, event | category | flops | bytes accessed | tf_op | source)
XLA Modules:
  0.0 314.3 jit_solution(7412380685253288023)
XLA Ops:
  7.2 0.7 all-gather.6.cloned.1.call-update
  8.0 44.9 %all-gather.6.cloned.1.call-done = bf16[512,1536]{1,0:T(8,128)(2,1)} async-done(((bf16[64,1536]{1,0:T(8,128)(2,1)}), bf16[512,1536]{1,0:T(8,128)(2,1)}) %all-gather.6.cloned.1.call-update) | async-done | bytes 1572880 | tf_op jit(solution)/shard_map/all_gather | solution.py:65
  52.9 3.5 %conditional.8 = (f32[512,3072]{1,0:T(8,128)}) conditional(s32[]{:T(128)} %convert_element_type.49, () %tuple.53, (bf16[512,1536]{1,0:T(8,128)(2,1)}, bf16[1536,3072]{1,0:T(8,128)(2,1)}) %tuple.96), branch_computations={%region_10.0_spmd, %region_11.0_spmd} | conditional | flops 4831838208 | bytes 17301512 | solution.py:24
  52.9 3.5 %broadcast.42 = f32[512,3072]{1,0:T(8,128)} broadcast(f32[]{:T(128)} %constant.19.clone), dimensions={} | broadcast | bytes 6291460 | tf_op jit(solution)/shard_map/broadcast.13
  56.4 0.0 reduce-scatter.5.cloned.1.call-start
  56.4 0.6 copy-done.6
  57.1 0.7 copy-done.2
  57.8 0.6 convert_reduce_fusion
  58.3 12.4 %all-reduce.1 = (f32[512]{0:T(512)S(1)}, f32[512]{0:T(512)S(1)}) all-reduce(f32[512]{0:T(512)S(1)} %get-tuple-element.62, f32[512]{0:T(512)S(1)} %get-tuple-element.61), channel_id=1, replica_groups=mesh['section'=2,'row'=8,'col'=8] {'row'}, use_global_device_ids=true, to_apply=%region_3.0 | all-reduce | flops 1024 | bytes 8192 | tf_op jit(solution)/shard_map/psum | solution.py:37
  70.8 2.2 fusion
  73.0 1.1 copy-done.4
  74.1 10.7 %conditional.6 = (f32[512,3072]{1,0:T(8,128)}) conditional(s32[]{:T(128)} %convert_element_type.50, () %tuple.49, (bf16[512,1536]{1,0:T(8,128)(2,1)S(1)}, bf16[1536,3072]{1,0:T(8,128)(2,1)}) %tuple.97), branch_computations={%region_4.0_spmd, %region_5.0_spmd} | conditional | flops 4831838208 | bytes 17301512 | solution.py:24
  74.1 10.7 %fusion.14 = f32[512,3072]{1,0:T(8,128)} fusion(bf16[512,1536]{1,0:T(8,128)(2,1)S(1)} %get-tuple-element.40, bf16[1536,3072]{1,0:T(8,128)(2,1)} %get-tuple-element.42), kind=kOutput, calls=%fused_computation.37 | convolution fusion | flops 4831838208 | bytes 17301504 | tf_op jit(solution)/shard_map/cond/branch_1_fun/dot_general | solution.py:44
  84.9 0.0 all-gather.8.cloned.1.call-start
  84.9 19.5 %reduce-scatter.9.cloned.1.call-done = f32[512,384]{1,0:T(8,128)} async-done(((f32[512,3072]{1,0:T(8,128)}), f32[512,384]{1,0:T(8,128)}) %reduce-scatter.9.cloned.1.call-update) | async-done | bytes 786448 | tf_op jit(solution)/shard_map/reduce_scatter | solution.py:79
  104.4 1.2 convert_element_type.55
  105.6 1.3 collective-permute-start.1
  106.9 42.2 %reduce-scatter.5.cloned.1.call-done = f32[512,384]{1,0:T(8,128)} async-done(((f32[512,3072]{1,0:T(8,128)}), f32[512,384]{1,0:T(8,128)}) %reduce-scatter.5.cloned.1.call-update) | async-done | bytes 786448 | tf_op jit(solution)/shard_map/reduce_scatter | solution.py:47
  149.1 2.5 fusion.4
  151.6 0.0 all-gather.4.cloned.1.call-start
  151.6 11.4 %all_to_all.19 = bf16[8,64,384]{2,1,0:T(8,128)(2,1)S(1)} all-to-all(bf16[8,64,384]{2,1,0:T(8,128)(2,1)S(1)} %bitcast.22), channel_id=1, replica_groups=mesh['section'=2,'row'=8,'col'=8] {'row'}, dimensions={0} | all-to-all | bytes 786432 | tf_op jit(solution)/shard_map/all_to_all | solution.py:49
  163.1 4.9 %collective-permute-start = (bf16[64,3072]{1,0:T(8,128)(2,1)S(1)}, bf16[64,3072]{1,0:T(8,128)(2,1)S(1)}, u32[]{:S(2)}, u32[]{:S(2)}) collective-permute-start(bf16[64,3072]{1,0:T(8,128)(2,1)S(1)} %bitcast.23), channel_id=1, source_target_pairs={{0,64},{1,65},{2,66},{3,67},{4,68},{5,69},{6,70},{7,71},{8,72},{9,... | collective-permute-start | bytes 1179656 | tf_op jit(solution)/shard_map/ppermute | solution.py:12
  168.0 8.1 %collective-permute-done = bf16[64,3072]{1,0:T(8,128)(2,1)S(1)} collective-permute-done((bf16[64,3072]{1,0:T(8,128)(2,1)S(1)}, bf16[64,3072]{1,0:T(8,128)(2,1)S(1)}, u32[]{:S(2)}, u32[]{:S(2)}) %collective-permute-start) | collective-permute-done | bytes 393248 | tf_op jit(solution)/shard_map/ppermute | solution.py:12
  176.2 0.8 copy-done.5
  177.0 0.0 reduce-scatter.11.cloned.1.call-start
  177.0 2.2 all-gather.8.cloned.1.call-done
  179.2 8.6 %conditional.9 = (f32[512,1536]{1,0:T(8,128)S(1)}) conditional(s32[]{:T(128)} %convert_element_type.50, () %tuple.52, (bf16[512,3072]{1,0:T(8,128)(2,1)}, bf16[1536,3072]{1,0:T(8,128)(2,1)}) %tuple.98), branch_computations={%region_13.0_spmd, %region_14.0_spmd} | conditional | flops 4831838208 | bytes 15728648 | solution.py:24
  179.2 8.6 %fusion.17 = f32[512,1536]{1,0:T(8,128)S(1)} fusion(bf16[512,3072]{1,0:T(8,128)(2,1)} %get-tuple-element.50, bf16[1536,3072]{1,0:T(8,128)(2,1)} %get-tuple-element.51), kind=kOutput, calls=%fused_computation.40 | convolution fusion | flops 4831838208 | bytes 15728640 | tf_op jit(solution)/shard_map/cond/branch_1_fun/dot_general | solution.py:96
  187.9 1.6 copy-done
  189.5 0.0 reduce-scatter.7.cloned.1.call-start
  189.6 19.0 %all-gather.4.cloned.1.call-done = bf16[512,3072]{1,0:T(8,128)(2,1)} async-done(((bf16[64,3072]{1,0:T(8,128)(2,1)}), bf16[512,3072]{1,0:T(8,128)(2,1)}) %all-gather.4.cloned.1.call-update) | async-done | bytes 3145744 | tf_op jit(solution)/shard_map/all_gather | solution.py:51
  208.5 0.6 conditional.7
  208.6 0.4 broadcast.41
  209.1 1.7 copy-done.1
  210.8 0.1 dynamic_slice.6
  210.9 1.7 convert_reduce_fusion.1
  212.6 9.6 %conditional.11 = (bf16[1536,3072]{1,0:T(8,128)(2,1)}) conditional(s32[]{:T(128)} %convert_element_type.50, () %tuple.58, (bf16[512,1536]{1,0:T(8,128)(2,1)}, bf16[512,3072]{1,0:T(8,128)(2,1)}) %tuple.95), branch_computations={%region_22.0_spmd, %region_23.0_spmd} | conditional | flops 4836556800 | bytes 14155784 | solution.py:24
  212.6 9.6 %convolution_convert_fusion.1 = bf16[1536,3072]{1,0:T(8,128)(2,1)} fusion(bf16[512,1536]{1,0:T(8,128)(2,1)} %get-tuple-element.54, bf16[512,3072]{1,0:T(8,128)(2,1)} %get-tuple-element.55), kind=kOutput, calls=%fused_computation.1 | convolution fusion | flops 4836556800 | bytes 14155776 | tf_op jit(solution)/shard_map/cond/branch_1_fun/dot_general | solution.py:88
  222.2 4.9 %conditional.10 = (bf16[1536,3072]{1,0:T(8,128)(2,1)}) conditional(s32[]{:T(128)} %convert_element_type.49, () %tuple.56, (bf16[512,1536]{1,0:T(8,128)(2,1)S(1)}, bf16[512,3072]{1,0:T(8,128)(2,1)}) %tuple.94), branch_computations={%region_20.0_spmd, %region_21.0_spmd} | conditional | flops 4836556800 | bytes 14155784 | solution.py:24
  222.2 4.9 %broadcast.44 = bf16[1536,3072]{1,0:T(8,128)(2,1)} broadcast(bf16[]{:T(256)} %constant.25.clone), dimensions={} | broadcast | bytes 9437186 | tf_op jit(solution)/shard_map/broadcast.25
  227.1 9.3 %select_bitcast_fusion = bf16[1,1536,3072]{2,1,0:T(8,128)(2,1)} fusion(bf16[1536,3072]{1,0:T(8,128)(2,1)} %get-tuple-element.80, bf16[1536,3072]{1,0:T(8,128)(2,1)} %get-tuple-element.81, pred[]{:T(512)S(6)} %eq.3), kind=kLoop, calls=%fused_computation.2 | loop fusion | flops 4718592 | bytes 28311552 | tf_op jit(solution)/shard_map/broadcast_in_dim | solution.py:119
  236.5 20.5 %reduce-scatter.11.cloned.1.call-done = f32[64,1536]{1,0:T(8,128)} async-done(((f32[512,1536]{1,0:T(8,128)}), f32[64,1536]{1,0:T(8,128)}) %reduce-scatter.11.cloned.1.call-update) | async-done | bytes 393232 | tf_op jit(solution)/shard_map/reduce_scatter | solution.py:100
  257.0 1.3 multiply_reduce_fusion
  258.3 19.0 %psum.39 = f32[1536]{0:T(1024)S(1)} all-reduce(f32[1536]{0:T(1024)S(1)} %get-tuple-element.59), channel_id=1, replica_groups=mesh['section'=2,'row'=8,'col'=8] {'col'}, use_global_device_ids=true, to_apply=%region_26.0 | all-reduce | flops 1536 | bytes 12288 | tf_op jit(solution)/shard_map/psum | solution.py:117
  277.4 0.6 broadcast_in_dim.16
  278.0 12.8 %all-reduce = (f32[64]{0:T(128)S(1)}, f32[64]{0:T(128)S(1)}) all-reduce(f32[64]{0:T(128)S(1)} %get-tuple-element.60, f32[64]{0:T(128)S(1)} %get-tuple-element.63), channel_id=1, replica_groups=mesh['section'=2,'row'=8,'col'=8] {'row'}, use_global_device_ids=true, to_apply=%region_19.0 | all-reduce | flops 128 | bytes 1024 | tf_op jit(solution)/shard_map/psum | solution.py:110
  290.8 14.6 %reduce-scatter.7.cloned.1.call-done = f32[64,1536]{1,0:T(8,128)} async-done(((f32[512,1536]{1,0:T(8,128)}), f32[64,1536]{1,0:T(8,128)}) %reduce-scatter.7.cloned.1.call-update) | async-done | bytes 393232 | tf_op jit(solution)/shard_map/reduce_scatter | solution.py:58
  305.4 2.1 fusion.13
  (22 shorter events, 0.3 us)
Async XLA Ops:
  7.2 45.7 %all-gather.6.cloned.1.call-start = ((), (), s32[]{:S(2)}) async-start(), calls=%async_computation.8 | async-start | bytes 1769472 | tf_op jit(solution)/shard_map/all_gather | solution.py:65
  7.9 96.5 %reduce-scatter.9.cloned.1.call-start = ((), (), s32[]{:S(2)}) async-start(), calls=%async_computation.9 | async-start | bytes 7077888 | tf_op jit(solution)/shard_map/reduce_scatter | solution.py:79
  56.3 0.7 copy-start.6
  56.3 1.4 copy-start.2
  56.4 92.7 %reduce-scatter.5.cloned.1.call-start = ((), (), s32[]{:S(2)}) async-start(), calls=%async_computation.5 | async-start | bytes 7077888 | tf_op jit(solution)/shard_map/reduce_scatter | solution.py:47
  73.0 1.1 copy-start.4
  84.9 94.3 %all-gather.8.cloned.1.call-start = ((), (), s32[]{:S(2)}) async-start(), calls=%async_computation.10 | async-start | bytes 3538944 | tf_op jit(solution)/shard_map/all_gather | solution.py:85
  105.6 43.5 %collective-permute-start.1 = (bf16[512,384]{1,0:T(8,128)(2,1)S(1)}, bf16[512,384]{1,0:T(8,128)(2,1)S(1)}, u32[]{:S(2)}, u32[]{:S(2)}) collective-permute-start(bf16[512,384]{1,0:T(8,128)(2,1)S(1)} %convert_element_type.55), channel_id=1, source_target_pairs={{64,0},{65,1},{66,2},{67,3},{68,4},{69,5},{70,6},{71,7},{72,8},{73... | collective-permute-start | bytes 1179656 | tf_op jit(solution)/shard_map/ppermute | solution.py:12
  151.6 57.0 %all-gather.4.cloned.1.call-start = ((), (), s32[]{:S(2)}) async-start(), calls=%async_computation.6 | async-start | bytes 3538944 | tf_op jit(solution)/shard_map/all_gather | solution.py:51
  163.1 13.0 %collective-permute-start = (bf16[64,3072]{1,0:T(8,128)(2,1)S(1)}, bf16[64,3072]{1,0:T(8,128)(2,1)S(1)}, u32[]{:S(2)}, u32[]{:S(2)}) collective-permute-start(bf16[64,3072]{1,0:T(8,128)(2,1)S(1)} %bitcast.23), channel_id=1, source_target_pairs={{0,64},{1,65},{2,66},{3,67},{4,68},{5,69},{6,70},{7,71},{8,72},{9,... | collective-permute-start | bytes 1179656 | tf_op jit(solution)/shard_map/ppermute | solution.py:12
  176.2 0.8 copy-start.5
  177.0 80.1 %reduce-scatter.11.cloned.1.call-start = ((), (), s32[]{:S(2)}) async-start(), calls=%async_computation.11 | async-start | bytes 3538944 | tf_op jit(solution)/shard_map/reduce_scatter | solution.py:100
  187.8 1.6 copy-start
  189.5 115.9 %reduce-scatter.7.cloned.1.call-start = ((), (), s32[]{:S(2)}) async-start(), calls=%async_computation.7 | async-start | bytes 3538944 | tf_op jit(solution)/shard_map/reduce_scatter | solution.py:58
  209.1 1.7 copy-start.1
  212.6 9.6 %copy-start.3 = (bf16[512,1536]{1,0:T(8,128)(2,1)S(1)}, bf16[512,1536]{1,0:T(8,128)(2,1)}, u32[]{:S(2)}) copy-start(bf16[512,1536]{1,0:T(8,128)(2,1)} %all-gather.6.cloned.1.call-done) | copy-start | bytes 4718596
Sparse Core Ops, SparseCore 0:
  9.6 43.1 all-gather.5
  56.5 47.8 reduce-scatter.8
  106.8 42.2 reduce-scatter.4
  151.7 27.4 all-gather.7
  180.7 27.7 all-gather.3
  210.8 46.1 reduce-scatter.10
  259.4 45.9 reduce-scatter.6
where the time goes:
time: 315 us; the launch traced here: 314 us
  waiting for transfers between devices  172 us (55%)
  blocking collectives  55.7 us (18%)
  matrix products  29 us (9%)
  other arithmetic  20.9 us (7%)
  local copies, waits for them, and re-layouts  16 us (5%)
  between operations  14.2 us (5%)
  starting transfers between devices  6.46 us (2%)
    all_gather x1, waiting for transfers between devices, local(): cot_full = lax.all_gather(cotangent, 'col', axis=0, tiled=True)  44.9 us
    reduce_scatter x1, waiting for transfers between devices, local(): lax.psum_scatter(partial_pre, 'row', scatter_dimension=1, tiled=True)  42.2 us
    reduce_scatter x1, waiting for transfers between devices, local(): lax.psum_scatter(only_when(first, compute, (lax.axis_size('col') * block_...  20.5 us
    reduce_scatter x1, waiting for transfers between devices, local(): lax.psum_scatter(partial_grad, 'row', scatter_dimension=1, tiled=True)  19.5 us
    psum x1, blocking collectives, local(): gain_grad = lax.psum(jnp.sum(grad_normed * centered_block, axis=0), 'col')  19 us
    all_gather x1, waiting for transfers between devices, local(): hidden_full = lax.all_gather(arrived, 'row', axis=0, tiled=True)  19 us
    reduce_scatter x1, waiting for transfers between devices, local(): lax.psum_scatter(only_when(second, compute, (lax.axis_size('col') * cotan...  14.6 us
    psum x1, blocking collectives, local(): lax.psum((jnp.sum(grad_centered, axis=1), jnp.sum(grad_centered * centere...  12.8 us
  transfers between devices with their start and end apart: 9, of which 8 were waited for; matrix products, arithmetic and copies ran while one was open for 16% of the time, Pallas kernels for 0%

commit v1 on v0

v1 whole, which is shorter than its diff:
```python
import jax
import jax.numpy as jnp
from jax import lax
from jax.sharding import PartitionSpec as P

D = 12288
F32 = jnp.float32
BF16 = jnp.bfloat16
CHUNKS = 1
Y_ORDERS = ((1, 3), (3, 1))
COL_ORDERS = ((1, 3, 4), (3, 4, 1), (4, 1, 3))


def exchange(block, axis, mask):
    ranks = range(lax.axis_size(axis))
    return lax.ppermute(block, axis, [(i, i ^ mask) for i in ranks])


def activation(values):
    return jax.nn.gelu(values, approximate=True)


def span(masks):
    found = [0]
    for mask in masks:
        found = found + [mask ^ f for f in found]
    return found


def scattered(block_of, send, order):
    kept = {r: block_of(r) for r in span(order)}
    for step, mask in enumerate(order):
        rest = span(order[step + 1 :])
        out = jnp.stack([kept[mask ^ q].astype(BF16) for q in rest])
        got = send(out, mask)
        kept = {q: kept[q] + got[i].astype(F32) for i, q in enumerate(rest)}
    return kept[0]


def gathered(piece, send, order):
    held = piece[None]
    relative = [0]
    for mask in order:
        held = jnp.concatenate([held, send(held, mask)])
        relative = relative + [mask ^ r for r in relative]
    return relative, held


def local(tokens, vectors, weights, cotangent):
    second = lax.axis_index("section") == 1
    row = lax.axis_index("row")
    col = lax.axis_index("col")
    core, y = row % 2, row // 2
    weight = weights[0]
    own_vector = vectors[0]
    features, hidden = weight.shape
    n = cotangent.shape[0] // CHUNKS

    def by_y(block, mask):
        return exchange(block, "row", 2 * mask)

    def by_col(block, mask):
        return exchange(block, "col", mask)

    def by_core(block):
        return exchange(block, "row", 1)

    def summed_over_y(values):
        return values + by_y(values, 1) + by_y(values, 2) + by_y(values, 3)

    def place(block):
        return ((block % 2) ^ core) * 4 + block // 2

    def own_core_first(values):
        parts = values.reshape(4, 2, CHUNKS, n, -1)
        mine = lax.dynamic_index_in_dim(parts, core, 1, keepdims=False)
        other = lax.dynamic_index_in_dim(parts, 1 - core, 1, keepdims=False)
        return jnp.stack([mine, other]).transpose(2, 0, 1, 3, 4).reshape(CHUNKS * 8 * n, -1)

    def over_row(sums):
        parts = sums.reshape(2, CHUNKS, 2, 4 * n)
        got = by_core(sums.reshape(8, 128)).reshape(2, CHUNKS, 2, 4 * n)
        return summed_over_y((parts + got[:, :, ::-1]).reshape(8, 128)).reshape(2, CHUNKS * 8 * n)

    cot_chunks = []
    for j in range(CHUNKS):
        piece = cotangent[j * n : (j + 1) * n]
        whole = jnp.zeros((8, n, features), BF16)
        width = features // 3
        for i, order in enumerate(COL_ORDERS):
            relative, held = gathered(piece[:, i * width : (i + 1) * width], by_col, order)
            for k, r in enumerate(relative):
                whole = lax.dynamic_update_slice(
                    whole, held[k : k + 1], (place(col ^ r), 0, i * width)
                )
        cot_chunks.append(whole.reshape(8 * n, features))
    cot_full = jnp.concatenate(cot_chunks)
    bias_grad = jnp.sum(cot_full.astype(F32), axis=0)

    inputs = own_core_first(tokens).astype(F32)
    sums = over_row(jnp.stack([jnp.sum(inputs, axis=1), jnp.sum(inputs * inputs, axis=1)]))
    mean, square = sums[0] / D, sums[1] / D
    inv_std = lax.rsqrt(square - mean * mean + 1e-05)
    centered = (inputs - mean[:, None]) * inv_std[:, None]
    normed = (centered * own_vector).astype(BF16)
    left = jnp.where(second, cot_full, normed)

    width = hidden // 2
    rights, products = [], []
    for j in range(CHUNKS):
        chunk = left[j * 8 * n : (j + 1) * 8 * n]
        sent = jnp.dot(chunk[4 * n :], weight, preferred_element_type=F32).astype(BF16)
        got = by_core(sent)
        kept = jnp.dot(chunk[: 4 * n], weight, preferred_element_type=F32)
        both = (kept + got.astype(F32)).reshape(4, n, hidden)
        pieces = []
        for h, order in enumerate(Y_ORDERS):
            part = both[:, :, h * width : (h + 1) * width]
            mine = scattered(
                lambda r: lax.dynamic_index_in_dim(part, y ^ r, 0, keepdims=False), by_y, order
            )
            values, pullback = jax.vjp(activation, mine)
            leaving = jnp.where(second, mine, values).astype(BF16)
            arrived = exchange(leaving, "section", 1)
            grad_pre = pullback(arrived.astype(F32))[0].astype(BF16)
            pieces.append(jnp.where(second, arrived, grad_pre))
        near = jnp.zeros((4, n, hidden), BF16)
        for h, order in enumerate(Y_ORDERS):
            relative, held = gathered(pieces[h], by_y, order)
            for k, r in enumerate(relative):
                near = lax.dynamic_update_slice(near, held[k : k + 1], (y ^ r, 0, h * width))
        near = near.reshape(4 * n, hidden)
        far = by_core(near)
        contract = (((1,), (1,)), ((), ()))
        products.append(lax.dot_general(near, weight, contract, preferred_element_type=F32))
        products.append(lax.dot_general(far, weight, contract, preferred_element_type=F32))
        rights += [near, far]

    product = jnp.concatenate(products)
    width = features // 3
    summed = []
    for j in range(CHUNKS):
        blocks = product[j * 8 * n : (j + 1) * 8 * n].reshape(8, n, features)
        thirds = []
        for i, order in enumerate(COL_ORDERS):
            part = blocks[:, :, i * width : (i + 1) * width]
            thirds.append(
                scattered(
                    lambda r: lax.dynamic_index_in_dim(part, place(col ^ r), 0, keepdims=False),
                    by_col,
                    order,
                )
            )
        summed.append(jnp.concatenate(thirds, axis=1))
    summed = jnp.concatenate(summed)

    scaled = product * own_vector
    sums = over_row(jnp.stack([jnp.sum(scaled, axis=1), jnp.sum(scaled * centered, axis=1)]))
    gain_part = jnp.sum(product * centered, axis=0)
    packed = jnp.concatenate([sums.reshape(8, 128), gain_part.reshape(-1, 128)])
    packed = packed + by_col(packed, 1) + by_col(packed, 2) + by_col(packed, 3)
    packed = packed + by_col(packed, 4)
    sums, gain_grad = packed[:8].reshape(2, -1), packed[8:].reshape(-1)

    right = jnp.concatenate(rights)
    weight_grads = lax.dot_general(
        left, right, (((0,), (0,)), ((), ())), preferred_element_type=F32
    ).astype(BF16)

    def own_tokens(values):
        parts = values.reshape((CHUNKS, 8, n) + values.shape[1:])
        found = lax.dynamic_index_in_dim(parts, place(col), 1, keepdims=False)
        return found.reshape((CHUNKS * n,) + values.shape[1:])

    mean_grad, slope_grad = own_tokens(sums[0]) / D, own_tokens(sums[1]) / D
    grad_inputs = own_tokens(inv_std)[:, None] * (
        summed * own_vector - mean_grad[:, None] - own_tokens(centered) * slope_grad[:, None]
    )
    output = summed + own_vector
    section_outputs = jnp.where(second, output, grad_inputs).astype(BF16)[None]
    vector_grads = jnp.where(second, bias_grad, gain_grad)[None]
    return (section_outputs, weight_grads[None], vector_grads)


def solution(mesh):
    in_specs = (P(None, "row"), P("section", "row"), P("section", "row", "col"), P("col", "row"))
    out_specs = (P("section", "col", "row"), P("section", "row", "col"), P("section", "row"))
    return jax.shard_map(local, mesh=mesh, in_specs=in_specs, out_specs=out_specs, check_vma=False)
```

time: 315 us -> 198 us (0.63)
  waiting for transfers between devices: 172 us -> 56.7 us
  blocking collectives: 55.7 us -> 0 us
  starting transfers between devices: 6.46 us -> 51.8 us
  between operations: 14.2 us -> 1.42 us
  other arithmetic: 20.9 us -> 31.6 us
  local copies, waits for them, and re-layouts: 16 us -> 25 us
    reduce_scatter x4 -> x0, waiting for transfers between devices: 96.8 us -> none  [the longest x1 42.2 us: local(): lax.psum_scatter(partial_pre, 'row', scatter_dimension=1, tiled=True)]
    all_gather x3 -> x0, waiting for transfers between devices: 66.1 us -> none  [the longest x1 44.9 us: local(): cot_full = lax.all_gather(cotangent, 'col', axis=0, tiled=True)]
    ppermute x2 -> x42, waiting for transfers between devices: 8.14 us -> 56.7 us  [exchange(): return lax.ppermute(block, axis, [(i, i ^ mask) for i in ranks])]
    ppermute x2 -> x42, starting transfers between devices: 6.18 us -> 51.8 us  [exchange(): return lax.ppermute(block, axis, [(i, i ^ mask) for i in ranks])]
    psum x3 -> x0, blocking collectives: 44.2 us -> none  [the longest x1 19 us: local(): gain_grad = lax.psum(jnp.sum(grad_normed * centered_block, axis=0), 'col')]
    all_to_all x1 -> x0, blocking collectives: 11.4 us -> none  [local(): lax.all_to_all(hidden_share, 'row', split_axis=0, concat_axis=1, tiled=True)]
    broadcast_in_dim x2 -> x0, other arithmetic: 11.4 us -> none  [the longest x1 9.34 us: local(): weight_grads = jnp.where(second, grad_down, grad_up)[None]]
    convert_element_type x2 -> x12, other arithmetic: 3.66 us -> 10.5 us  [the longest x8 6.36 us: scattered(): out = jnp.stack([kept[mask ^ q].astype(BF16) for q in rest])]
  transfers between devices with their start and end apart: 9 -> 42, of which waited for: 8 -> 20; matrix products, arithmetic and copies ran while one was open for 16% -> 29% of each run, Pallas kernels for 0% -> 0%
where the time goes in v1:
time: 198 us; the launch traced here: 197 us
  waiting for transfers between devices  56.7 us (29%)
  starting transfers between devices  51.8 us (26%)
  other arithmetic  31.6 us (16%)
  matrix products  30.4 us (15%)
  local copies, waits for them, and re-layouts  25 us (13%)
    ppermute x42, waiting for transfers between devices, exchange(): return lax.ppermute(block, axis, [(i, i ^ mask) for i in ranks])  56.7 us
    ppermute x42, starting transfers between devices, exchange(): return lax.ppermute(block, axis, [(i, i ^ mask) for i in ranks])  51.8 us
    dot_general x1, matrix products, local(): lax.dot_general(left, right, (((0,), (0,)), ((), ())), preferred_element_...  9.4 us
    dot_general x1, matrix products, local(): kept = jnp.dot(chunk[:4 * n], weight, preferred_element_type=F32)  6.96 us
    convert_element_type x8, other arithmetic, scattered(): out = jnp.stack([kept[mask ^ q].astype(BF16) for q in rest])  6.36 us
    dot_general x1, matrix products, local(): lax.dot_general(near, weight, contract, preferred_element_type=F32)  6.18 us
    dynamic_update_slice x6, local copies, waits for them, and re-layouts, local(): near = lax.dynamic_update_slice(near, held[k:k + 1], (y ^ r, 0, h * width))  4.3 us
    another operation x8, other arithmetic, scattered(): out = jnp.stack([kept[mask ^ q].astype(BF16) for q in rest])  4.21 us
  transfers between devices with their start and end apart: 42, of which 20 were waited for; matrix products, arithmetic and copies ran while one was open for 29% of the time, Pallas kernels for 0%

profile of v1, /device:TPU:0, one launch (start us, length us, event | category | flops | bytes accessed | tf_op | source)
XLA Modules:
  0.0 196.8 jit_solution(17769945397216074170)
XLA Ops:
  0.6 1.6 slice_bitcast_fusion
  2.2 1.6 collective-permute-start.6
  3.8 1.9 collective-permute-start
  5.7 1.5 dynamic-slice_bitcast_fusion.1
  10.8 3.1 %collective-permute-start.12 = (f32[8,128]{1,0:T(8,128)S(1)}, f32[8,128]{1,0:T(8,128)S(1)}, u32[]{:S(2)}, u32[]{:S(2)}) collective-permute-start(f32[8,128]{1,0:T(8,128)S(1)} %reshape.628), channel_id=1, source_target_pairs={{0,48},{8,56},{16,32},{24,40},{32,16},{40,24},{48,0},{56,8},{1,49}... | collective-permute-start | bytes 12296 | tf_op jit(solution)/shard_map/ppermute | solution.py:16
  15.7 2.6 %collective-permute-start.3 = (bf16[1,64,512]{2,1,0:T(8,128)(2,1)S(1)}, bf16[1,64,512]{2,1,0:T(8,128)(2,1)S(1)}, u32[]{:S(2)}, u32[]{:S(2)}) collective-permute-start(bf16[1,64,512]{2,1,0:T(8,128)(2,1)S(1)} %get-tuple-element.44), channel_id=1, source_target_pairs={{0,3},{1,2},{2,1},{3,0},{4,7},{5,6},{6,5},{7,4},{8,11},{9,10},{10,... | collective-permute-start | bytes 196616 | tf_op jit(solution)/shard_map/ppermute | solution.py:16
  22.5 4.0 %collective-permute-start.1 = (bf16[2,64,512]{2,1,0:T(8,128)(2,1)S(1)}, bf16[2,64,512]{2,1,0:T(8,128)(2,1)S(1)}, u32[]{:S(2)}, u32[]{:S(2)}) collective-permute-start(bf16[2,64,512]{2,1,0:T(8,128)(2,1)S(1)} %pad_maximum_fusion.13), channel_id=1, source_target_pairs={{0,3},{1,2},{2,1},{3,0},{4,7},{5,6},{6,5},{7,4},{8,11},{9,10},{10,... | collective-permute-start | bytes 393224 | tf_op jit(solution)/shard_map/ppermute | solution.py:16
  28.3 1.9 collective-permute-start.8
  32.5 5.0 %collective-permute-done.2 = bf16[4,64,512]{2,1,0:T(8,128)(2,1)S(1)} collective-permute-done((bf16[4,64,512]{2,1,0:T(8,128)(2,1)S(1)}, bf16[4,64,512]{2,1,0:T(8,128)(2,1)S(1)}, u32[]{:S(2)}, u32[]{:S(2)}) %collective-permute-start.2) | collective-permute-done | bytes 262176 | tf_op jit(solution)/shard_map/ppermute | solution.py:16
  39.3 3.7 %fusion.9 = bf16[256,3072]{1,0:T(8,128)(2,1)} fusion(bf16[1,1536,3072]{2,1,0:T(8,128)(2,1)S(1)} %copy-done.16, bf16[512,1536]{1,0:T(8,128)(2,1)S(1)} %fusion.16), kind=kOutput, calls=%fused_computation.10 | convolution fusion | flops 2416705536 | bytes 11796480 | tf_op jit(solution)/shard_map/dot_general | solution.py:112
  43.0 3.7 %collective-permute-done.13 = bf16[256,3072]{1,0:T(8,128)(2,1)} collective-permute-done((bf16[256,3072]{1,0:T(8,128)(2,1)}, bf16[256,3072]{1,0:T(8,128)(2,1)}, u32[]{:S(2)}, u32[]{:S(2)}) %collective-permute-start.13) | collective-permute-done | bytes 1572896 | tf_op jit(solution)/shard_map/ppermute | solution.py:16
  46.7 7.0 %convert_add_fusion = f32[256,3072]{1,0:T(8,128)S(1)} fusion(bf16[256,3072]{1,0:T(8,128)(2,1)} %collective-permute-done.13, bf16[1,1536,3072]{2,1,0:T(8,128)(2,1)} %param.6, bf16[512,1536]{1,0:T(8,128)(2,1)} %copy-done.3), kind=kOutput, calls=%fused_computation.19 | convolution fusion | flops 2417491968 | bytes 14942208 | tf_op jit(solution)/shard_map/dot_general | solution.py:114
  53.7 1.3 fusion.69
  57.4 11.0 %collective-permute-done.14 = bf16[2,64,1536]{2,1,0:T(8,128)(2,1)S(1)} collective-permute-done((bf16[2,64,1536]{2,1,0:T(8,128)(2,1)}, bf16[2,64,1536]{2,1,0:T(8,128)(2,1)S(1)}, u32[]{:S(2)}, u32[]{:S(2)}) %collective-permute-start.14) | collective-permute-done | bytes 393248 | tf_op jit(solution)/shard_map/ppermute | solution.py:16
  69.5 1.8 collective-permute-start.15
  72.4 4.4 %collective-permute-done.15 = bf16[1,64,1536]{2,1,0:T(8,128)(2,1)S(1)} collective-permute-done((bf16[1,64,1536]{2,1,0:T(8,128)(2,1)S(1)}, bf16[1,64,1536]{2,1,0:T(8,128)(2,1)S(1)}, u32[]{:S(2)}, u32[]{:S(2)}) %collective-permute-start.15) | collective-permute-done | bytes 196640 | tf_op jit(solution)/shard_map/ppermute | solution.py:16
  77.1 3.0 %collective-permute-start.16 = (bf16[64,1536]{1,0:T(8,128)(2,1)S(1)}, bf16[64,1536]{1,0:T(8,128)(2,1)S(1)}, u32[]{:S(2)}, u32[]{:S(2)}) collective-permute-start(bf16[64,1536]{1,0:T(8,128)(2,1)S(1)} %fusion.43), channel_id=1, source_target_pairs={{0,64},{64,0},{1,65},{65,1},{2,66},{66,2},{3,67},{67,3},{4,68},{68... | collective-permute-start | bytes 589832 | tf_op jit(solution)/shard_map/ppermute | solution.py:16
  80.1 1.7 collective-permute-start.19
  81.8 2.6 %collective-permute-done.16 = bf16[64,1536]{1,0:T(8,128)(2,1)S(1)} collective-permute-done((bf16[64,1536]{1,0:T(8,128)(2,1)S(1)}, bf16[64,1536]{1,0:T(8,128)(2,1)S(1)}, u32[]{:S(2)}, u32[]{:S(2)}) %collective-permute-start.16) | collective-permute-done | bytes 196640 | tf_op jit(solution)/shard_map/ppermute | solution.py:16
  84.3 1.4 broadcast_in_dim.30
  86.8 3.7 %collective-permute-done.19 = bf16[2,64,1536]{2,1,0:T(8,128)(2,1)S(1)} collective-permute-done((bf16[2,64,1536]{2,1,0:T(8,128)(2,1)S(1)}, bf16[2,64,1536]{2,1,0:T(8,128)(2,1)S(1)}, u32[]{:S(2)}, u32[]{:S(2)}) %collective-permute-start.19) | collective-permute-done | bytes 393248 | tf_op jit(solution)/shard_map/ppermute | solution.py:16
  90.6 3.8 %collective-permute-done.17 = bf16[1,64,1536]{2,1,0:T(8,128)(2,1)S(1)} collective-permute-done((bf16[1,64,1536]{2,1,0:T(8,128)(2,1)S(1)}, bf16[1,64,1536]{2,1,0:T(8,128)(2,1)S(1)}, u32[]{:S(2)}, u32[]{:S(2)}) %collective-permute-start.17) | collective-permute-done | bytes 196640 | tf_op jit(solution)/shard_map/ppermute | solution.py:16
  94.5 1.8 collective-permute-start.18
  96.8 1.3 collective-permute-start.21
  98.9 4.7 %collective-permute-done.18 = bf16[2,64,1536]{2,1,0:T(8,128)(2,1)S(1)} collective-permute-done((bf16[2,64,1536]{2,1,0:T(8,128)(2,1)S(1)}, bf16[2,64,1536]{2,1,0:T(8,128)(2,1)S(1)}, u32[]{:S(2)}, u32[]{:S(2)}) %collective-permute-start.18) | collective-permute-done | bytes 393248 | tf_op jit(solution)/shard_map/ppermute | solution.py:16
  106.1 1.7 collective-permute-start.22
  107.8 5.2 %collective-permute-done.22 = bf16[1,64,1536]{2,1,0:T(8,128)(2,1)S(1)} collective-permute-done((bf16[1,64,1536]{2,1,0:T(8,128)(2,1)S(1)}, bf16[1,64,1536]{2,1,0:T(8,128)(2,1)S(1)}, u32[]{:S(2)}, u32[]{:S(2)}) %collective-permute-start.22) | collective-permute-done | bytes 196640 | tf_op jit(solution)/shard_map/ppermute | solution.py:16
  113.8 7.0 %collective-permute-done.23 = bf16[2,64,1536]{2,1,0:T(8,128)(2,1)S(1)} collective-permute-done((bf16[2,64,1536]{2,1,0:T(8,128)(2,1)S(1)}, bf16[2,64,1536]{2,1,0:T(8,128)(2,1)S(1)}, u32[]{:S(2)}, u32[]{:S(2)}) %collective-permute-start.23) | collective-permute-done | bytes 393248 | tf_op jit(solution)/shard_map/ppermute | solution.py:16
  122.3 1.8 fusion.65
  126.3 6.2 %fusion.3 = f32[256,1536]{1,0:T(8,128)S(1)} fusion(bf16[256,3072]{1,0:T(8,128)(2,1)} %bitcast.16, bf16[1,1536,3072]{2,1,0:T(8,128)(2,1)} %param.6), kind=kOutput, calls=%fused_computation.4 | convolution fusion | flops 2415919104 | bytes 12582912 | tf_op jit(solution)/shard_map/dot_general | solution.py:135
  132.6 4.2 %fusion.1 = f32[256,1536]{1,0:T(8,128)S(1)} fusion(bf16[256,3072]{1,0:T(8,128)(2,1)} %collective-permute-done.24, bf16[1,1536,3072]{2,1,0:T(8,128)(2,1)S(1)} %bitcast.141), kind=kOutput, calls=%fused_computation.2 | convolution fusion | flops 2415919104 | bytes 12582912 | tf_op jit(solution)/shard_map/dot_general | solution.py:136
  136.8 1.6 multiply_reduce_fusion.1
  143.9 3.1 %collective-permute-start.28 = (bf16[4,64,512]{2,1,0:T(8,128)(2,1)S(1)}, bf16[4,64,512]{2,1,0:T(8,128)(2,1)}, u32[]{:S(2)}, u32[]{:S(2)}) collective-permute-start(bf16[4,64,512]{2,1,0:T(8,128)(2,1)S(1)} %pad_maximum_fusion.11), channel_id=1, source_target_pairs={{0,3},{1,2},{2,1},{3,0},{4,7},{5,6},{6,5},{7,4},{8,11},{9,10},{10,... | collective-permute-start | bytes 786440 | tf_op jit(solution)/shard_map/ppermute | solution.py:16
  148.3 1.3 rev.7
  149.5 1.3 maximum_add_fusion.1
  150.8 1.3 reshape.634
  154.2 2.0 %collective-permute-start.35 = (f32[8,128]{1,0:T(8,128)}, f32[8,128]{1,0:T(8,128)S(1)}, u32[]{:S(2)}, u32[]{:S(2)}) collective-permute-start(f32[8,128]{1,0:T(8,128)} %reshape.634), channel_id=1, source_target_pairs={{0,16},{8,24},{16,0},{24,8},{32,48},{40,56},{48,32},{56,40},{1,17}... | collective-permute-start | bytes 12296 | tf_op jit(solution)/shard_map/ppermute | solution.py:16
  156.2 1.7 pad_maximum_fusion.12
  159.8 2.1 %collective-permute-start.40 = (f32[20,128]{1,0:T(8,128)S(1)}, f32[20,128]{1,0:T(8,128)S(1)}, u32[]{:S(2)}, u32[]{:S(2)}) collective-permute-start(f32[20,128]{1,0:T(8,128)S(1)} %pad_maximum_fusion.19), channel_id=1, source_target_pairs={{0,3},{1,2},{2,1},{3,0},{4,7},{5,6},{6,5},{7,4},{8,11},{9,10},{10,... | collective-permute-start | bytes 30728 | tf_op jit(solution)/shard_map/ppermute | solution.py:16
  161.8 1.4 collective-permute-start.38
  163.2 1.6 pad_maximum_fusion.10
  165.6 1.3 collective-permute-start.41
  166.9 9.4 %fusion = bf16[1,1536,3072]{2,1,0:T(8,128)(2,1)} fusion(bf16[512,1536]{1,0:T(8,128)(2,1)} %copy-done.3, bf16[256,3072]{1,0:T(8,128)(2,1)} %collective-permute-done.24, bf16[256,3072]{1,0:T(8,128)(2,1)} %bitcast.16), kind=kOutput, calls=%fused_computation.1 | convolution fusion | flops 4842848256 | bytes 14155776 | tf_op jit(solution)/shard_map/dot_general | solution.py:166
  180.1 1.5 collective-permute-start.32
  184.0 1.4 collective-permute-start.30
  186.3 1.8 collective-permute-start.33
  192.7 1.3 collective-permute-done.27
  194.9 1.9 fusion.51
  (198 shorter events, 53.3 us)
Async XLA Ops:
  2.2 18.2 %collective-permute-start.6 = (bf16[1,64,512]{2,1,0:T(8,128)(2,1)}, bf16[1,64,512]{2,1,0:T(8,128)(2,1)S(1)}, u32[]{:S(2)}, u32[]{:S(2)}) collective-permute-start(bf16[1,64,512]{2,1,0:T(8,128)(2,1)} %get-tuple-element.42), channel_id=1, source_target_pairs={{0,4},{1,5},{2,6},{3,7},{4,0},{5,1},{6,2},{7,3},{8,12},{9,13},{10,... | collective-permute-start | bytes 196616 | tf_op jit(solution)/shard_map/ppermute | solution.py:16
  3.8 17.8 %collective-permute-start = (bf16[1,64,512]{2,1,0:T(8,128)(2,1)}, bf16[1,64,512]{2,1,0:T(8,128)(2,1)S(1)}, u32[]{:S(2)}, u32[]{:S(2)}) collective-permute-start(bf16[1,64,512]{2,1,0:T(8,128)(2,1)} %get-tuple-element.43), channel_id=1, source_target_pairs={{0,1},{1,0},{2,3},{3,2},{4,5},{5,4},{6,7},{7,6},{8,9},{9,8},{10,11... | collective-permute-start | bytes 196616 | tf_op jit(solution)/shard_map/ppermute | solution.py:16
  8.5 1.5 collective-permute-start.9
  10.8 4.9 %collective-permute-start.12 = (f32[8,128]{1,0:T(8,128)S(1)}, f32[8,128]{1,0:T(8,128)S(1)}, u32[]{:S(2)}, u32[]{:S(2)}) collective-permute-start(f32[8,128]{1,0:T(8,128)S(1)} %reshape.628), channel_id=1, source_target_pairs={{0,48},{8,56},{16,32},{24,40},{32,16},{40,24},{48,0},{56,8},{1,49}... | collective-permute-start | bytes 12296 | tf_op jit(solution)/shard_map/ppermute | solution.py:16
  13.9 5.2 %collective-permute-start.11 = (f32[8,128]{1,0:T(8,128)S(1)}, f32[8,128]{1,0:T(8,128)}, u32[]{:S(2)}, u32[]{:S(2)}) collective-permute-start(f32[8,128]{1,0:T(8,128)S(1)} %reshape.628), channel_id=1, source_target_pairs={{0,32},{8,40},{16,48},{24,56},{32,0},{40,8},{48,16},{56,24},{1,33}... | collective-permute-start | bytes 12296 | tf_op jit(solution)/shard_map/ppermute | solution.py:16
  14.6 4.6 %collective-permute-start.10 = (f32[8,128]{1,0:T(8,128)S(1)}, f32[8,128]{1,0:T(8,128)}, u32[]{:S(2)}, u32[]{:S(2)}) collective-permute-start(f32[8,128]{1,0:T(8,128)S(1)} %reshape.628), channel_id=1, source_target_pairs={{0,16},{8,24},{16,0},{24,8},{32,48},{40,56},{48,32},{56,40},{1,17}... | collective-permute-start | bytes 12296 | tf_op jit(solution)/shard_map/ppermute | solution.py:16
  15.7 10.7 %collective-permute-start.3 = (bf16[1,64,512]{2,1,0:T(8,128)(2,1)S(1)}, bf16[1,64,512]{2,1,0:T(8,128)(2,1)S(1)}, u32[]{:S(2)}, u32[]{:S(2)}) collective-permute-start(bf16[1,64,512]{2,1,0:T(8,128)(2,1)S(1)} %get-tuple-element.44), channel_id=1, source_target_pairs={{0,3},{1,2},{2,1},{3,0},{4,7},{5,6},{6,5},{7,4},{8,11},{9,10},{10,... | collective-permute-start | bytes 196616 | tf_op jit(solution)/shard_map/ppermute | solution.py:16
  20.4 18.1 %copy-start.6 = (f32[512]{0:T(512)}, f32[512]{0:T(512)S(1)}, u32[]{:S(2)}) copy-start(f32[512]{0:T(512)S(1)} %get-tuple-element.48) | copy-start | bytes 6148
  20.4 103.8 %copy-start.8 = (f32[4,128]{1,0:T(4,128)}, f32[4,128]{1,0:T(4,128)S(1)}, u32[]{:S(2)}) copy-start(f32[4,128]{1,0:T(4,128)S(1)} %get-tuple-element.47) | copy-start | bytes 6148
  21.3 5.8 %collective-permute-start.7 = (bf16[2,64,512]{2,1,0:T(8,128)(2,1)S(1)}, bf16[2,64,512]{2,1,0:T(8,128)(2,1)S(1)}, u32[]{:S(2)}, u32[]{:S(2)}) collective-permute-start(bf16[2,64,512]{2,1,0:T(8,128)(2,1)S(1)} %pad_maximum_fusion.15), channel_id=1, source_target_pairs={{0,1},{1,0},{2,3},{3,2},{4,5},{5,4},{6,7},{7,6},{8,9},{9,8},{10,11... | collective-permute-start | bytes 393224 | tf_op jit(solution)/shard_map/ppermute | solution.py:16
  22.5 7.7 %collective-permute-start.1 = (bf16[2,64,512]{2,1,0:T(8,128)(2,1)S(1)}, bf16[2,64,512]{2,1,0:T(8,128)(2,1)S(1)}, u32[]{:S(2)}, u32[]{:S(2)}) collective-permute-start(bf16[2,64,512]{2,1,0:T(8,128)(2,1)S(1)} %pad_maximum_fusion.13), channel_id=1, source_target_pairs={{0,3},{1,2},{2,1},{3,0},{4,7},{5,6},{6,5},{7,4},{8,11},{9,10},{10,... | collective-permute-start | bytes 393224 | tf_op jit(solution)/shard_map/ppermute | solution.py:16
  26.5 5.3 %collective-permute-start.4 = (bf16[2,64,512]{2,1,0:T(8,128)(2,1)S(1)}, bf16[2,64,512]{2,1,0:T(8,128)(2,1)S(1)}, u32[]{:S(2)}, u32[]{:S(2)}) collective-permute-start(bf16[2,64,512]{2,1,0:T(8,128)(2,1)S(1)} %pad_maximum_fusion.14), channel_id=1, source_target_pairs={{0,4},{1,5},{2,6},{3,7},{4,0},{5,1},{6,2},{7,3},{8,12},{9,13},{10,... | collective-permute-start | bytes 393224 | tf_op jit(solution)/shard_map/ppermute | solution.py:16
  28.3 10.1 %collective-permute-start.8 = (bf16[4,64,512]{2,1,0:T(8,128)(2,1)S(1)}, bf16[4,64,512]{2,1,0:T(8,128)(2,1)S(1)}, u32[]{:S(2)}, u32[]{:S(2)}) collective-permute-start(bf16[4,64,512]{2,1,0:T(8,128)(2,1)S(1)} %pad_maximum_fusion.9), channel_id=1, source_target_pairs={{0,3},{1,2},{2,1},{3,0},{4,7},{5,6},{6,5},{7,4},{8,11},{9,10},{10,... | collective-permute-start | bytes 786440 | tf_op jit(solution)/shard_map/ppermute | solution.py:16
  31.0 6.5 %collective-permute-start.2 = (bf16[4,64,512]{2,1,0:T(8,128)(2,1)S(1)}, bf16[4,64,512]{2,1,0:T(8,128)(2,1)S(1)}, u32[]{:S(2)}, u32[]{:S(2)}) collective-permute-start(bf16[4,64,512]{2,1,0:T(8,128)(2,1)S(1)} %pad_maximum_fusion.7), channel_id=1, source_target_pairs={{0,4},{1,5},{2,6},{3,7},{4,0},{5,1},{6,2},{7,3},{8,12},{9,13},{10,... | collective-permute-start | bytes 786440 | tf_op jit(solution)/shard_map/ppermute | solution.py:16
  31.8 6.5 %collective-permute-start.5 = (bf16[4,64,512]{2,1,0:T(8,128)(2,1)S(1)}, bf16[4,64,512]{2,1,0:T(8,128)(2,1)S(1)}, u32[]{:S(2)}, u32[]{:S(2)}) collective-permute-start(bf16[4,64,512]{2,1,0:T(8,128)(2,1)S(1)} %pad_maximum_fusion.8), channel_id=1, source_target_pairs={{0,1},{1,0},{2,3},{3,2},{4,5},{5,4},{6,7},{7,6},{8,9},{9,8},{10,11... | collective-permute-start | bytes 786440 | tf_op jit(solution)/shard_map/ppermute | solution.py:16
  43.0 3.8 %collective-permute-start.13 = (bf16[256,3072]{1,0:T(8,128)(2,1)}, bf16[256,3072]{1,0:T(8,128)(2,1)}, u32[]{:S(2)}, u32[]{:S(2)}) collective-permute-start(bf16[256,3072]{1,0:T(8,128)(2,1)} %fusion.9), channel_id=1, source_target_pairs={{0,8},{8,0},{16,24},{24,16},{32,40},{40,32},{48,56},{56,48},{1,9},... | collective-permute-start | bytes 4718600 | tf_op jit(solution)/shard_map/ppermute | solution.py:16
  57.1 11.4 %collective-permute-start.14 = (bf16[2,64,1536]{2,1,0:T(8,128)(2,1)}, bf16[2,64,1536]{2,1,0:T(8,128)(2,1)S(1)}, u32[]{:S(2)}, u32[]{:S(2)}) collective-permute-start(bf16[2,64,1536]{2,1,0:T(8,128)(2,1)} %pad_maximum_fusion.2), channel_id=1, source_target_pairs={{0,16},{8,24},{16,0},{24,8},{32,48},{40,56},{48,32},{56,40},{1,17}... | collective-permute-start | bytes 1179656 | tf_op jit(solution)/shard_map/ppermute | solution.py:16
  57.4 19.4 %copy-start.2 = (f32[4,64,1536]{2,1,0:T(8,128)S(1)}, f32[4,64,1536]{2,1,0:T(8,128)}, u32[]{:S(2)}) copy-start(f32[4,64,1536]{2,1,0:T(8,128)} %copy-done.1) | copy-start | bytes 4718596
  69.5 7.4 %collective-permute-start.15 = (bf16[1,64,1536]{2,1,0:T(8,128)(2,1)S(1)}, bf16[1,64,1536]{2,1,0:T(8,128)(2,1)S(1)}, u32[]{:S(2)}, u32[]{:S(2)}) collective-permute-start(bf16[1,64,1536]{2,1,0:T(8,128)(2,1)S(1)} %add_convert_fusion.1), channel_id=1, source_target_pairs={{0,48},{8,56},{16,32},{24,40},{32,16},{40,24},{48,0},{56,8},{1,49}... | collective-permute-start | bytes 589832 | tf_op jit(solution)/shard_map/ppermute | solution.py:16
  77.1 7.3 %collective-permute-start.16 = (bf16[64,1536]{1,0:T(8,128)(2,1)S(1)}, bf16[64,1536]{1,0:T(8,128)(2,1)S(1)}, u32[]{:S(2)}, u32[]{:S(2)}) collective-permute-start(bf16[64,1536]{1,0:T(8,128)(2,1)S(1)} %fusion.43), channel_id=1, source_target_pairs={{0,64},{64,0},{1,65},{65,1},{2,66},{66,2},{3,67},{67,3},{4,68},{68... | collective-permute-start | bytes 589832 | tf_op jit(solution)/shard_map/ppermute | solution.py:16
  80.1 10.4 %collective-permute-start.19 = (bf16[2,64,1536]{2,1,0:T(8,128)(2,1)S(1)}, bf16[2,64,1536]{2,1,0:T(8,128)(2,1)S(1)}, u32[]{:S(2)}, u32[]{:S(2)}) collective-permute-start(bf16[2,64,1536]{2,1,0:T(8,128)(2,1)S(1)} %pad_maximum_fusion.4), channel_id=1, source_target_pairs={{0,48},{8,56},{16,32},{24,40},{32,16},{40,24},{48,0},{56,8},{1,49}... | collective-permute-start | bytes 1179656 | tf_op jit(solution)/shard_map/ppermute | solution.py:16
  86.8 7.7 %collective-permute-start.17 = (bf16[1,64,1536]{2,1,0:T(8,128)(2,1)S(1)}, bf16[1,64,1536]{2,1,0:T(8,128)(2,1)S(1)}, u32[]{:S(2)}, u32[]{:S(2)}) collective-permute-start(bf16[1,64,1536]{2,1,0:T(8,128)(2,1)S(1)} %get-tuple-element.11), channel_id=1, source_target_pairs={{0,16},{8,24},{16,0},{24,8},{32,48},{40,56},{48,32},{56,40},{1,17}... | collective-permute-start | bytes 589832 | tf_op jit(solution)/shard_map/ppermute | solution.py:16
  90.5 6.1 %collective-permute-start.20 = (bf16[1,64,1536]{2,1,0:T(8,128)(2,1)S(1)}, bf16[1,64,1536]{2,1,0:T(8,128)(2,1)S(1)}, u32[]{:S(2)}, u32[]{:S(2)}) collective-permute-start(bf16[1,64,1536]{2,1,0:T(8,128)(2,1)S(1)} %add_convert_fusion), channel_id=1, source_target_pairs={{0,16},{8,24},{16,0},{24,8},{32,48},{40,56},{48,32},{56,40},{1,17}... | collective-permute-start | bytes 589832 | tf_op jit(solution)/shard_map/ppermute | solution.py:16
  94.5 9.1 %collective-permute-start.18 = (bf16[2,64,1536]{2,1,0:T(8,128)(2,1)S(1)}, bf16[2,64,1536]{2,1,0:T(8,128)(2,1)S(1)}, u32[]{:S(2)}, u32[]{:S(2)}) collective-permute-start(bf16[2,64,1536]{2,1,0:T(8,128)(2,1)S(1)} %pad_maximum_fusion.3), channel_id=1, source_target_pairs={{0,48},{8,56},{16,32},{24,40},{32,16},{40,24},{48,0},{56,8},{1,49}... | collective-permute-start | bytes 1179656 | tf_op jit(solution)/shard_map/ppermute | solution.py:16
  96.8 8.2 %collective-permute-start.21 = (bf16[64,1536]{1,0:T(8,128)(2,1)S(1)}, bf16[64,1536]{1,0:T(8,128)(2,1)S(1)}, u32[]{:S(2)}, u32[]{:S(2)}) collective-permute-start(bf16[64,1536]{1,0:T(8,128)(2,1)S(1)} %fusion.44), channel_id=1, source_target_pairs={{0,64},{64,0},{1,65},{65,1},{2,66},{66,2},{3,67},{67,3},{4,68},{68... | collective-permute-start | bytes 589832 | tf_op jit(solution)/shard_map/ppermute | solution.py:16
  106.1 6.9 %collective-permute-start.22 = (bf16[1,64,1536]{2,1,0:T(8,128)(2,1)S(1)}, bf16[1,64,1536]{2,1,0:T(8,128)(2,1)S(1)}, u32[]{:S(2)}, u32[]{:S(2)}) collective-permute-start(bf16[1,64,1536]{2,1,0:T(8,128)(2,1)S(1)} %get-tuple-element.9), channel_id=1, source_target_pairs={{0,48},{8,56},{16,32},{24,40},{32,16},{40,24},{48,0},{56,8},{1,49}... | collective-permute-start | bytes 589832 | tf_op jit(solution)/shard_map/ppermute | solution.py:16
  113.0 7.9 %collective-permute-start.23 = (bf16[2,64,1536]{2,1,0:T(8,128)(2,1)S(1)}, bf16[2,64,1536]{2,1,0:T(8,128)(2,1)S(1)}, u32[]{:S(2)}, u32[]{:S(2)}) collective-permute-start(bf16[2,64,1536]{2,1,0:T(8,128)(2,1)S(1)} %pad_maximum_fusion.5), channel_id=1, source_target_pairs={{0,16},{8,24},{16,0},{24,8},{32,48},{40,56},{48,32},{56,40},{1,17}... | collective-permute-start | bytes 1179656 | tf_op jit(solution)/shard_map/ppermute | solution.py:16
  122.3 10.3 %collective-permute-start.24 = (bf16[256,3072]{1,0:T(8,128)(2,1)}, bf16[256,3072]{1,0:T(8,128)(2,1)}, u32[]{:S(2)}, u32[]{:S(2)}) collective-permute-start(bf16[256,3072]{1,0:T(8,128)(2,1)} %bitcast.16), channel_id=1, source_target_pairs={{0,8},{8,0},{16,24},{24,16},{32,40},{40,32},{48,56},{56,48},{1,9},... | collective-permute-start | bytes 4718600 | tf_op jit(solution)/shard_map/ppermute | solution.py:16
  139.5 7.5 %collective-permute-start.34 = (f32[8,128]{1,0:T(8,128)}, f32[8,128]{1,0:T(8,128)}, u32[]{:S(2)}, u32[]{:S(2)}) collective-permute-start(f32[8,128]{1,0:T(8,128)} %reshape.632), channel_id=1, source_target_pairs={{0,8},{8,0},{16,24},{24,16},{32,40},{40,32},{48,56},{56,48},{1,9},... | collective-permute-start | bytes 12296 | tf_op jit(solution)/shard_map/ppermute | solution.py:16
  143.9 33.2 %collective-permute-start.28 = (bf16[4,64,512]{2,1,0:T(8,128)(2,1)S(1)}, bf16[4,64,512]{2,1,0:T(8,128)(2,1)}, u32[]{:S(2)}, u32[]{:S(2)}) collective-permute-start(bf16[4,64,512]{2,1,0:T(8,128)(2,1)S(1)} %pad_maximum_fusion.11), channel_id=1, source_target_pairs={{0,3},{1,2},{2,1},{3,0},{4,7},{5,6},{6,5},{7,4},{8,11},{9,10},{10,... | collective-permute-start | bytes 786440 | tf_op jit(solution)/shard_map/ppermute | solution.py:16
  152.1 6.9 %collective-permute-start.37 = (f32[8,128]{1,0:T(8,128)}, f32[8,128]{1,0:T(8,128)S(1)}, u32[]{:S(2)}, u32[]{:S(2)}) collective-permute-start(f32[8,128]{1,0:T(8,128)} %reshape.634), channel_id=1, source_target_pairs={{0,48},{8,56},{16,32},{24,40},{32,16},{40,24},{48,0},{56,8},{1,49}... | collective-permute-start | bytes 12296 | tf_op jit(solution)/shard_map/ppermute | solution.py:16
  153.0 6.0 %collective-permute-start.36 = (f32[8,128]{1,0:T(8,128)}, f32[8,128]{1,0:T(8,128)S(1)}, u32[]{:S(2)}, u32[]{:S(2)}) collective-permute-start(f32[8,128]{1,0:T(8,128)} %reshape.634), channel_id=1, source_target_pairs={{0,32},{8,40},{16,48},{24,56},{32,0},{40,8},{48,16},{56,24},{1,33}... | collective-permute-start | bytes 12296 | tf_op jit(solution)/shard_map/ppermute | solution.py:16
  154.2 4.8 %collective-permute-start.35 = (f32[8,128]{1,0:T(8,128)}, f32[8,128]{1,0:T(8,128)S(1)}, u32[]{:S(2)}, u32[]{:S(2)}) collective-permute-start(f32[8,128]{1,0:T(8,128)} %reshape.634), channel_id=1, source_target_pairs={{0,16},{8,24},{16,0},{24,8},{32,48},{40,56},{48,32},{56,40},{1,17}... | collective-permute-start | bytes 12296 | tf_op jit(solution)/shard_map/ppermute | solution.py:16
  157.9 21.3 %collective-permute-start.31 = (bf16[4,64,512]{2,1,0:T(8,128)(2,1)}, bf16[4,64,512]{2,1,0:T(8,128)(2,1)}, u32[]{:S(2)}, u32[]{:S(2)}) collective-permute-start(bf16[4,64,512]{2,1,0:T(8,128)(2,1)} %pad_maximum_fusion.12), channel_id=1, source_target_pairs={{0,4},{1,5},{2,6},{3,7},{4,0},{5,1},{6,2},{7,3},{8,12},{9,13},{10,... | collective-permute-start | bytes 786440 | tf_op jit(solution)/shard_map/ppermute | solution.py:16
  159.7 5.3 %collective-permute-start.39 = (f32[20,128]{1,0:T(8,128)S(1)}, f32[20,128]{1,0:T(8,128)S(1)}, u32[]{:S(2)}, u32[]{:S(2)}) collective-permute-start(f32[20,128]{1,0:T(8,128)S(1)} %pad_maximum_fusion.19), channel_id=1, source_target_pairs={{0,2},{1,3},{2,0},{3,1},{4,6},{5,7},{6,4},{7,5},{8,10},{9,11},{10,... | collective-permute-start | bytes 30728 | tf_op jit(solution)/shard_map/ppermute | solution.py:16
  159.8 5.7 %collective-permute-start.40 = (f32[20,128]{1,0:T(8,128)S(1)}, f32[20,128]{1,0:T(8,128)S(1)}, u32[]{:S(2)}, u32[]{:S(2)}) collective-permute-start(f32[20,128]{1,0:T(8,128)S(1)} %pad_maximum_fusion.19), channel_id=1, source_target_pairs={{0,3},{1,2},{2,1},{3,0},{4,7},{5,6},{6,5},{7,4},{8,11},{9,10},{10,... | collective-permute-start | bytes 30728 | tf_op jit(solution)/shard_map/ppermute | solution.py:16
  161.8 3.8 %collective-permute-start.38 = (f32[20,128]{1,0:T(8,128)S(1)}, f32[20,128]{1,0:T(8,128)S(1)}, u32[]{:S(2)}, u32[]{:S(2)}) collective-permute-start(f32[20,128]{1,0:T(8,128)S(1)} %pad_maximum_fusion.19), channel_id=1, source_target_pairs={{0,1},{1,0},{2,3},{3,2},{4,5},{5,4},{6,7},{7,6},{8,9},{9,8},{10,11... | collective-permute-start | bytes 30728 | tf_op jit(solution)/shard_map/ppermute | solution.py:16
  164.9 16.7 %collective-permute-start.25 = (bf16[4,64,512]{2,1,0:T(8,128)(2,1)}, bf16[4,64,512]{2,1,0:T(8,128)(2,1)}, u32[]{:S(2)}, u32[]{:S(2)}) collective-permute-start(bf16[4,64,512]{2,1,0:T(8,128)(2,1)} %pad_maximum_fusion.10), channel_id=1, source_target_pairs={{0,1},{1,0},{2,3},{3,2},{4,5},{5,4},{6,7},{7,6},{8,9},{9,8},{10,11... | collective-permute-start | bytes 786440 | tf_op jit(solution)/shard_map/ppermute | solution.py:16
  165.6 10.7 %collective-permute-start.41 = (f32[20,128]{1,0:T(8,128)S(1)}, f32[20,128]{1,0:T(8,128)S(1)}, u32[]{:S(2)}, u32[]{:S(2)}) collective-permute-start(f32[20,128]{1,0:T(8,128)S(1)} %add_add_fusion), channel_id=1, source_target_pairs={{0,4},{1,5},{2,6},{3,7},{4,0},{5,1},{6,2},{7,3},{8,12},{9,13},{10,... | collective-permute-start | bytes 30728 | tf_op jit(solution)/shard_map/ppermute | solution.py:16
  178.1 5.1 %collective-permute-start.29 = (bf16[2,64,512]{2,1,0:T(8,128)(2,1)S(1)}, bf16[2,64,512]{2,1,0:T(8,128)(2,1)S(1)}, u32[]{:S(2)}, u32[]{:S(2)}) collective-permute-start(bf16[2,64,512]{2,1,0:T(8,128)(2,1)S(1)} %pad_maximum_fusion.17), channel_id=1, source_target_pairs={{0,4},{1,5},{2,6},{3,7},{4,0},{5,1},{6,2},{7,3},{8,12},{9,13},{10,... | collective-permute-start | bytes 393224 | tf_op jit(solution)/shard_map/ppermute | solution.py:16
  180.1 14.8 %copy-start.13 = (f32[1,64]{1,0:T(1,128)S(1)}, f32[1,64]{1,0:T(1,128)}, u32[]{:S(2)}) copy-start(f32[1,64]{1,0:T(1,128)} %get-tuple-element.51) | copy-start | bytes 772
  180.1 14.8 %copy-start.14 = (f32[1,64]{1,0:T(1,128)S(1)}, f32[1,64]{1,0:T(1,128)}, u32[]{:S(2)}) copy-start(f32[1,64]{1,0:T(1,128)} %get-tuple-element.52) | copy-start | bytes 772
  180.1 14.8 %copy-start.15 = (f32[64]{0:T(128)S(1)}, f32[64]{0:T(128)}, u32[]{:S(2)}) copy-start(f32[64]{0:T(128)} %fusion.58) | copy-start | bytes 772
  180.1 5.3 %collective-permute-start.32 = (bf16[2,64,512]{2,1,0:T(8,128)(2,1)S(1)}, bf16[2,64,512]{2,1,0:T(8,128)(2,1)S(1)}, u32[]{:S(2)}, u32[]{:S(2)}) collective-permute-start(bf16[2,64,512]{2,1,0:T(8,128)(2,1)S(1)} %pad_maximum_fusion.18), channel_id=1, source_target_pairs={{0,1},{1,0},{2,3},{3,2},{4,5},{5,4},{6,7},{7,6},{8,9},{9,8},{10,11... | collective-permute-start | bytes 393224 | tf_op jit(solution)/shard_map/ppermute | solution.py:16
  182.6 6.3 %collective-permute-start.26 = (bf16[2,64,512]{2,1,0:T(8,128)(2,1)S(1)}, bf16[2,64,512]{2,1,0:T(8,128)(2,1)S(1)}, u32[]{:S(2)}, u32[]{:S(2)}) collective-permute-start(bf16[2,64,512]{2,1,0:T(8,128)(2,1)S(1)} %pad_maximum_fusion.16), channel_id=1, source_target_pairs={{0,3},{1,2},{2,1},{3,0},{4,7},{5,6},{6,5},{7,4},{8,11},{9,10},{10,... | collective-permute-start | bytes 393224 | tf_op jit(solution)/shard_map/ppermute | solution.py:16
  184.0 6.7 %collective-permute-start.30 = (bf16[1,64,512]{2,1,0:T(8,128)(2,1)S(1)}, bf16[1,64,512]{2,1,0:T(8,128)(2,1)S(1)}, u32[]{:S(2)}, u32[]{:S(2)}) collective-permute-start(bf16[1,64,512]{2,1,0:T(8,128)(2,1)S(1)} %add_convert_fusion.5), channel_id=1, source_target_pairs={{0,1},{1,0},{2,3},{3,2},{4,5},{5,4},{6,7},{7,6},{8,9},{9,8},{10,11... | collective-permute-start | bytes 196616 | tf_op jit(solution)/shard_map/ppermute | solution.py:16
  186.3 5.6 %collective-permute-start.33 = (bf16[1,64,512]{2,1,0:T(8,128)(2,1)S(1)}, bf16[1,64,512]{2,1,0:T(8,128)(2,1)S(1)}, u32[]{:S(2)}, u32[]{:S(2)}) collective-permute-start(bf16[1,64,512]{2,1,0:T(8,128)(2,1)S(1)} %add_convert_fusion.2), channel_id=1, source_target_pairs={{0,3},{1,2},{2,1},{3,0},{4,7},{5,6},{6,5},{7,4},{8,11},{9,10},{10,... | collective-permute-start | bytes 196616 | tf_op jit(solution)/shard_map/ppermute | solution.py:16
  189.7 4.3 %collective-permute-start.27 = (bf16[1,64,512]{2,1,0:T(8,128)(2,1)S(1)}, bf16[1,64,512]{2,1,0:T(8,128)(2,1)S(1)}, u32[]{:S(2)}, u32[]{:S(2)}) collective-permute-start(bf16[1,64,512]{2,1,0:T(8,128)(2,1)S(1)} %add_convert_fusion.8), channel_id=1, source_target_pairs={{0,4},{1,5},{2,6},{3,7},{4,0},{5,1},{6,2},{7,3},{8,12},{9,13},{10,... | collective-permute-start | bytes 196616 | tf_op jit(solution)/shard_map/ppermute | solution.py:16
  (14 other events, 71.3 us)

commit v2 on v0

v2 whole, which is shorter than its diff:
```python
import jax
import jax.numpy as jnp
from jax import lax
from jax.sharding import PartitionSpec as P

D = 12288
F32 = jnp.float32
BF16 = jnp.bfloat16
Y_ORDERS = ((1, 3), (3, 1))
Y_PLACES = (0, 1, 3, 2)
COL_ORDERS = ((1, 3, 4), (3, 4, 1), (4, 1, 3))
CONTRACT_LAST = (((1,), (1,)), ((), ()))
CONTRACT_FIRST = (((0,), (0,)), ((), ()))


def exchange(block, axis, mask):
    ranks = range(lax.axis_size(axis))
    return lax.ppermute(block, axis, [(i, i ^ mask) for i in ranks])


def transposed(block):
    rows, cols = lax.axis_size("row"), lax.axis_size("col")
    route = [(r * cols + c, c * cols + r) for r in range(rows) for c in range(cols)]
    return lax.ppermute(block, ("section", "row", "col"), route)


def activation(values):
    return jax.nn.gelu(values, approximate=True)


def span(masks):
    found = [0]
    for mask in masks:
        found = found + [mask ^ f for f in found]
    return found


def local(tokens, vectors, weights, cotangent):
    second = lax.axis_index("section") == 1
    row = lax.axis_index("row")
    col = lax.axis_index("col")
    weight = weights[0]
    own_vector = vectors[0]
    features, hidden = weight.shape
    n = cotangent.shape[0]

    def by_y(block, mask):
        return exchange(block, "row", 2 * mask)

    def place(block):
        relative = block ^ row
        y = relative // 2
        return (relative % 2) * 4 + (y ^ (y // 2))

    width = features // 3
    held = [cotangent[None, :, i * width : (i + 1) * width] for i in range(3)]
    relative = [[0], [0], [0]]
    inputs = tokens.astype(F32)
    sums = None
    for step in range(3):
        got = [exchange(held[i], "col", order[step]) for i, order in enumerate(COL_ORDERS)]
        if step == 0:
            inputs, held = lax.optimization_barrier((inputs, held))
            sums = jnp.concatenate([jnp.sum(inputs, axis=1), jnp.sum(inputs * inputs, axis=1)])
        sums = sums + exchange(sums, "row", (1, 2, 4)[step])
        held = [jnp.concatenate([h, g]) for h, g in zip(held, got)]
        relative = [
            rel + [order[step] ^ r for r in rel] for rel, order in zip(relative, COL_ORDERS)
        ]
        if step < 2:
            held, sums = lax.optimization_barrier((held, sums))
    whole = jnp.zeros((8, n, features), BF16)
    for i in range(3):
        for k, r in enumerate(relative[i]):
            whole = lax.dynamic_update_slice(
                whole, held[i][k : k + 1], (place(col ^ r), 0, i * width)
            )
    cot_full = whole.reshape(8 * n, features)
    bias_grad = jnp.sum(cot_full.astype(F32), axis=0)
    total_rows = tokens.shape[0]
    mean, square = sums[:total_rows] / D, sums[total_rows:] / D
    inv_std = lax.rsqrt(square - mean * mean + 1e-05)
    normed = ((inputs - mean[:, None]) * inv_std[:, None] * own_vector).astype(BF16)
    blocks = [row ^ (2 * y + core) for core in range(2) for y in Y_PLACES]
    normed = jnp.concatenate([lax.dynamic_slice_in_dim(normed, b * n, n, 0) for b in blocks])
    left = jnp.where(second, cot_full, normed)

    sent = jnp.dot(left[4 * n :], weight, preferred_element_type=F32).astype(BF16)
    got = exchange(sent, "row", 1)
    kept = jnp.dot(left[: 4 * n], weight, preferred_element_type=F32)
    kept = lax.optimization_barrier(kept)
    both = (kept + got.astype(F32)).reshape(4, n, hidden)
    high = own_vector.astype(BF16)
    low = (own_vector - high.astype(F32)).astype(BF16)
    gain_rows = jnp.stack([high, low] + [jnp.zeros_like(high)] * 6)
    gain_image = None
    width = hidden // 2
    parts = [
        {r: both[i, :, h * width : (h + 1) * width] for i, r in enumerate(Y_PLACES)}
        for h in range(2)
    ]
    for step in range(2):
        sends = []
        for part, order in zip(parts, Y_ORDERS):
            rest = span(order[step + 1 :])
            sends.append(jnp.stack([part[order[step] ^ q].astype(BF16) for q in rest]))
        sends, gain_rows, gain_image = lax.optimization_barrier((sends, gain_rows, gain_image))
        got = [by_y(s, order[step]) for s, order in zip(sends, Y_ORDERS)]
        if step == 0:
            gain_image = jnp.dot(gain_rows, weight, preferred_element_type=F32)
            gain_image = jnp.sum(gain_image, axis=0)
        gain_image = gain_image + exchange(gain_image, "row", (1, 2)[step])
        parts = [
            {q: part[q] + g[i].astype(F32) for i, q in enumerate(span(order[step + 1 :]))}
            for part, g, order in zip(parts, got, Y_ORDERS)
        ]
    mine = jnp.concatenate([parts[0][0], parts[1][0]], axis=1)

    values, pullback = jax.vjp(activation, mine)
    leaving = jnp.where(second, mine, values).astype(BF16)
    leaving, gain_image = lax.optimization_barrier((leaving, gain_image))
    arrived = exchange(leaving, "section", 1)
    gain_image = gain_image + exchange(gain_image, "row", 4)
    grad_pre = pullback(arrived.astype(F32))[0].astype(BF16)
    piece = jnp.where(second, arrived, grad_pre)
    grads = piece.astype(F32)
    token_sums = jnp.concatenate([jnp.sum(grads * gain_image, axis=1), jnp.sum(grads * mine, axis=1)])
    held = [piece[None, :, :width], piece[None, :, width:]]
    got = [by_y(h, order[0]) for h, order in zip(held, Y_ORDERS)]
    token_sums = token_sums + exchange(token_sums, "col", 1)
    held = [jnp.concatenate([h, g]) for h, g in zip(held, got)]
    held, token_sums = lax.optimization_barrier((held, token_sums))
    got = [by_y(h, order[1]) for h, order in zip(held, Y_ORDERS)]
    token_sums = token_sums + exchange(token_sums, "col", 2)
    near = jnp.concatenate(
        [
            jnp.concatenate([held[0], got[0]]).reshape(4 * n, width),
            jnp.stack([held[1], got[1]], axis=1).reshape(4 * n, width),
        ],
        axis=1,
    )
    near, token_sums = lax.optimization_barrier((near, token_sums))
    far = exchange(near, "row", 1)
    token_sums = token_sums + exchange(token_sums, "col", 4)

    product = jnp.concatenate(
        [
            lax.dot_general(near, weight, CONTRACT_LAST, preferred_element_type=F32),
            lax.dot_general(far, weight, CONTRACT_LAST, preferred_element_type=F32),
        ]
    )
    gain_grad = jnp.sum(product * left.astype(F32), axis=0) / own_vector
    width = features // 3
    split = product.reshape(8, n, features)
    parts = [
        {
            r: lax.dynamic_slice(split, (place(col ^ r), 0, i * width), (1, n, width))
            for r in range(8)
        }
        for i in range(3)
    ]
    right = jnp.concatenate([near, far])
    weight_grads = None
    for step in range(3):
        sends = []
        for part, order in zip(parts, COL_ORDERS):
            rest = span(order[step + 1 :])
            sends.append(jnp.concatenate([part[order[step] ^ q].astype(BF16) for q in rest]))
        sends, right, gain_grad, token_sums = lax.optimization_barrier(
            (sends, right, gain_grad, token_sums)
        )
        got = [exchange(s, "col", order[step]) for s, order in zip(sends, COL_ORDERS)]
        gain_grad = gain_grad + exchange(gain_grad, "col", (1, 2, 4)[step])
        if step == 0:
            weight_grads = lax.dot_general(
                left, right, CONTRACT_FIRST, preferred_element_type=F32
            ).astype(BF16)
            weight_grads, got = lax.optimization_barrier((weight_grads, got))
        parts = [
            {q: part[q] + g[i : i + 1].astype(F32) for i, q in enumerate(span(order[step + 1 :]))}
            for part, g, order in zip(parts, got, COL_ORDERS)
        ]
    token_sums = transposed(token_sums) / D
    mean_grad, slope_grad = token_sums[:n], token_sums[n:]
    summed = jnp.concatenate([part[0][0] for part in parts], axis=1)

    first_row = col * n
    own_mean = lax.dynamic_slice_in_dim(mean, first_row, n, 0)
    own_inv = lax.dynamic_slice_in_dim(inv_std, first_row, n, 0)
    own_inputs = lax.dynamic_slice_in_dim(tokens, first_row, n, 0).astype(F32)
    own_centered = (own_inputs - own_mean[:, None]) * own_inv[:, None]
    grad_inputs = own_inv[:, None] * (
        summed * own_vector - mean_grad[:, None] - own_centered * slope_grad[:, None]
    )
    output = summed + own_vector
    section_outputs = jnp.where(second, output, grad_inputs).astype(BF16)[None]
    vector_grads = jnp.where(second, bias_grad, gain_grad)[None]
    return (section_outputs, weight_grads[None], vector_grads)


def solution(mesh):
    in_specs = (P(None, "row"), P("section", "row"), P("section", "row", "col"), P("col", "row"))
    out_specs = (P("section", "col", "row"), P("section", "row", "col"), P("section", "row"))
    return jax.shard_map(local, mesh=mesh, in_specs=in_specs, out_specs=out_specs, check_vma=False)
```

time: 315 us -> 151 us (0.48)
  waiting for transfers between devices: 172 us -> 45.1 us
  blocking collectives: 55.7 us -> 0 us
  starting transfers between devices: 6.46 us -> 52.6 us
  between operations: 14.2 us -> 1.53 us
  local copies, waits for them, and re-layouts: 16 us -> 4.68 us
  matrix products: 29 us -> 23.4 us
    reduce_scatter x4 -> x0, waiting for transfers between devices: 96.8 us -> none  [the longest x1 42.2 us: local(): lax.psum_scatter(partial_pre, 'row', scatter_dimension=1, tiled=True)]
    all_gather x3 -> x0, waiting for transfers between devices: 66.1 us -> none  [the longest x1 44.9 us: local(): cot_full = lax.all_gather(cotangent, 'col', axis=0, tiled=True)]
    ppermute x2 -> x42, starting transfers between devices: 6.18 us -> 52.6 us  [the longest x41 51.3 us: exchange(): return lax.ppermute(block, axis, [(i, i ^ mask) for i in ranks])]
    psum x3 -> x0, blocking collectives: 44.2 us -> none  [the longest x1 19 us: local(): gain_grad = lax.psum(jnp.sum(grad_normed * centered_block, axis=0), 'col')]
    ppermute x2 -> x42, waiting for transfers between devices: 8.14 us -> 45.1 us  [the longest x41 45.1 us: exchange(): return lax.ppermute(block, axis, [(i, i ^ mask) for i in ranks])]
    all_to_all x1 -> x0, blocking collectives: 11.4 us -> none  [local(): lax.all_to_all(hidden_share, 'row', split_axis=0, concat_axis=1, tiled=True)]
    broadcast_in_dim x2 -> x1, other arithmetic: 11.4 us -> 1.82 us  [local(): section_outputs = jnp.where(second, output, grad_inputs).astype(BF16)[None]]
    another operation x3 -> x5, local copies, waits for them, and re-layouts: 8.77 us -> 0.19 us  [the longest x4 0.16 us: local(): gain_rows = jnp.stack([high, low] + [jnp.zeros_like(high)] * 6)]
  transfers between devices with their start and end apart: 9 -> 42, of which waited for: 8 -> 22; matrix products, arithmetic and copies ran while one was open for 16% -> 18% of each run, Pallas kernels for 0% -> 0%
where the time goes in v2:
time: 151 us; the launch traced here: 149 us
  starting transfers between devices  52.6 us (35%)
  waiting for transfers between devices  45.1 us (30%)
  matrix products  23.4 us (15%)
  other arithmetic  21.9 us (15%)
  local copies, waits for them, and re-layouts  4.68 us (3%)
  between operations  1.53 us (1%)
    ppermute x41, starting transfers between devices, exchange(): return lax.ppermute(block, axis, [(i, i ^ mask) for i in ranks])  51.3 us
    ppermute x41, waiting for transfers between devices, exchange(): return lax.ppermute(block, axis, [(i, i ^ mask) for i in ranks])  45.1 us
    dot_general x1, matrix products, local(): lax.dot_general(left, right, CONTRACT_FIRST, preferred_element_type=F32)  7.55 us
    dot_general x1, matrix products, local(): jnp.dot(left[4 * n:], weight, preferred_element_type=F32).astype(BF16)  6.62 us
    concatenate x8, other arithmetic, local(): held = [jnp.concatenate([h, g]) for h, g in zip(held, got)]  3.72 us
  transfers between devices with their start and end apart: 42, of which 22 were waited for; matrix products, arithmetic and copies ran while one was open for 18% of the time, Pallas kernels for 0%

profile of v2, /device:TPU:0, one launch (start us, length us, event | category | flops | bytes accessed | tf_op | source)
XLA Modules:
  0.0 149.2 jit_solution(6985768479218196490)
XLA Ops:
  1.6 1.7 %collective-permute-start.2 = (bf16[1,64,512]{2,1,0:T(8,128)(2,1)S(1)}, bf16[1,64,512]{2,1,0:T(8,128)(2,1)}, u32[]{:S(2)}, u32[]{:S(2)}) collective-permute-start(bf16[1,64,512]{2,1,0:T(8,128)(2,1)S(1)} %get-tuple-element.50), channel_id=1, source_target_pairs={{0,4},{1,5},{2,6},{3,7},{4,0},{5,1},{6,2},{7,3},{8,12},{9,13},{10,... | collective-permute-start | bytes 196616 | tf_op jit(solution)/shard_map/ppermute | solution.py:18
  3.2 1.9 %collective-permute-start = (bf16[1,64,512]{2,1,0:T(8,128)(2,1)S(1)}, bf16[1,64,512]{2,1,0:T(8,128)(2,1)S(1)}, u32[]{:S(2)}, u32[]{:S(2)}) collective-permute-start(bf16[1,64,512]{2,1,0:T(8,128)(2,1)S(1)} %get-tuple-element.48), channel_id=1, source_target_pairs={{0,1},{1,0},{2,3},{3,2},{4,5},{5,4},{6,7},{7,6},{8,9},{9,8},{10,11... | collective-permute-start | bytes 196616 | tf_op jit(solution)/shard_map/ppermute | solution.py:18
  5.1 2.5 %collective-permute-start.1 = (bf16[1,64,512]{2,1,0:T(8,128)(2,1)S(1)}, bf16[1,64,512]{2,1,0:T(8,128)(2,1)}, u32[]{:S(2)}, u32[]{:S(2)}) collective-permute-start(bf16[1,64,512]{2,1,0:T(8,128)(2,1)S(1)} %get-tuple-element.49), channel_id=1, source_target_pairs={{0,3},{1,2},{2,1},{3,0},{4,7},{5,6},{6,5},{7,4},{8,11},{9,10},{10,... | collective-permute-start | bytes 196616 | tf_op jit(solution)/shard_map/ppermute | solution.py:18
  7.7 1.8 %convert_element_type.220 = f32[512,1536]{1,0:T(8,128)S(1)} convert(bf16[512,1536]{1,0:T(8,128)(2,1)} %param.4) | non-fusion elementwise | flops 786432 | bytes 4718592 | tf_op jit(solution)/shard_map/convert_element_type | solution.py:58
  13.6 1.5 collective-permute-start.4
  15.1 1.4 fusion.43
  17.0 1.6 %collective-permute-start.7 = (f32[1024]{0:T(1024)}, f32[1024]{0:T(1024)}, u32[]{:S(2)}, u32[]{:S(2)}) collective-permute-start(f32[1024]{0:T(1024)} %fusion.39), channel_id=1, source_target_pairs={{0,16},{8,24},{16,0},{24,8},{32,48},{40,56},{48,32},{56,40},{1,17}... | collective-permute-start | bytes 12296 | tf_op jit(solution)/shard_map/ppermute | solution.py:18
  18.6 2.3 %collective-permute-done.7 = f32[1024]{0:T(1024)} collective-permute-done((f32[1024]{0:T(1024)}, f32[1024]{0:T(1024)}, u32[]{:S(2)}, u32[]{:S(2)}) %collective-permute-start.7) | collective-permute-done | bytes 4128 | tf_op jit(solution)/shard_map/ppermute | solution.py:18
  23.6 3.2 %collective-permute-start.11 = (f32[1024]{0:T(1024)S(1)}, f32[1024]{0:T(1024)S(1)}, u32[]{:S(2)}, u32[]{:S(2)}) collective-permute-start(f32[1024]{0:T(1024)S(1)} %add.390), channel_id=1, source_target_pairs={{0,32},{8,40},{16,48},{24,56},{32,0},{40,8},{48,16},{56,24},{1,33}... | collective-permute-start | bytes 12296 | tf_op jit(solution)/shard_map/ppermute | solution.py:18
  26.8 1.5 collective-permute-start.8
  28.3 2.3 %collective-permute-start.10 = (bf16[4,64,512]{2,1,0:T(8,128)(2,1)S(1)}, bf16[4,64,512]{2,1,0:T(8,128)(2,1)S(1)}, u32[]{:S(2)}, u32[]{:S(2)}) collective-permute-start(bf16[4,64,512]{2,1,0:T(8,128)(2,1)S(1)} %pad_maximum_fusion.12), channel_id=1, source_target_pairs={{0,3},{1,2},{2,1},{3,0},{4,7},{5,6},{6,5},{7,4},{8,11},{9,10},{10,... | collective-permute-start | bytes 786440 | tf_op jit(solution)/shard_map/ppermute | solution.py:18
  33.3 1.3 collective-permute-done.9
  34.8 1.1 collective-permute-done.10
  36.3 6.6 %fusion.10 = bf16[256,3072]{1,0:T(8,128)(2,1)S(1)} fusion(bf16[1,1536,3072]{2,1,0:T(8,128)(2,1)} %param.6, bf16[512,1536]{1,0:T(8,128)(2,1)S(1)} %bitcast_select_fusion), kind=kOutput, calls=%fused_computation.11 | convolution fusion | flops 2416705536 | bytes 11796480 | tf_op jit(solution)/shard_map/dot_general | solution.py:88
  43.3 2.6 %fusion.8 = f32[256,3072]{1,0:T(8,128)S(1)} fusion(bf16[1,1536,3072]{2,1,0:T(8,128)(2,1)S(1)} %bitcast.57, bf16[512,1536]{1,0:T(8,128)(2,1)S(1)} %bitcast_select_fusion), kind=kOutput, calls=%fused_computation.9 | convolution fusion | flops 2415919104 | bytes 13369344 | tf_op jit(solution)/shard_map/dot_general | solution.py:90
  48.6 1.3 fusion.13
  50.0 1.2 collective-permute-done.15
  51.2 7.2 %collective-permute-done.13 = bf16[2,64,1536]{2,1,0:T(8,128)(2,1)S(1)} collective-permute-done((bf16[2,64,1536]{2,1,0:T(8,128)(2,1)S(1)}, bf16[2,64,1536]{2,1,0:T(8,128)(2,1)S(1)}, u32[]{:S(2)}, u32[]{:S(2)}) %collective-permute-start.13) | collective-permute-done | bytes 393248 | tf_op jit(solution)/shard_map/ppermute | solution.py:18
  58.4 1.6 %collective-permute-done.14 = bf16[2,64,1536]{2,1,0:T(8,128)(2,1)S(1)} collective-permute-done((bf16[2,64,1536]{2,1,0:T(8,128)(2,1)S(1)}, bf16[2,64,1536]{2,1,0:T(8,128)(2,1)S(1)}, u32[]{:S(2)}, u32[]{:S(2)}) %collective-permute-start.14) | collective-permute-done | bytes 393248 | tf_op jit(solution)/shard_map/ppermute | solution.py:18
  61.1 2.0 %collective-permute-start.18 = (f32[3072]{0:T(1024)S(1)}, f32[3072]{0:T(1024)S(1)}, u32[]{:S(2)}, u32[]{:S(2)}) collective-permute-start(f32[3072]{0:T(1024)S(1)} %add.430), channel_id=1, source_target_pairs={{0,16},{8,24},{16,0},{24,8},{32,48},{40,56},{48,32},{56,40},{1,17}... | collective-permute-start | bytes 36872 | tf_op jit(solution)/shard_map/ppermute | solution.py:18
  63.1 4.1 %collective-permute-done.18 = f32[3072]{0:T(1024)S(1)} collective-permute-done((f32[3072]{0:T(1024)S(1)}, f32[3072]{0:T(1024)S(1)}, u32[]{:S(2)}, u32[]{:S(2)}) %collective-permute-start.18) | collective-permute-done | bytes 12320 | tf_op jit(solution)/shard_map/ppermute | solution.py:18
  67.6 2.8 %collective-permute-start.19 = (bf16[64,3072]{1,0:T(8,128)(2,1)S(1)}, bf16[64,3072]{1,0:T(8,128)(2,1)S(1)}, u32[]{:S(2)}, u32[]{:S(2)}) collective-permute-start(bf16[64,3072]{1,0:T(8,128)(2,1)S(1)} %fusion.28), channel_id=1, source_target_pairs={{0,64},{64,0},{1,65},{65,1},{2,66},{66,2},{3,67},{67,3},{4,68},{68... | collective-permute-start | bytes 1179656 | tf_op jit(solution)/shard_map/ppermute | solution.py:18
  70.4 1.7 %collective-permute-start.22 = (f32[3072]{0:T(1024)S(1)}, f32[3072]{0:T(1024)S(1)}, u32[]{:S(2)}, u32[]{:S(2)}) collective-permute-start(f32[3072]{0:T(1024)S(1)} %add.438), channel_id=1, source_target_pairs={{0,32},{8,40},{16,48},{24,56},{32,0},{40,8},{48,16},{56,24},{1,33}... | collective-permute-start | bytes 36872 | tf_op jit(solution)/shard_map/ppermute | solution.py:18
  72.1 3.5 %collective-permute-done.22 = f32[3072]{0:T(1024)S(1)} collective-permute-done((f32[3072]{0:T(1024)S(1)}, f32[3072]{0:T(1024)S(1)}, u32[]{:S(2)}, u32[]{:S(2)}) %collective-permute-start.22) | collective-permute-done | bytes 12320 | tf_op jit(solution)/shard_map/ppermute | solution.py:18
  75.6 2.7 %collective-permute-done.19 = bf16[64,3072]{1,0:T(8,128)(2,1)S(1)} collective-permute-done((bf16[64,3072]{1,0:T(8,128)(2,1)S(1)}, bf16[64,3072]{1,0:T(8,128)(2,1)S(1)}, u32[]{:S(2)}, u32[]{:S(2)}) %collective-permute-start.19) | collective-permute-done | bytes 393248 | tf_op jit(solution)/shard_map/ppermute | solution.py:18
  80.0 1.8 %collective-permute-start.21 = (bf16[1,64,1536]{2,1,0:T(8,128)(2,1)S(1)}, bf16[1,64,1536]{2,1,0:T(8,128)(2,1)S(1)}, u32[]{:S(2)}, u32[]{:S(2)}) collective-permute-start(bf16[1,64,1536]{2,1,0:T(8,128)(2,1)S(1)} %get-tuple-element.134), channel_id=1, source_target_pairs={{0,48},{8,56},{16,32},{24,40},{32,16},{40,24},{48,0},{56,8},{1,49}... | collective-permute-start | bytes 589832 | tf_op jit(solution)/shard_map/ppermute | solution.py:18
  82.8 4.2 %collective-permute-done.21 = bf16[1,64,1536]{2,1,0:T(8,128)(2,1)S(1)} collective-permute-done((bf16[1,64,1536]{2,1,0:T(8,128)(2,1)S(1)}, bf16[1,64,1536]{2,1,0:T(8,128)(2,1)S(1)}, u32[]{:S(2)}, u32[]{:S(2)}) %collective-permute-start.21) | collective-permute-done | bytes 196640 | tf_op jit(solution)/shard_map/ppermute | solution.py:18
  87.1 2.4 %collective-permute-done.20 = bf16[1,64,1536]{2,1,0:T(8,128)(2,1)S(1)} collective-permute-done((bf16[1,64,1536]{2,1,0:T(8,128)(2,1)S(1)}, bf16[1,64,1536]{2,1,0:T(8,128)(2,1)S(1)}, u32[]{:S(2)}, u32[]{:S(2)}) %collective-permute-start.20) | collective-permute-done | bytes 196640 | tf_op jit(solution)/shard_map/ppermute | solution.py:18
  89.7 1.4 collective-permute-start.24
  91.0 2.9 %collective-permute-start.26 = (f32[128]{0:T(128)S(1)}, f32[128]{0:T(128)S(1)}, u32[]{:S(2)}, u32[]{:S(2)}) collective-permute-start(f32[128]{0:T(128)S(1)} %fusion.50), channel_id=1, source_target_pairs={{0,2},{1,3},{2,0},{3,1},{4,6},{5,7},{6,4},{7,5},{8,10},{9,11},{10,... | collective-permute-start | bytes 1544 | tf_op jit(solution)/shard_map/ppermute | solution.py:18
  94.0 2.1 %collective-permute-done.26 = f32[128]{0:T(128)S(1)} collective-permute-done((f32[128]{0:T(128)S(1)}, f32[128]{0:T(128)S(1)}, u32[]{:S(2)}, u32[]{:S(2)}) %collective-permute-start.26) | collective-permute-done | bytes 544 | tf_op jit(solution)/shard_map/ppermute | solution.py:18
  96.1 1.3 collective-permute-done.25
  97.5 1.2 collective-permute-done.24
  99.7 2.6 %fusion.2 = f32[256,1536]{1,0:T(8,128)S(1)} fusion(bf16[256,3072]{1,0:T(8,128)(2,1)S(1)} %pad_maximum_fusion.2, bf16[1,1536,3072]{2,1,0:T(8,128)(2,1)S(1)} %bitcast.57), kind=kOutput, calls=%fused_computation.3 | convolution fusion | flops 2415919104 | bytes 12582912 | tf_op jit(solution)/shard_map/dot_general | solution.py:148
  103.2 2.6 %fusion = f32[256,1536]{1,0:T(8,128)S(1)} fusion(bf16[256,3072]{1,0:T(8,128)(2,1)S(1)} %collective-permute-done.27, bf16[1,1536,3072]{2,1,0:T(8,128)(2,1)S(1)} %bitcast.57), kind=kOutput, calls=%fused_computation.1 | convolution fusion | flops 2415919104 | bytes 12582912 | tf_op jit(solution)/shard_map/dot_general | solution.py:149
  107.3 1.3 collective-permute-start.32
  109.4 1.9 %collective-permute-start.30 = (bf16[4,64,512]{2,1,0:T(8,128)(2,1)S(1)}, bf16[4,64,512]{2,1,0:T(8,128)(2,1)}, u32[]{:S(2)}, u32[]{:S(2)}) collective-permute-start(bf16[4,64,512]{2,1,0:T(8,128)(2,1)S(1)} %get-tuple-element.75), channel_id=1, source_target_pairs={{0,3},{1,2},{2,1},{3,0},{4,7},{5,6},{6,5},{7,4},{8,11},{9,10},{10,... | collective-permute-start | bytes 786440 | tf_op jit(solution)/shard_map/ppermute | solution.py:18
  111.3 1.1 collective-permute-start.31
  112.4 7.5 %convolution_convert_fusion = bf16[1536,3072]{1,0:T(8,128)(2,1)} fusion(bf16[512,1536]{1,0:T(8,128)(2,1)S(1)} %bitcast_select_fusion, bf16[512,3072]{1,0:T(8,128)(2,1)S(1)} %pad_maximum_fusion.1), kind=kOutput, calls=%fused_computation | convolution fusion | flops 4836556800 | bytes 14155776 | tf_op jit(solution)/shard_map/dot_general | solution.py:175
  120.6 1.1 add_convert_fusion.4
  123.7 1.3 collective-permute-start.33
  125.9 3.3 %collective-permute-start.36 = (f32[1536]{0:T(1024)}, f32[1536]{0:T(1024)}, u32[]{:S(2)}, u32[]{:S(2)}) collective-permute-start(f32[1536]{0:T(1024)} %add.450), channel_id=1, source_target_pairs={{0,2},{1,3},{2,0},{3,1},{4,6},{5,7},{6,4},{7,5},{8,10},{9,11},{10,... | collective-permute-start | bytes 18440 | tf_op jit(solution)/shard_map/ppermute | solution.py:18
  129.2 3.3 %collective-permute-done.36 = f32[1536]{0:T(1024)} collective-permute-done((f32[1536]{0:T(1024)}, f32[1536]{0:T(1024)}, u32[]{:S(2)}, u32[]{:S(2)}) %collective-permute-start.36) | collective-permute-done | bytes 6176 | tf_op jit(solution)/shard_map/ppermute | solution.py:18
  134.3 1.3 collective-permute-start.40
  137.2 3.5 %collective-permute-start.41 = (f32[1536]{0:T(1024)S(1)}, f32[1536]{0:T(1024)S(1)}, u32[]{:S(2)}, u32[]{:S(2)}) collective-permute-start(f32[1536]{0:T(1024)S(1)} %add.458), channel_id=1, source_target_pairs={{0,4},{1,5},{2,6},{3,7},{4,0},{5,1},{6,2},{7,3},{8,12},{9,13},{10,... | collective-permute-start | bytes 18440 | tf_op jit(solution)/shard_map/ppermute | solution.py:18
  140.7 3.4 %collective-permute-start.39 = (bf16[1,64,512]{2,1,0:T(8,128)(2,1)S(1)}, bf16[1,64,512]{2,1,0:T(8,128)(2,1)S(1)}, u32[]{:S(2)}, u32[]{:S(2)}) collective-permute-start(bf16[1,64,512]{2,1,0:T(8,128)(2,1)S(1)} %get-tuple-element.89), channel_id=1, source_target_pairs={{0,3},{1,2},{2,1},{3,0},{4,7},{5,6},{6,5},{7,4},{8,11},{9,10},{10,... | collective-permute-start | bytes 196616 | tf_op jit(solution)/shard_map/ppermute | solution.py:18
  145.0 1.3 collective-permute-done.39
  147.4 1.8 %fusion.38 = bf16[1,64,1536]{2,1,0:T(8,128)(2,1)} fusion(f32[64]{0:T(128)S(1)} %get-tuple-element.145, f32[64]{0:T(128)S(1)} %dynamic_slice.139, bf16[512,1536]{1,0:T(8,128)(2,1)} %param.4, s32[]{:T(128)S(6)} %select_n.428, f32[64]{0:T(128)S(1)} %get-tuple-element.144, f32[64]{0:T(128)S(1)} %dynamic_slice.137, f32[1536]{0:T(1024)S(1)} %get-tuple-element.140, ...), kind=kLoop, calls=%fused_computation.79 | loop fusion | flops 1277952 | bytes 793605 | tf_op jit(solution)/shard_map/broadcast_in_dim | solution.py:196
  (156 shorter events, 31.1 us)
Async XLA Ops:
  1.6 11.2 %copy-start = (bf16[1,64,512]{2,1,0:T(8,128)(2,1)}, bf16[1,64,512]{2,1,0:T(8,128)(2,1)S(1)}, u32[]{:S(2)}) copy-start(bf16[1,64,512]{2,1,0:T(8,128)(2,1)S(1)} %get-tuple-element.50) | copy-start | bytes 196612
  1.6 11.2 %collective-permute-start.2 = (bf16[1,64,512]{2,1,0:T(8,128)(2,1)S(1)}, bf16[1,64,512]{2,1,0:T(8,128)(2,1)}, u32[]{:S(2)}, u32[]{:S(2)}) collective-permute-start(bf16[1,64,512]{2,1,0:T(8,128)(2,1)S(1)} %get-tuple-element.50), channel_id=1, source_target_pairs={{0,4},{1,5},{2,6},{3,7},{4,0},{5,1},{6,2},{7,3},{8,12},{9,13},{10,... | collective-permute-start | bytes 196616 | tf_op jit(solution)/shard_map/ppermute | solution.py:18
  3.2 8.6 %collective-permute-start = (bf16[1,64,512]{2,1,0:T(8,128)(2,1)S(1)}, bf16[1,64,512]{2,1,0:T(8,128)(2,1)S(1)}, u32[]{:S(2)}, u32[]{:S(2)}) collective-permute-start(bf16[1,64,512]{2,1,0:T(8,128)(2,1)S(1)} %get-tuple-element.48), channel_id=1, source_target_pairs={{0,1},{1,0},{2,3},{3,2},{4,5},{5,4},{6,7},{7,6},{8,9},{9,8},{10,11... | collective-permute-start | bytes 196616 | tf_op jit(solution)/shard_map/ppermute | solution.py:18
  5.1 6.7 %collective-permute-start.1 = (bf16[1,64,512]{2,1,0:T(8,128)(2,1)S(1)}, bf16[1,64,512]{2,1,0:T(8,128)(2,1)}, u32[]{:S(2)}, u32[]{:S(2)}) collective-permute-start(bf16[1,64,512]{2,1,0:T(8,128)(2,1)S(1)} %get-tuple-element.49), channel_id=1, source_target_pairs={{0,3},{1,2},{2,1},{3,0},{4,7},{5,6},{6,5},{7,4},{8,11},{9,10},{10,... | collective-permute-start | bytes 196616 | tf_op jit(solution)/shard_map/ppermute | solution.py:18
  10.0 1.2 collective-permute-start.3
  13.6 8.0 %collective-permute-start.4 = (bf16[2,64,512]{2,1,0:T(8,128)(2,1)S(1)}, bf16[2,64,512]{2,1,0:T(8,128)(2,1)}, u32[]{:S(2)}, u32[]{:S(2)}) collective-permute-start(bf16[2,64,512]{2,1,0:T(8,128)(2,1)S(1)} %pad_maximum_fusion.16), channel_id=1, source_target_pairs={{0,3},{1,2},{2,1},{3,0},{4,7},{5,6},{6,5},{7,4},{8,11},{9,10},{10,... | collective-permute-start | bytes 393224 | tf_op jit(solution)/shard_map/ppermute | solution.py:18
  16.5 6.1 %collective-permute-start.5 = (bf16[2,64,512]{2,1,0:T(8,128)(2,1)S(1)}, bf16[2,64,512]{2,1,0:T(8,128)(2,1)}, u32[]{:S(2)}, u32[]{:S(2)}) collective-permute-start(bf16[2,64,512]{2,1,0:T(8,128)(2,1)S(1)} %pad_maximum_fusion.17), channel_id=1, source_target_pairs={{0,4},{1,5},{2,6},{3,7},{4,0},{5,1},{6,2},{7,3},{8,12},{9,13},{10,... | collective-permute-start | bytes 393224 | tf_op jit(solution)/shard_map/ppermute | solution.py:18
  17.0 3.9 %collective-permute-start.7 = (f32[1024]{0:T(1024)}, f32[1024]{0:T(1024)}, u32[]{:S(2)}, u32[]{:S(2)}) collective-permute-start(f32[1024]{0:T(1024)} %fusion.39), channel_id=1, source_target_pairs={{0,16},{8,24},{16,0},{24,8},{32,48},{40,56},{48,32},{56,40},{1,17}... | collective-permute-start | bytes 12296 | tf_op jit(solution)/shard_map/ppermute | solution.py:18
  18.6 5.0 %collective-permute-start.6 = (bf16[2,64,512]{2,1,0:T(8,128)(2,1)S(1)}, bf16[2,64,512]{2,1,0:T(8,128)(2,1)S(1)}, u32[]{:S(2)}, u32[]{:S(2)}) collective-permute-start(bf16[2,64,512]{2,1,0:T(8,128)(2,1)S(1)} %pad_maximum_fusion.18), channel_id=1, source_target_pairs={{0,1},{1,0},{2,3},{3,2},{4,5},{5,4},{6,7},{7,6},{8,9},{9,8},{10,11... | collective-permute-start | bytes 393224 | tf_op jit(solution)/shard_map/ppermute | solution.py:18
  23.6 7.2 %collective-permute-start.11 = (f32[1024]{0:T(1024)S(1)}, f32[1024]{0:T(1024)S(1)}, u32[]{:S(2)}, u32[]{:S(2)}) collective-permute-start(f32[1024]{0:T(1024)S(1)} %add.390), channel_id=1, source_target_pairs={{0,32},{8,40},{16,48},{24,56},{32,0},{40,8},{48,16},{56,24},{1,33}... | collective-permute-start | bytes 12296 | tf_op jit(solution)/shard_map/ppermute | solution.py:18
  26.8 6.4 %collective-permute-start.8 = (bf16[4,64,512]{2,1,0:T(8,128)(2,1)S(1)}, bf16[4,64,512]{2,1,0:T(8,128)(2,1)S(1)}, u32[]{:S(2)}, u32[]{:S(2)}) collective-permute-start(bf16[4,64,512]{2,1,0:T(8,128)(2,1)S(1)} %pad_maximum_fusion.10), channel_id=1, source_target_pairs={{0,4},{1,5},{2,6},{3,7},{4,0},{5,1},{6,2},{7,3},{8,12},{9,13},{10,... | collective-permute-start | bytes 786440 | tf_op jit(solution)/shard_map/ppermute | solution.py:18
  28.3 6.4 %collective-permute-start.9 = (bf16[4,64,512]{2,1,0:T(8,128)(2,1)S(1)}, bf16[4,64,512]{2,1,0:T(8,128)(2,1)S(1)}, u32[]{:S(2)}, u32[]{:S(2)}) collective-permute-start(bf16[4,64,512]{2,1,0:T(8,128)(2,1)S(1)} %pad_maximum_fusion.11), channel_id=1, source_target_pairs={{0,1},{1,0},{2,3},{3,2},{4,5},{5,4},{6,7},{7,6},{8,9},{9,8},{10,11... | collective-permute-start | bytes 786440 | tf_op jit(solution)/shard_map/ppermute | solution.py:18
  28.3 7.6 %collective-permute-start.10 = (bf16[4,64,512]{2,1,0:T(8,128)(2,1)S(1)}, bf16[4,64,512]{2,1,0:T(8,128)(2,1)S(1)}, u32[]{:S(2)}, u32[]{:S(2)}) collective-permute-start(bf16[4,64,512]{2,1,0:T(8,128)(2,1)S(1)} %pad_maximum_fusion.12), channel_id=1, source_target_pairs={{0,3},{1,2},{2,1},{3,0},{4,7},{5,6},{6,5},{7,4},{8,11},{9,10},{10,... | collective-permute-start | bytes 786440 | tf_op jit(solution)/shard_map/ppermute | solution.py:18
  30.8 0.6 copy-start.3
  36.0 7.3 %slice-start = ((s8[9437184]{0:T(1024)(128)(4,1)}), s8[4194304]{0:T(1024)(128)(4,1)S(1)}, s32[]{:S(2)}) async-start(s8[9437184]{0:T(1024)(128)(4,1)} %bitcast.56), calls=%async_computation | async-start | bytes 8388608
  36.2 6.9 %copy-start.1 = (bf16[1,1536]{1,0:T(2,128)(2,1)S(1)}, bf16[1,1536]{1,0:T(2,128)(2,1)}, u32[]{:S(2)}) copy-start(bf16[1,1536]{1,0:T(2,128)(2,1)} %get-tuple-element.141) | copy-start | bytes 9220
  36.3 7.0 %slice-start.1 = ((s8[9437184]{0:T(1024)(128)(4,1)}), s8[4194304]{0:T(1024)(128)(4,1)S(1)}, s32[]{:S(2)}) async-start(s8[9437184]{0:T(1024)(128)(4,1)} %bitcast.56), calls=%async_computation.1 | async-start | bytes 8388608
  36.3 7.0 %slice-start.2 = ((s8[9437184]{0:T(1024)(128)(4,1)}), s8[1048576]{0:T(1024)(128)(4,1)S(1)}, s32[]{:S(2)}) async-start(s8[9437184]{0:T(1024)(128)(4,1)} %bitcast.56), calls=%async_computation.2 | async-start | bytes 2097152
  42.9 3.5 %collective-permute-start.12 = (bf16[256,3072]{1,0:T(8,128)(2,1)S(1)}, bf16[256,3072]{1,0:T(8,128)(2,1)S(1)}, u32[]{:S(2)}, u32[]{:S(2)}) collective-permute-start(bf16[256,3072]{1,0:T(8,128)(2,1)S(1)} %fusion.10), channel_id=1, source_target_pairs={{0,8},{8,0},{16,24},{24,16},{32,40},{40,32},{48,56},{56,48},{1,9},... | collective-permute-start | bytes 4718600 | tf_op jit(solution)/shard_map/ppermute | solution.py:18
  47.2 11.2 %collective-permute-start.13 = (bf16[2,64,1536]{2,1,0:T(8,128)(2,1)S(1)}, bf16[2,64,1536]{2,1,0:T(8,128)(2,1)S(1)}, u32[]{:S(2)}, u32[]{:S(2)}) collective-permute-start(bf16[2,64,1536]{2,1,0:T(8,128)(2,1)S(1)} %pad_maximum_fusion.6), channel_id=1, source_target_pairs={{0,16},{8,24},{16,0},{24,8},{32,48},{40,56},{48,32},{56,40},{1,17}... | collective-permute-start | bytes 1179656 | tf_op jit(solution)/shard_map/ppermute | solution.py:18
  47.9 12.1 %collective-permute-start.14 = (bf16[2,64,1536]{2,1,0:T(8,128)(2,1)S(1)}, bf16[2,64,1536]{2,1,0:T(8,128)(2,1)S(1)}, u32[]{:S(2)}, u32[]{:S(2)}) collective-permute-start(bf16[2,64,1536]{2,1,0:T(8,128)(2,1)S(1)} %slice.282), channel_id=1, source_target_pairs={{0,48},{8,56},{16,32},{24,40},{32,16},{40,24},{48,0},{56,8},{1,49}... | collective-permute-start | bytes 1179656 | tf_op jit(solution)/shard_map/ppermute | solution.py:18
  49.9 1.3 collective-permute-start.15
  60.1 7.1 %collective-permute-start.16 = (bf16[1,64,1536]{2,1,0:T(8,128)(2,1)S(1)}, bf16[1,64,1536]{2,1,0:T(8,128)(2,1)S(1)}, u32[]{:S(2)}, u32[]{:S(2)}) collective-permute-start(bf16[1,64,1536]{2,1,0:T(8,128)(2,1)S(1)} %get-tuple-element.63), channel_id=1, source_target_pairs={{0,48},{8,56},{16,32},{24,40},{32,16},{40,24},{48,0},{56,8},{1,49}... | collective-permute-start | bytes 589832 | tf_op jit(solution)/shard_map/ppermute | solution.py:18
  61.1 6.1 %collective-permute-start.17 = (bf16[1,64,1536]{2,1,0:T(8,128)(2,1)S(1)}, bf16[1,64,1536]{2,1,0:T(8,128)(2,1)S(1)}, u32[]{:S(2)}, u32[]{:S(2)}) collective-permute-start(bf16[1,64,1536]{2,1,0:T(8,128)(2,1)S(1)} %get-tuple-element.64), channel_id=1, source_target_pairs={{0,16},{8,24},{16,0},{24,8},{32,48},{40,56},{48,32},{56,40},{1,17}... | collective-permute-start | bytes 589832 | tf_op jit(solution)/shard_map/ppermute | solution.py:18
  61.1 6.1 %collective-permute-start.18 = (f32[3072]{0:T(1024)S(1)}, f32[3072]{0:T(1024)S(1)}, u32[]{:S(2)}, u32[]{:S(2)}) collective-permute-start(f32[3072]{0:T(1024)S(1)} %add.430), channel_id=1, source_target_pairs={{0,16},{8,24},{16,0},{24,8},{32,48},{40,56},{48,32},{56,40},{1,17}... | collective-permute-start | bytes 36872 | tf_op jit(solution)/shard_map/ppermute | solution.py:18
  67.6 10.7 %collective-permute-start.19 = (bf16[64,3072]{1,0:T(8,128)(2,1)S(1)}, bf16[64,3072]{1,0:T(8,128)(2,1)S(1)}, u32[]{:S(2)}, u32[]{:S(2)}) collective-permute-start(bf16[64,3072]{1,0:T(8,128)(2,1)S(1)} %fusion.28), channel_id=1, source_target_pairs={{0,64},{64,0},{1,65},{65,1},{2,66},{66,2},{3,67},{67,3},{4,68},{68... | collective-permute-start | bytes 1179656 | tf_op jit(solution)/shard_map/ppermute | solution.py:18
  70.4 5.2 %collective-permute-start.22 = (f32[3072]{0:T(1024)S(1)}, f32[3072]{0:T(1024)S(1)}, u32[]{:S(2)}, u32[]{:S(2)}) collective-permute-start(f32[3072]{0:T(1024)S(1)} %add.438), channel_id=1, source_target_pairs={{0,32},{8,40},{16,48},{24,56},{32,0},{40,8},{48,16},{56,24},{1,33}... | collective-permute-start | bytes 36872 | tf_op jit(solution)/shard_map/ppermute | solution.py:18
  79.2 3.6 %collective-permute-start.23 = (f32[128]{0:T(128)S(1)}, f32[128]{0:T(128)S(1)}, u32[]{:S(2)}, u32[]{:S(2)}) collective-permute-start(f32[128]{0:T(128)S(1)} %pad_maximum_fusion.23), channel_id=1, source_target_pairs={{0,1},{1,0},{2,3},{3,2},{4,5},{5,4},{6,7},{7,6},{8,9},{9,8},{10,11... | collective-permute-start | bytes 1544 | tf_op jit(solution)/shard_map/ppermute | solution.py:18
  80.0 7.0 %collective-permute-start.21 = (bf16[1,64,1536]{2,1,0:T(8,128)(2,1)S(1)}, bf16[1,64,1536]{2,1,0:T(8,128)(2,1)S(1)}, u32[]{:S(2)}, u32[]{:S(2)}) collective-permute-start(bf16[1,64,1536]{2,1,0:T(8,128)(2,1)S(1)} %get-tuple-element.134), channel_id=1, source_target_pairs={{0,48},{8,56},{16,32},{24,40},{32,16},{40,24},{48,0},{56,8},{1,49}... | collective-permute-start | bytes 589832 | tf_op jit(solution)/shard_map/ppermute | solution.py:18
  81.9 7.6 %collective-permute-start.20 = (bf16[1,64,1536]{2,1,0:T(8,128)(2,1)S(1)}, bf16[1,64,1536]{2,1,0:T(8,128)(2,1)S(1)}, u32[]{:S(2)}, u32[]{:S(2)}) collective-permute-start(bf16[1,64,1536]{2,1,0:T(8,128)(2,1)S(1)} %get-tuple-element.135), channel_id=1, source_target_pairs={{0,16},{8,24},{16,0},{24,8},{32,48},{40,56},{48,32},{56,40},{1,17}... | collective-permute-start | bytes 589832 | tf_op jit(solution)/shard_map/ppermute | solution.py:18
  89.6 7.9 %collective-permute-start.25 = (bf16[2,64,1536]{2,1,0:T(8,128)(2,1)S(1)}, bf16[2,64,1536]{2,1,0:T(8,128)(2,1)S(1)}, u32[]{:S(2)}, u32[]{:S(2)}) collective-permute-start(bf16[2,64,1536]{2,1,0:T(8,128)(2,1)S(1)} %pad_maximum_fusion.8), channel_id=1, source_target_pairs={{0,16},{8,24},{16,0},{24,8},{32,48},{40,56},{48,32},{56,40},{1,17}... | collective-permute-start | bytes 1179656 | tf_op jit(solution)/shard_map/ppermute | solution.py:18
  89.7 9.1 %collective-permute-start.24 = (bf16[2,64,1536]{2,1,0:T(8,128)(2,1)S(1)}, bf16[2,64,1536]{2,1,0:T(8,128)(2,1)S(1)}, u32[]{:S(2)}, u32[]{:S(2)}) collective-permute-start(bf16[2,64,1536]{2,1,0:T(8,128)(2,1)S(1)} %pad_maximum_fusion.7), channel_id=1, source_target_pairs={{0,48},{8,56},{16,32},{24,40},{32,16},{40,24},{48,0},{56,8},{1,49}... | collective-permute-start | bytes 1179656 | tf_op jit(solution)/shard_map/ppermute | solution.py:18
  91.0 5.0 %collective-permute-start.26 = (f32[128]{0:T(128)S(1)}, f32[128]{0:T(128)S(1)}, u32[]{:S(2)}, u32[]{:S(2)}) collective-permute-start(f32[128]{0:T(128)S(1)} %fusion.50), channel_id=1, source_target_pairs={{0,2},{1,3},{2,0},{3,1},{4,6},{5,7},{6,4},{7,5},{8,10},{9,11},{10,... | collective-permute-start | bytes 1544 | tf_op jit(solution)/shard_map/ppermute | solution.py:18
  99.0 4.2 %collective-permute-start.27 = (bf16[256,3072]{1,0:T(8,128)(2,1)S(1)}, bf16[256,3072]{1,0:T(8,128)(2,1)S(1)}, u32[]{:S(2)}, u32[]{:S(2)}) collective-permute-start(bf16[256,3072]{1,0:T(8,128)(2,1)S(1)} %pad_maximum_fusion.2), channel_id=1, source_target_pairs={{0,8},{8,0},{16,24},{24,16},{32,40},{40,32},{48,56},{56,48},{1,9},... | collective-permute-start | bytes 4718600 | tf_op jit(solution)/shard_map/ppermute | solution.py:18
  99.1 3.6 %collective-permute-start.28 = (f32[128]{0:T(128)S(1)}, f32[128]{0:T(128)S(1)}, u32[]{:S(2)}, u32[]{:S(2)}) collective-permute-start(f32[128]{0:T(128)S(1)} %add.441), channel_id=1, source_target_pairs={{0,4},{1,5},{2,6},{3,7},{4,0},{5,1},{6,2},{7,3},{8,12},{9,13},{10,... | collective-permute-start | bytes 1544 | tf_op jit(solution)/shard_map/ppermute | solution.py:18
  107.3 12.7 %collective-permute-start.32 = (f32[1536]{0:T(1024)S(1)}, f32[1536]{0:T(1024)S(1)}, u32[]{:S(2)}, u32[]{:S(2)}) collective-permute-start(f32[1536]{0:T(1024)S(1)} %div.258), channel_id=1, source_target_pairs={{0,1},{1,0},{2,3},{3,2},{4,5},{5,4},{6,7},{7,6},{8,9},{9,8},{10,11... | collective-permute-start | bytes 18440 | tf_op jit(solution)/shard_map/ppermute | solution.py:18
  108.6 12.0 %collective-permute-start.29 = (bf16[4,64,512]{2,1,0:T(8,128)(2,1)S(1)}, bf16[4,64,512]{2,1,0:T(8,128)(2,1)S(1)}, u32[]{:S(2)}, u32[]{:S(2)}) collective-permute-start(bf16[4,64,512]{2,1,0:T(8,128)(2,1)S(1)} %get-tuple-element.74), channel_id=1, source_target_pairs={{0,1},{1,0},{2,3},{3,2},{4,5},{5,4},{6,7},{7,6},{8,9},{9,8},{10,11... | collective-permute-start | bytes 786440 | tf_op jit(solution)/shard_map/ppermute | solution.py:18
  109.4 11.2 %collective-permute-start.30 = (bf16[4,64,512]{2,1,0:T(8,128)(2,1)S(1)}, bf16[4,64,512]{2,1,0:T(8,128)(2,1)}, u32[]{:S(2)}, u32[]{:S(2)}) collective-permute-start(bf16[4,64,512]{2,1,0:T(8,128)(2,1)S(1)} %get-tuple-element.75), channel_id=1, source_target_pairs={{0,3},{1,2},{2,1},{3,0},{4,7},{5,6},{6,5},{7,4},{8,11},{9,10},{10,... | collective-permute-start | bytes 786440 | tf_op jit(solution)/shard_map/ppermute | solution.py:18
  111.3 9.3 %collective-permute-start.31 = (bf16[4,64,512]{2,1,0:T(8,128)(2,1)S(1)}, bf16[4,64,512]{2,1,0:T(8,128)(2,1)}, u32[]{:S(2)}, u32[]{:S(2)}) collective-permute-start(bf16[4,64,512]{2,1,0:T(8,128)(2,1)S(1)} %pad_maximum_fusion.15), channel_id=1, source_target_pairs={{0,4},{1,5},{2,6},{3,7},{4,0},{5,1},{6,2},{7,3},{8,12},{9,13},{10,... | collective-permute-start | bytes 786440 | tf_op jit(solution)/shard_map/ppermute | solution.py:18
  123.7 9.6 %collective-permute-start.33 = (bf16[2,64,512]{2,1,0:T(8,128)(2,1)}, bf16[2,64,512]{2,1,0:T(8,128)(2,1)S(1)}, u32[]{:S(2)}, u32[]{:S(2)}) collective-permute-start(bf16[2,64,512]{2,1,0:T(8,128)(2,1)} %pad_maximum_fusion.19), channel_id=1, source_target_pairs={{0,3},{1,2},{2,1},{3,0},{4,7},{5,6},{6,5},{7,4},{8,11},{9,10},{10,... | collective-permute-start | bytes 393224 | tf_op jit(solution)/shard_map/ppermute | solution.py:18
  125.0 8.3 %collective-permute-start.34 = (bf16[2,64,512]{2,1,0:T(8,128)(2,1)}, bf16[2,64,512]{2,1,0:T(8,128)(2,1)}, u32[]{:S(2)}, u32[]{:S(2)}) collective-permute-start(bf16[2,64,512]{2,1,0:T(8,128)(2,1)} %pad_maximum_fusion.20), channel_id=1, source_target_pairs={{0,4},{1,5},{2,6},{3,7},{4,0},{5,1},{6,2},{7,3},{8,12},{9,13},{10,... | collective-permute-start | bytes 393224 | tf_op jit(solution)/shard_map/ppermute | solution.py:18
  125.9 7.4 %collective-permute-start.35 = (bf16[2,64,512]{2,1,0:T(8,128)(2,1)}, bf16[2,64,512]{2,1,0:T(8,128)(2,1)}, u32[]{:S(2)}, u32[]{:S(2)}) collective-permute-start(bf16[2,64,512]{2,1,0:T(8,128)(2,1)} %pad_maximum_fusion.21), channel_id=1, source_target_pairs={{0,1},{1,0},{2,3},{3,2},{4,5},{5,4},{6,7},{7,6},{8,9},{9,8},{10,11... | collective-permute-start | bytes 393224 | tf_op jit(solution)/shard_map/ppermute | solution.py:18
  125.9 6.7 %collective-permute-start.36 = (f32[1536]{0:T(1024)}, f32[1536]{0:T(1024)}, u32[]{:S(2)}, u32[]{:S(2)}) collective-permute-start(f32[1536]{0:T(1024)} %add.450), channel_id=1, source_target_pairs={{0,2},{1,3},{2,0},{3,1},{4,6},{5,7},{6,4},{7,5},{8,10},{9,11},{10,... | collective-permute-start | bytes 18440 | tf_op jit(solution)/shard_map/ppermute | solution.py:18
  134.3 9.7 %collective-permute-start.40 = (f32[128]{0:T(128)}, f32[128]{0:T(128)S(1)}, u32[]{:S(2)}, u32[]{:S(2)}) collective-permute-start(f32[128]{0:T(128)} %add.442), channel_id=1, source_target_pairs={{0,0},{1,8},{2,16},{3,24},{4,32},{5,40},{6,48},{7,56},{8,1},{9,9},... | collective-permute-start | bytes 1544 | tf_op jit(solution)/shard_map/ppermute | solution.py:24
  137.2 7.0 %collective-permute-start.41 = (f32[1536]{0:T(1024)S(1)}, f32[1536]{0:T(1024)S(1)}, u32[]{:S(2)}, u32[]{:S(2)}) collective-permute-start(f32[1536]{0:T(1024)S(1)} %add.458), channel_id=1, source_target_pairs={{0,4},{1,5},{2,6},{3,7},{4,0},{5,1},{6,2},{7,3},{8,12},{9,13},{10,... | collective-permute-start | bytes 18440 | tf_op jit(solution)/shard_map/ppermute | solution.py:18
  140.7 4.3 %collective-permute-start.37 = (bf16[1,64,512]{2,1,0:T(8,128)(2,1)S(1)}, bf16[1,64,512]{2,1,0:T(8,128)(2,1)S(1)}, u32[]{:S(2)}, u32[]{:S(2)}) collective-permute-start(bf16[1,64,512]{2,1,0:T(8,128)(2,1)S(1)} %get-tuple-element.87), channel_id=1, source_target_pairs={{0,4},{1,5},{2,6},{3,7},{4,0},{5,1},{6,2},{7,3},{8,12},{9,13},{10,... | collective-permute-start | bytes 196616 | tf_op jit(solution)/shard_map/ppermute | solution.py:18
  140.7 4.3 %collective-permute-start.38 = (bf16[1,64,512]{2,1,0:T(8,128)(2,1)S(1)}, bf16[1,64,512]{2,1,0:T(8,128)(2,1)S(1)}, u32[]{:S(2)}, u32[]{:S(2)}) collective-permute-start(bf16[1,64,512]{2,1,0:T(8,128)(2,1)S(1)} %get-tuple-element.88), channel_id=1, source_target_pairs={{0,1},{1,0},{2,3},{3,2},{4,5},{5,4},{6,7},{7,6},{8,9},{9,8},{10,11... | collective-permute-start | bytes 196616 | tf_op jit(solution)/shard_map/ppermute | solution.py:18
  140.7 5.6 %collective-permute-start.39 = (bf16[1,64,512]{2,1,0:T(8,128)(2,1)S(1)}, bf16[1,64,512]{2,1,0:T(8,128)(2,1)S(1)}, u32[]{:S(2)}, u32[]{:S(2)}) collective-permute-start(bf16[1,64,512]{2,1,0:T(8,128)(2,1)S(1)} %get-tuple-element.89), channel_id=1, source_target_pairs={{0,3},{1,2},{2,1},{3,0},{4,7},{5,6},{6,5},{7,4},{8,11},{9,10},{10,... | collective-permute-start | bytes 196616 | tf_op jit(solution)/shard_map/ppermute | solution.py:18
  (1 other events, 0.6 us)

commit v3 on v0

v3 whole, which is shorter than its diff:
```python
import jax
import jax.numpy as jnp
from jax import lax
from jax.sharding import PartitionSpec as P

D = 12288
F32 = jnp.float32
BF16 = jnp.bfloat16
CHUNKS = 2
COL_ORDERS = ((1, 3, 4), (3, 4, 1), (4, 1, 3))
CONTRACT_LAST = (((1,), (1,)), ((), ()))
CONTRACT_FIRST = (((0,), (0,)), ((), ()))


def exchange(block, axis, mask):
    ranks = range(lax.axis_size(axis))
    return lax.ppermute(block, axis, [(i, i ^ mask) for i in ranks])


def mask_of(core, turn):
    return 1 + 2 * (core ^ turn)


def over_y(block, turn):
    ranks = range(lax.axis_size("row"))
    return lax.ppermute(block, "row", [(i, i ^ (2 * mask_of(i % 2, turn))) for i in ranks])


def over_z(block, turn):
    rows, cols = lax.axis_size("row"), lax.axis_size("col")
    route = [
        (r * cols + c, r * cols + (c ^ mask_of(r % 2, turn)))
        for r in range(rows)
        for c in range(cols)
    ]
    return lax.ppermute(block, ("row", "col"), route)


def activation(values):
    return jax.nn.gelu(values, approximate=True)


def local(tokens, vectors, weights, cotangent):
    second = lax.axis_index("section") == 1
    row = lax.axis_index("row")
    col = lax.axis_index("col")
    core = row % 2
    weight = weights[0]
    own_vector = vectors[0]
    features, hidden = weight.shape
    block_rows = cotangent.shape[0]
    n = block_rows // CHUNKS
    total_rows = tokens.shape[0]
    chunks = range(CHUNKS)
    first, then = mask_of(core, 0), mask_of(core, 1)
    col_order = [6, 2, first ^ 4, first, then ^ 4, then, 4, 0]

    def block_at(place):
        other, q = place // 4, place % 4
        y = (2, mask_of(core ^ other, 0), mask_of(core ^ other, 1), 0)[q]
        return row ^ (2 * y + other)

    def place_of(block):
        relative = block ^ row
        y, other = relative // 2, relative % 2
        odd = 1 + ((y // 2) ^ core ^ other)
        return other * 4 + jnp.where(y % 2 == 1, odd, jnp.where(y == 2, 0, 3))

    width = features // 3
    held = [cotangent[None, :, i * width : (i + 1) * width] for i in range(3)]
    relative = [[0], [0], [0]]
    for step in range(3):
        got = [exchange(held[i], "col", order[step]) for i, order in enumerate(COL_ORDERS)]
        if step == 1:
            inputs = tokens.astype(F32)
            sums = jnp.concatenate([jnp.sum(inputs, axis=1), jnp.sum(inputs * inputs, axis=1)])
            sums = sums + exchange(sums, "row", 1)
            image_start = jnp.sum(weight[:8].astype(F32) * own_vector[:8, None], axis=0)
        held = [jnp.concatenate([h, g]) for h, g in zip(held, got)]
        relative = [
            rel + [order[step] ^ r for r in rel] for rel, order in zip(relative, COL_ORDERS)
        ]
        if step == 0:
            held, tokens, own_vector = lax.optimization_barrier((held, tokens, own_vector))
        if step == 1:
            held, sums, image_start = lax.optimization_barrier((held, sums, image_start))
    sums = sums + exchange(sums, "row", 2)
    sums = sums + exchange(sums, "row", 4)
    whole = jnp.zeros((8, block_rows, features), BF16)
    for i in range(3):
        for k, r in enumerate(relative[i]):
            whole = lax.dynamic_update_slice(
                whole, held[i][k : k + 1], (place_of(col ^ r), 0, i * width)
            )
    mean, square = sums[:total_rows] / D, sums[total_rows:] / D
    inv_std = lax.rsqrt(square - mean * mean + 1e-05)
    normed_rows = ((inputs - mean[:, None]) * inv_std[:, None] * own_vector).astype(BF16)
    cots, norms = [], []
    for c in chunks:
        cots.append(whole[:, c * n : (c + 1) * n].reshape(8 * n, features))
        norms.append(
            jnp.concatenate(
                [
                    lax.dynamic_slice_in_dim(normed_rows, block_at(k) * block_rows + c * n, n, 0)
                    for k in range(8)
                ]
            )
        )

    both, sent = [], []
    for c in chunks:
        left = jnp.where(second, cots[c], norms[c])
        partial = jnp.dot(left, weight, preferred_element_type=F32)
        partial = lax.optimization_barrier(partial)
        both.append(partial[: 4 * n])
        sent.append(exchange(partial[4 * n :].astype(BF16), "row", 1))
    both = [(b + g.astype(F32)).reshape(4, n, hidden) for b, g in zip(both, sent)]
    send = [b[:2].astype(BF16) for b in both]
    later = jnp.where(lax.iota(jnp.int32, features) < 8, 0.0, own_vector)
    high = later.astype(BF16)
    low = (later - high.astype(F32)).astype(BF16)
    gain_rows = jnp.stack([high, low] + [jnp.zeros_like(high)] * 6)
    send[-1], gain_rows, cots, norms = lax.optimization_barrier((send[-1], gain_rows, cots, norms))
    got = [over_y(s, 0) for s in send]
    gain_image = jnp.dot(gain_rows, weight, preferred_element_type=F32)
    gain_image = jnp.sum(gain_image, axis=0) + image_start
    gain_image = gain_image + exchange(gain_image, "row", 1)
    left = jnp.concatenate([jnp.where(second, cots[c], norms[c]) for c in chunks])
    both = [b[2:] + g.astype(F32) for b, g in zip(both, got)]
    send = [b[:1].astype(BF16) for b in both]
    send[-1], gain_image = lax.optimization_barrier((send[-1], gain_image))
    got = [over_y(s, 1) for s in send]
    gain_image = gain_image + exchange(gain_image, "row", 2)
    mine = [b[1] + g[0].astype(F32) for b, g in zip(both, got)]

    leaving, pullbacks = [], []
    for c in chunks:
        values, pullback = jax.vjp(activation, mine[c])
        leaving.append(jnp.where(second, mine[c], values).astype(BF16))
        pullbacks.append(pullback)
    leaving[-1], gain_image, mean, inv_std = lax.optimization_barrier(
        (leaving[-1], gain_image, mean, inv_std)
    )
    arrived = [exchange(l, "section", 1) for l in leaving]
    gain_image = gain_image + exchange(gain_image, "row", 4)
    first_row = col * block_rows
    own_mean = lax.dynamic_slice_in_dim(mean, first_row, block_rows, 0)
    own_inv = lax.dynamic_slice_in_dim(inv_std, first_row, block_rows, 0)
    own_inputs = lax.dynamic_slice_in_dim(tokens, first_row, block_rows, 0).astype(F32)
    own_centered = (own_inputs - own_mean[:, None]) * own_inv[:, None]
    pieces = [
        jnp.where(second, a, pullbacks[c](a.astype(F32))[0].astype(BF16))
        for c, a in enumerate(arrived)
    ]
    held = []
    for p, m in zip(pieces, mine):
        grads = p.astype(F32)
        token_sums = [
            jnp.sum(grads * gain_image, axis=1, keepdims=True),
            jnp.sum(grads * m, axis=1, keepdims=True),
        ]
        token_sums = [t.astype(BF16) for t in token_sums]
        held.append(jnp.concatenate([p] + token_sums + [jnp.zeros((n, 126), BF16)], axis=1)[None])
    got = [over_y(h, 1) for h in held]
    held = [jnp.concatenate([g, h]) for g, h in zip(got, held)]
    held[-1], own_centered, own_inv = lax.optimization_barrier((held[-1], own_centered, own_inv))
    got = [over_y(h, 0) for h in held]
    near = [jnp.concatenate([g, h]).reshape(4 * n, -1) for g, h in zip(got, held)]
    far = [exchange(x, "row", 1) for x in near]

    rights = [jnp.concatenate([x[:, :hidden], f[:, :hidden]]) for x, f in zip(near, far)]
    extras = [jnp.concatenate([x[:, hidden:], f[:, hidden:]]) for x, f in zip(near, far)]
    products = [
        lax.dot_general(r, weight, CONTRACT_LAST, preferred_element_type=F32) for r in rights
    ]
    parts = []
    for p, e in zip(products, extras):
        split = p.reshape(8, n, features)
        beside = e.astype(F32).reshape(8, n, 128)
        blocks = []
        for r in col_order:
            place = place_of(col ^ r)
            blocks.append(
                jnp.concatenate(
                    [
                        lax.dynamic_slice_in_dim(split, place, 1, 0),
                        lax.dynamic_slice_in_dim(beside, place, 1, 0),
                    ],
                    axis=2,
                )
            )
        parts.append(jnp.concatenate(blocks))
    send = [p[:4].astype(BF16) for p in parts]
    products, left = lax.optimization_barrier((products, left))
    gain_grad = jnp.sum(jnp.concatenate(products) * left.astype(F32), axis=0) / own_vector
    bias_grad = jnp.sum(left.astype(F32), axis=0)
    right = jnp.concatenate(rights)
    send[-1], right, gain_grad = lax.optimization_barrier((send[-1], right, gain_grad))
    got = [over_z(s, 0) for s in send]
    gain_grad = gain_grad + exchange(gain_grad, "col", 1)
    right, gain_grad = lax.optimization_barrier((right, gain_grad))
    gain_grad = gain_grad + exchange(gain_grad, "col", 2)
    weight_grads = lax.dot_general(
        left, right, CONTRACT_FIRST, preferred_element_type=F32
    ).astype(BF16)
    weight_grads, got = lax.optimization_barrier((weight_grads, got))
    parts = [p[4:] + g.astype(F32) for p, g in zip(parts, got)]
    send = [p[:2].astype(BF16) for p in parts]
    send[-1], gain_grad = lax.optimization_barrier((send[-1], gain_grad))
    got = [over_z(s, 1) for s in send]
    other_gain = exchange(gain_grad, "col", 4)
    got, other_gain = lax.optimization_barrier((got, other_gain))
    gain_grad = gain_grad + other_gain
    parts = [p[2:] + g.astype(F32) for p, g in zip(parts, got)]
    summed = jnp.concatenate(
        [p[1] + exchange(p[0].astype(BF16), "col", 4).astype(F32) for p in parts]
    )

    mean_grad = summed[:, features : features + 1] / D
    slope_grad = summed[:, features + 1 : features + 2] / D
    summed = summed[:, :features]
    grad_inputs = own_inv[:, None] * (
        summed * own_vector - mean_grad - own_centered * slope_grad
    )
    output = summed + own_vector
    section_outputs = jnp.where(second, output, grad_inputs).astype(BF16)[None]
    vector_grads = jnp.where(second, bias_grad, gain_grad)[None]
    return (section_outputs, weight_grads[None], vector_grads)


def solution(mesh):
    in_specs = (P(None, "row"), P("section", "row"), P("section", "row", "col"), P("col", "row"))
    out_specs = (P("section", "col", "row"), P("section", "row", "col"), P("section", "row"))
    return jax.shard_map(local, mesh=mesh, in_specs=in_specs, out_specs=out_specs, check_vma=False)
```

time: 315 us -> 141 us (0.45)
  waiting for transfers between devices: 172 us -> 49.3 us
  blocking collectives: 55.7 us -> 0 us
  starting transfers between devices: 6.46 us -> 48.4 us
  between operations: 14.2 us -> 1.76 us
  matrix products: 29 us -> 19.3 us
  other arithmetic: 20.9 us -> 12.6 us
  local copies, waits for them, and re-layouts: 16 us -> 9.32 us
    reduce_scatter x4 -> x0, waiting for transfers between devices: 96.8 us -> none  [the longest x1 42.2 us: local(): lax.psum_scatter(partial_pre, 'row', scatter_dimension=1, tiled=True)]
    all_gather x3 -> x0, waiting for transfers between devices: 66.1 us -> none  [the longest x1 44.9 us: local(): cot_full = lax.all_gather(cotangent, 'col', axis=0, tiled=True)]
    psum x3 -> x0, blocking collectives: 44.2 us -> none  [the longest x1 19 us: local(): gain_grad = lax.psum(jnp.sum(grad_normed * centered_block, axis=0), 'col')]
    ppermute x2 -> x38, starting transfers between devices: 6.18 us -> 48.4 us  [the longest x26 32.3 us: exchange(): return lax.ppermute(block, axis, [(i, i ^ mask) for i in ranks])]
    ppermute x2 -> x38, waiting for transfers between devices: 8.14 us -> 49.3 us  [the longest x26 23.9 us: exchange(): return lax.ppermute(block, axis, [(i, i ^ mask) for i in ranks])]
    all_to_all x1 -> x0, blocking collectives: 11.4 us -> none  [local(): lax.all_to_all(hidden_share, 'row', split_axis=0, concat_axis=1, tiled=True)]
    broadcast_in_dim x2 -> x1, other arithmetic: 11.4 us -> 0.85 us  [local(): section_outputs = jnp.where(second, output, grad_inputs).astype(BF16)[None]]
    dot_general x3 -> x6, matrix products: 29 us -> 19.3 us  [the longest x1 7.55 us: local(): lax.dot_general(left, right, CONTRACT_FIRST, preferred_element_type=F32)]
  transfers between devices with their start and end apart: 9 -> 38, of which waited for: 8 -> 23; matrix products, arithmetic and copies ran while one was open for 16% -> 16% of each run, Pallas kernels for 0% -> 0%
where the time goes in v3:
time: 141 us
  waiting for transfers between devices  49.3 us (35%)
  starting transfers between devices  48.4 us (34%)
  matrix products  19.3 us (14%)
  other arithmetic  12.6 us (9%)
  local copies, waits for them, and re-layouts  9.32 us (7%)
  between operations  1.76 us (1%)
    ppermute x26, starting transfers between devices, exchange(): return lax.ppermute(block, axis, [(i, i ^ mask) for i in ranks])  32.3 us
    ppermute x26, waiting for transfers between devices, exchange(): return lax.ppermute(block, axis, [(i, i ^ mask) for i in ranks])  23.9 us
    ppermute x8, waiting for transfers between devices, over_y(): lax.ppermute(block, 'row', [(i, i ^ 2 * mask_of(i % 2, turn)) for i in ra...  22.9 us
    ppermute x8, starting transfers between devices, over_y(): lax.ppermute(block, 'row', [(i, i ^ 2 * mask_of(i % 2, turn)) for i in ra...  10.7 us
    dot_general x1, matrix products, local(): lax.dot_general(left, right, CONTRACT_FIRST, preferred_element_type=F32)  7.55 us
    ppermute x4, starting transfers between devices, over_z(): return lax.ppermute(block, ('row', 'col'), route)  5.42 us
    dot_general x2, matrix products, local(): lax.dot_general(r, weight, CONTRACT_LAST, preferred_element_type=F32)  5.26 us
    dot_general x2, matrix products, local(): partial = jnp.dot(left, weight, preferred_element_type=F32)  5.19 us
  transfers between devices with their start and end apart: 38, of which 23 were waited for; matrix products, arithmetic and copies ran while one was open for 16% of the time, Pallas kernels for 0%

profile of v3, /device:TPU:0, one launch (start us, length us, event | category | flops | bytes accessed | tf_op | source)
XLA Modules:
  0.0 140.7 jit_solution(9916928289815602492)
XLA Ops:
  0.7 1.1 slice_bitcast_fusion.2
  1.7 1.7 %collective-permute-start.2 = (bf16[1,64,512]{2,1,0:T(8,128)(2,1)S(1)}, bf16[1,64,512]{2,1,0:T(8,128)(2,1)S(1)}, u32[]{:S(2)}, u32[]{:S(2)}) collective-permute-start(bf16[1,64,512]{2,1,0:T(8,128)(2,1)S(1)} %get-tuple-element.133), channel_id=1, source_target_pairs={{0,4},{1,5},{2,6},{3,7},{4,0},{5,1},{6,2},{7,3},{8,12},{9,13},{10,... | collective-permute-start | bytes 196616 | tf_op jit(solution)/shard_map/ppermute | solution.py:17
  3.4 1.9 %collective-permute-start = (bf16[1,64,512]{2,1,0:T(8,128)(2,1)S(1)}, bf16[1,64,512]{2,1,0:T(8,128)(2,1)S(1)}, u32[]{:S(2)}, u32[]{:S(2)}) collective-permute-start(bf16[1,64,512]{2,1,0:T(8,128)(2,1)S(1)} %get-tuple-element.134), channel_id=1, source_target_pairs={{0,1},{1,0},{2,3},{3,2},{4,5},{5,4},{6,7},{7,6},{8,9},{9,8},{10,11... | collective-permute-start | bytes 196616 | tf_op jit(solution)/shard_map/ppermute | solution.py:17
  5.3 2.5 %collective-permute-start.1 = (bf16[1,64,512]{2,1,0:T(8,128)(2,1)S(1)}, bf16[1,64,512]{2,1,0:T(8,128)(2,1)S(1)}, u32[]{:S(2)}, u32[]{:S(2)}) collective-permute-start(bf16[1,64,512]{2,1,0:T(8,128)(2,1)S(1)} %get-tuple-element.135), channel_id=1, source_target_pairs={{0,3},{1,2},{2,1},{3,0},{4,7},{5,6},{6,5},{7,4},{8,11},{9,10},{10,... | collective-permute-start | bytes 196616 | tf_op jit(solution)/shard_map/ppermute | solution.py:17
  8.8 1.9 %collective-permute-done.1 = bf16[1,64,512]{2,1,0:T(8,128)(2,1)S(1)} collective-permute-done((bf16[1,64,512]{2,1,0:T(8,128)(2,1)S(1)}, bf16[1,64,512]{2,1,0:T(8,128)(2,1)S(1)}, u32[]{:S(2)}, u32[]{:S(2)}) %collective-permute-start.1) | collective-permute-done | bytes 65568 | tf_op jit(solution)/shard_map/ppermute | solution.py:17
  12.5 2.6 %collective-permute-start.3 = (bf16[2,64,512]{2,1,0:T(8,128)(2,1)S(1)}, bf16[2,64,512]{2,1,0:T(8,128)(2,1)S(1)}, u32[]{:S(2)}, u32[]{:S(2)}) collective-permute-start(bf16[2,64,512]{2,1,0:T(8,128)(2,1)S(1)} %pad_maximum_fusion.9), channel_id=1, source_target_pairs={{0,3},{1,2},{2,1},{3,0},{4,7},{5,6},{6,5},{7,4},{8,11},{9,10},{10,... | collective-permute-start | bytes 393224 | tf_op jit(solution)/shard_map/ppermute | solution.py:17
  15.6 4.0 %collective-permute-done.3 = bf16[2,64,512]{2,1,0:T(8,128)(2,1)S(1)} collective-permute-done((bf16[2,64,512]{2,1,0:T(8,128)(2,1)S(1)}, bf16[2,64,512]{2,1,0:T(8,128)(2,1)S(1)}, u32[]{:S(2)}, u32[]{:S(2)}) %collective-permute-start.3) | collective-permute-done | bytes 131104 | tf_op jit(solution)/shard_map/ppermute | solution.py:17
  19.7 1.0 collective-permute-done.4
  21.0 1.7 %collective-permute-start.10 = (f32[1024]{0:T(1024)S(1)}, f32[1024]{0:T(1024)S(1)}, u32[]{:S(2)}, u32[]{:S(2)}) collective-permute-start(f32[1024]{0:T(1024)S(1)} %fusion.78), channel_id=1, source_target_pairs={{0,16},{8,24},{16,0},{24,8},{32,48},{40,56},{48,32},{56,40},{1,17}... | collective-permute-start | bytes 12296 | tf_op jit(solution)/shard_map/ppermute | solution.py:17
  22.6 1.5 %collective-permute-start.7 = (bf16[4,64,512]{2,1,0:T(8,128)(2,1)S(1)}, bf16[4,64,512]{2,1,0:T(8,128)(2,1)S(1)}, u32[]{:S(2)}, u32[]{:S(2)}) collective-permute-start(bf16[4,64,512]{2,1,0:T(8,128)(2,1)S(1)} %pad_maximum_fusion.6), channel_id=1, source_target_pairs={{0,4},{1,5},{2,6},{3,7},{4,0},{5,1},{6,2},{7,3},{8,12},{9,13},{10,... | collective-permute-start | bytes 786440 | tf_op jit(solution)/shard_map/ppermute | solution.py:17
  25.3 3.0 %collective-permute-start.11 = (f32[1024]{0:T(1024)S(1)}, f32[1024]{0:T(1024)S(1)}, u32[]{:S(2)}, u32[]{:S(2)}) collective-permute-start(f32[1024]{0:T(1024)S(1)} %add.623), channel_id=1, source_target_pairs={{0,32},{8,40},{16,48},{24,56},{32,0},{40,8},{48,16},{56,24},{1,33}... | collective-permute-start | bytes 12296 | tf_op jit(solution)/shard_map/ppermute | solution.py:17
  28.3 2.2 %collective-permute-done.11 = f32[1024]{0:T(1024)S(1)} collective-permute-done((f32[1024]{0:T(1024)S(1)}, f32[1024]{0:T(1024)S(1)}, u32[]{:S(2)}, u32[]{:S(2)}) %collective-permute-start.11) | collective-permute-done | bytes 4128 | tf_op jit(solution)/shard_map/ppermute | solution.py:17
  32.4 1.3 broadcast_select_fusion.3
  33.8 1.4 %slice-done.2 = s8[4194304]{0:T(1024)(128)(4,1)S(1)} async-done(((s8[9437184]{0:T(1024)(128)(4,1)}), s8[4194304]{0:T(1024)(128)(4,1)S(1)}, s32[]{:S(2)}) %slice-start.2) | async-done | bytes 4194328
  35.2 2.6 %fusion.8 = f32[256,3072]{1,0:T(8,128)S(1)} fusion(bf16[256,1536]{1,0:T(8,128)(2,1)S(1)} %bitcast.118, bf16[1,1536,3072]{2,1,0:T(8,128)(2,1)S(1)} %bitcast.93), kind=kOutput, calls=%fused_computation.9 | convolution fusion | flops 2415919104 | bytes 13369344 | tf_op jit(solution)/shard_map/dot_general | solution.py:113
  38.0 2.6 %fusion.6 = f32[256,3072]{1,0:T(8,128)S(1)} fusion(bf16[256,1536]{1,0:T(8,128)(2,1)S(1)} %bitcast.117, bf16[1,1536,3072]{2,1,0:T(8,128)(2,1)S(1)} %bitcast.93), kind=kOutput, calls=%fused_computation.7 | convolution fusion | flops 2415919104 | bytes 13369344 | tf_op jit(solution)/shard_map/dot_general | solution.py:113
  41.6 1.1 collective-permute-start.13
  43.4 1.3 fusion.21
  46.4 3.3 %collective-permute-done.13 = bf16[2,32,3072]{2,1,0:T(8,128)(2,1)S(1)} collective-permute-done((bf16[2,32,3072]{2,1,0:T(8,128)(2,1)S(1)}, bf16[2,32,3072]{2,1,0:T(8,128)(2,1)S(1)}, u32[]{:S(2)}, u32[]{:S(2)}) %collective-permute-start.13) | collective-permute-done | bytes 393248 | tf_op jit(solution)/shard_map/ppermute | solution.py:26
  49.8 2.3 %collective-permute-start.14 = (bf16[1,32,3072]{2,1,0:T(8,128)(2,1)S(1)}, bf16[1,32,3072]{2,1,0:T(8,128)(2,1)S(1)}, u32[]{:S(2)}, u32[]{:S(2)}) collective-permute-start(bf16[1,32,3072]{2,1,0:T(8,128)(2,1)S(1)} %slice.440), channel_id=1, source_target_pairs={{0,48},{8,24},{16,32},{24,8},{32,16},{40,56},{48,0},{56,40},{1,49}... | collective-permute-start | bytes 589832 | tf_op jit(solution)/shard_map/ppermute | solution.py:26
  52.1 3.0 %collective-permute-done.17 = bf16[2,32,3072]{2,1,0:T(8,128)(2,1)S(1)} collective-permute-done((bf16[2,32,3072]{2,1,0:T(8,128)(2,1)S(1)}, bf16[2,32,3072]{2,1,0:T(8,128)(2,1)S(1)}, u32[]{:S(2)}, u32[]{:S(2)}) %collective-permute-start.17) | collective-permute-done | bytes 393248 | tf_op jit(solution)/shard_map/ppermute | solution.py:26
  55.3 1.5 %collective-permute-start.20 = (f32[3072]{0:T(1024)S(1)}, f32[3072]{0:T(1024)S(1)}, u32[]{:S(2)}, u32[]{:S(2)}) collective-permute-start(f32[3072]{0:T(1024)S(1)} %add.665), channel_id=1, source_target_pairs={{0,16},{8,24},{16,0},{24,8},{32,48},{40,56},{48,32},{56,40},{1,17}... | collective-permute-start | bytes 36872 | tf_op jit(solution)/shard_map/ppermute | solution.py:17
  56.7 3.0 %collective-permute-start.19 = (bf16[1,32,3072]{2,1,0:T(8,128)(2,1)S(1)}, bf16[1,32,3072]{2,1,0:T(8,128)(2,1)S(1)}, u32[]{:S(2)}, u32[]{:S(2)}) collective-permute-start(bf16[1,32,3072]{2,1,0:T(8,128)(2,1)S(1)} %slice.439), channel_id=1, source_target_pairs={{0,48},{8,24},{16,32},{24,8},{32,16},{40,56},{48,0},{56,40},{1,49}... | collective-permute-start | bytes 589832 | tf_op jit(solution)/shard_map/ppermute | solution.py:26
  60.6 2.4 %collective-permute-start.15 = (bf16[32,3072]{1,0:T(8,128)(2,1)}, bf16[32,3072]{1,0:T(8,128)(2,1)}, u32[]{:S(2)}, u32[]{:S(2)}) collective-permute-start(bf16[32,3072]{1,0:T(8,128)(2,1)} %fusion.49), channel_id=1, source_target_pairs={{0,64},{64,0},{1,65},{65,1},{2,66},{66,2},{3,67},{67,3},{4,68},{68... | collective-permute-start | bytes 589832 | tf_op jit(solution)/shard_map/ppermute | solution.py:17
  64.4 3.3 %collective-permute-start.25 = (bf16[32,3072]{1,0:T(8,128)(2,1)}, bf16[32,3072]{1,0:T(8,128)(2,1)}, u32[]{:S(2)}, u32[]{:S(2)}) collective-permute-start(bf16[32,3072]{1,0:T(8,128)(2,1)} %fusion.50), channel_id=1, source_target_pairs={{0,64},{64,0},{1,65},{65,1},{2,66},{66,2},{3,67},{67,3},{4,68},{68... | collective-permute-start | bytes 589832 | tf_op jit(solution)/shard_map/ppermute | solution.py:17
  68.8 4.2 %collective-permute-done.21 = f32[3072]{0:T(1024)S(1)} collective-permute-done((f32[3072]{0:T(1024)S(1)}, f32[3072]{0:T(1024)S(1)}, u32[]{:S(2)}, u32[]{:S(2)}) %collective-permute-start.21) | collective-permute-done | bytes 12320 | tf_op jit(solution)/shard_map/ppermute | solution.py:17
  73.0 3.1 %fusion.30 = (bf16[32]{0:T(256)(128)(2,1)S(1)}, bf16[32]{0:T(256)(128)(2,1)S(1)}, bf16[32,3072]{1,0:T(8,128)(2,1)}, bf16[32]{0:T(256)(128)(2,1)S(1)}, bf16[32]{0:T(256)(128)(2,1)S(1)}, /*index=5*/bf16[32,3072]{1,0:T(8,128)(2,1)}) fusion(bf16[1,32,3072]{2,1,0:T(8,128)(2,1)} %copy-done.10, f32[2,32,3072]{2,1,0:T(8,128)S(1)} %convert_add_fusion.1, ...), kind=kLoop, calls=%fused_computation.78 | loop fusion | flops 5701504 | bytes 1978625 | tf_op jit(solution)/shard_map/reduce_sum | solution.py:160
  76.3 1.0 concatenate.158
  77.3 2.2 %collective-permute-start.22 = (bf16[1,32,3200]{2,1,0:T(8,128)(2,1)S(1)}, bf16[1,32,3200]{2,1,0:T(8,128)(2,1)S(1)}, u32[]{:S(2)}, u32[]{:S(2)}) collective-permute-start(bf16[1,32,3200]{2,1,0:T(8,128)(2,1)S(1)} %bitcast.112), channel_id=1, source_target_pairs={{0,48},{8,24},{16,32},{24,8},{32,16},{40,56},{48,0},{56,40},{1,49}... | collective-permute-start | bytes 614408 | tf_op jit(solution)/shard_map/ppermute | solution.py:26
  79.9 1.0 concatenate.168
  80.9 1.2 collective-permute-start.26
  82.1 4.3 %collective-permute-done.22 = bf16[1,32,3200]{2,1,0:T(8,128)(2,1)S(1)} collective-permute-done((bf16[1,32,3200]{2,1,0:T(8,128)(2,1)S(1)}, bf16[1,32,3200]{2,1,0:T(8,128)(2,1)S(1)}, u32[]{:S(2)}, u32[]{:S(2)}) %collective-permute-start.22) | collective-permute-done | bytes 204832 | tf_op jit(solution)/shard_map/ppermute | solution.py:26
  86.6 4.2 %collective-permute-done.26 = bf16[1,32,3200]{2,1,0:T(8,128)(2,1)S(1)} collective-permute-done((bf16[1,32,3200]{2,1,0:T(8,128)(2,1)S(1)}, bf16[1,32,3200]{2,1,0:T(8,128)(2,1)S(1)}, u32[]{:S(2)}, u32[]{:S(2)}) %collective-permute-start.26) | collective-permute-done | bytes 204832 | tf_op jit(solution)/shard_map/ppermute | solution.py:26
  91.0 3.5 %collective-permute-done.23 = bf16[2,32,3200]{2,1,0:T(8,128)(2,1)S(1)} collective-permute-done((bf16[2,32,3200]{2,1,0:T(8,128)(2,1)S(1)}, bf16[2,32,3200]{2,1,0:T(8,128)(2,1)S(1)}, u32[]{:S(2)}, u32[]{:S(2)}) %collective-permute-start.23) | collective-permute-done | bytes 409632 | tf_op jit(solution)/shard_map/ppermute | solution.py:26
  95.0 3.9 %collective-permute-done.27 = bf16[2,32,3200]{2,1,0:T(8,128)(2,1)S(1)} collective-permute-done((bf16[2,32,3200]{2,1,0:T(8,128)(2,1)S(1)}, bf16[2,32,3200]{2,1,0:T(8,128)(2,1)S(1)}, u32[]{:S(2)}, u32[]{:S(2)}) %collective-permute-start.27) | collective-permute-done | bytes 409632 | tf_op jit(solution)/shard_map/ppermute | solution.py:26
  99.7 1.8 %slice-done.5 = s8[4194304]{0:T(1024)(128)(4,1)S(1)} async-done(((s8[9437184]{0:T(1024)(128)(4,1)}), s8[4194304]{0:T(1024)(128)(4,1)S(1)}, s32[]{:S(2)}) %slice-start.5) | async-done | bytes 4194328
  101.5 2.6 %fusion.2 = f32[256,1536]{1,0:T(8,128)S(1)} fusion(bf16[1,1536,3072]{2,1,0:T(8,128)(2,1)S(1)} %bitcast.95, bf16[128,3072]{1,0:T(8,128)(2,1)S(1)} %slice.312, bf16[128,3072]{1,0:T(8,128)(2,1)S(1)} %slice.311), kind=kOutput, calls=%fused_computation.3 | convolution fusion | flops 2419064832 | bytes 12582912 | tf_op jit(solution)/shard_map/dot_general | solution.py:174
  104.2 2.6 %fusion = f32[256,1536]{1,0:T(8,128)S(1)} fusion(bf16[1,1536,3072]{2,1,0:T(8,128)(2,1)S(1)} %bitcast.95, bf16[128,3072]{1,0:T(8,128)(2,1)S(1)} %slice.316, bf16[128,3072]{1,0:T(8,128)(2,1)S(1)} %slice.315), kind=kOutput, calls=%fused_computation.1 | convolution fusion | flops 2419064832 | bytes 12582912 | tf_op jit(solution)/shard_map/dot_general | solution.py:174
  109.1 1.2 collective-permute-start.31
  111.9 2.8 %collective-permute-start.33 = (f32[1536]{0:T(1024)S(1)}, f32[1536]{0:T(1024)S(1)}, u32[]{:S(2)}, u32[]{:S(2)}) collective-permute-start(f32[1536]{0:T(1024)S(1)} %add.693), channel_id=1, source_target_pairs={{0,2},{1,3},{2,0},{3,1},{4,6},{5,7},{6,4},{7,5},{8,10},{9,11},{10,... | collective-permute-start | bytes 18440 | tf_op jit(solution)/shard_map/ppermute | solution.py:17
  114.7 7.5 %convolution_convert_fusion = bf16[1536,3072]{1,0:T(8,128)(2,1)} fusion(bf16[512,1536]{1,0:T(8,128)(2,1)S(1)} %pad_maximum_fusion.1, bf16[512,3072]{1,0:T(8,128)(2,1)S(1)} %pad_maximum_fusion), kind=kOutput, calls=%fused_computation | convolution fusion | flops 4836556800 | bytes 14155776 | tf_op jit(solution)/shard_map/dot_general | solution.py:203
  122.2 1.7 %collective-permute-done.33 = f32[1536]{0:T(1024)S(1)} collective-permute-done((f32[1536]{0:T(1024)S(1)}, f32[1536]{0:T(1024)S(1)}, u32[]{:S(2)}, u32[]{:S(2)}) %collective-permute-start.33) | collective-permute-done | bytes 6176 | tf_op jit(solution)/shard_map/ppermute | solution.py:17
  125.1 2.4 %collective-permute-start.34 = (bf16[2,32,1664]{2,1,0:T(8,128)(2,1)S(1)}, bf16[2,32,1664]{2,1,0:T(8,128)(2,1)S(1)}, u32[]{:S(2)}, u32[]{:S(2)}) collective-permute-start(bf16[2,32,1664]{2,1,0:T(8,128)(2,1)S(1)} %slice.437), channel_id=1, source_target_pairs={{0,3},{1,2},{2,1},{3,0},{4,7},{5,6},{6,5},{7,4},{8,9},{9,8},{10,11... | collective-permute-start | bytes 638984 | tf_op jit(solution)/shard_map/ppermute | solution.py:36
  127.7 3.4 %collective-permute-done.35 = f32[1536]{0:T(1024)S(1)} collective-permute-done((f32[1536]{0:T(1024)S(1)}, f32[1536]{0:T(1024)S(1)}, u32[]{:S(2)}, u32[]{:S(2)}) %collective-permute-start.35) | collective-permute-done | bytes 6176 | tf_op jit(solution)/shard_map/ppermute | solution.py:17
  131.3 2.3 %collective-permute-done.34 = bf16[2,32,1664]{2,1,0:T(8,128)(2,1)S(1)} collective-permute-done((bf16[2,32,1664]{2,1,0:T(8,128)(2,1)S(1)}, bf16[2,32,1664]{2,1,0:T(8,128)(2,1)S(1)}, u32[]{:S(2)}, u32[]{:S(2)}) %collective-permute-start.34) | collective-permute-done | bytes 213024 | tf_op jit(solution)/shard_map/ppermute | solution.py:36
  134.6 1.8 %collective-permute-start.36 = (bf16[32,1664]{1,0:T(8,128)(2,1)S(1)}, bf16[32,1664]{1,0:T(8,128)(2,1)S(1)}, u32[]{:S(2)}, u32[]{:S(2)}) collective-permute-start(bf16[32,1664]{1,0:T(8,128)(2,1)S(1)} %fusion.58), channel_id=1, source_target_pairs={{0,4},{1,5},{2,6},{3,7},{4,0},{5,1},{6,2},{7,3},{8,12},{9,13},{10,... | collective-permute-start | bytes 319496 | tf_op jit(solution)/shard_map/ppermute | solution.py:17
  136.4 2.1 %collective-permute-done.37 = bf16[32,1664]{1,0:T(8,128)(2,1)S(1)} collective-permute-done((bf16[32,1664]{1,0:T(8,128)(2,1)S(1)}, bf16[32,1664]{1,0:T(8,128)(2,1)S(1)}, u32[]{:S(2)}, u32[]{:S(2)}) %collective-permute-start.37) | collective-permute-done | bytes 106528 | tf_op jit(solution)/shard_map/ppermute | solution.py:17
  138.5 1.1 collective-permute-done.36
  (206 shorter events, 22.5 us)
Async XLA Ops:
  0.6 10.2 %copy-start = (bf16[512,1536]{1,0:T(8,128)(2,1)S(1)}, bf16[512,1536]{1,0:T(8,128)(2,1)}, u32[]{:S(2)}) copy-start(bf16[512,1536]{1,0:T(8,128)(2,1)} %param.4) | copy-start | bytes 4718596
  0.6 33.1 %slice-start = ((s8[9437184]{0:T(1024)(128)(4,1)}), s8[1048576]{0:T(1024)(128)(4,1)S(1)}, s32[]{:S(2)}) async-start(s8[9437184]{0:T(1024)(128)(4,1)} %bitcast.92), calls=%async_computation | async-start | bytes 2097152
  1.7 7.0 %collective-permute-start.2 = (bf16[1,64,512]{2,1,0:T(8,128)(2,1)S(1)}, bf16[1,64,512]{2,1,0:T(8,128)(2,1)S(1)}, u32[]{:S(2)}, u32[]{:S(2)}) collective-permute-start(bf16[1,64,512]{2,1,0:T(8,128)(2,1)S(1)} %get-tuple-element.133), channel_id=1, source_target_pairs={{0,4},{1,5},{2,6},{3,7},{4,0},{5,1},{6,2},{7,3},{8,12},{9,13},{10,... | collective-permute-start | bytes 196616 | tf_op jit(solution)/shard_map/ppermute | solution.py:17
  3.4 5.4 %collective-permute-start = (bf16[1,64,512]{2,1,0:T(8,128)(2,1)S(1)}, bf16[1,64,512]{2,1,0:T(8,128)(2,1)S(1)}, u32[]{:S(2)}, u32[]{:S(2)}) collective-permute-start(bf16[1,64,512]{2,1,0:T(8,128)(2,1)S(1)} %get-tuple-element.134), channel_id=1, source_target_pairs={{0,1},{1,0},{2,3},{3,2},{4,5},{5,4},{6,7},{7,6},{8,9},{9,8},{10,11... | collective-permute-start | bytes 196616 | tf_op jit(solution)/shard_map/ppermute | solution.py:17
  5.3 5.5 %collective-permute-start.1 = (bf16[1,64,512]{2,1,0:T(8,128)(2,1)S(1)}, bf16[1,64,512]{2,1,0:T(8,128)(2,1)S(1)}, u32[]{:S(2)}, u32[]{:S(2)}) collective-permute-start(bf16[1,64,512]{2,1,0:T(8,128)(2,1)S(1)} %get-tuple-element.135), channel_id=1, source_target_pairs={{0,3},{1,2},{2,1},{3,0},{4,7},{5,6},{6,5},{7,4},{8,11},{9,10},{10,... | collective-permute-start | bytes 196616 | tf_op jit(solution)/shard_map/ppermute | solution.py:17
  11.4 4.2 %collective-permute-start.6 = (f32[1024]{0:T(1024)S(1)}, f32[1024]{0:T(1024)S(1)}, u32[]{:S(2)}, u32[]{:S(2)}) collective-permute-start(f32[1024]{0:T(1024)S(1)} %pad_maximum_fusion.15), channel_id=1, source_target_pairs={{0,8},{8,0},{16,24},{24,16},{32,40},{40,32},{48,56},{56,48},{1,9},... | collective-permute-start | bytes 12296 | tf_op jit(solution)/shard_map/ppermute | solution.py:17
  12.5 7.2 %collective-permute-start.3 = (bf16[2,64,512]{2,1,0:T(8,128)(2,1)S(1)}, bf16[2,64,512]{2,1,0:T(8,128)(2,1)S(1)}, u32[]{:S(2)}, u32[]{:S(2)}) collective-permute-start(bf16[2,64,512]{2,1,0:T(8,128)(2,1)S(1)} %pad_maximum_fusion.9), channel_id=1, source_target_pairs={{0,3},{1,2},{2,1},{3,0},{4,7},{5,6},{6,5},{7,4},{8,11},{9,10},{10,... | collective-permute-start | bytes 393224 | tf_op jit(solution)/shard_map/ppermute | solution.py:17
  15.1 5.6 %collective-permute-start.4 = (bf16[2,64,512]{2,1,0:T(8,128)(2,1)S(1)}, bf16[2,64,512]{2,1,0:T(8,128)(2,1)S(1)}, u32[]{:S(2)}, u32[]{:S(2)}) collective-permute-start(bf16[2,64,512]{2,1,0:T(8,128)(2,1)S(1)} %pad_maximum_fusion.10), channel_id=1, source_target_pairs={{0,4},{1,5},{2,6},{3,7},{4,0},{5,1},{6,2},{7,3},{8,12},{9,13},{10,... | collective-permute-start | bytes 393224 | tf_op jit(solution)/shard_map/ppermute | solution.py:17
  15.6 5.3 %collective-permute-start.5 = (bf16[2,64,512]{2,1,0:T(8,128)(2,1)S(1)}, bf16[2,64,512]{2,1,0:T(8,128)(2,1)S(1)}, u32[]{:S(2)}, u32[]{:S(2)}) collective-permute-start(bf16[2,64,512]{2,1,0:T(8,128)(2,1)S(1)} %pad_maximum_fusion.11), channel_id=1, source_target_pairs={{0,1},{1,0},{2,3},{3,2},{4,5},{5,4},{6,7},{7,6},{8,9},{9,8},{10,11... | collective-permute-start | bytes 393224 | tf_op jit(solution)/shard_map/ppermute | solution.py:17
  21.0 4.3 %collective-permute-start.10 = (f32[1024]{0:T(1024)S(1)}, f32[1024]{0:T(1024)S(1)}, u32[]{:S(2)}, u32[]{:S(2)}) collective-permute-start(f32[1024]{0:T(1024)S(1)} %fusion.78), channel_id=1, source_target_pairs={{0,16},{8,24},{16,0},{24,8},{32,48},{40,56},{48,32},{56,40},{1,17}... | collective-permute-start | bytes 12296 | tf_op jit(solution)/shard_map/ppermute | solution.py:17
  22.6 8.7 %collective-permute-start.7 = (bf16[4,64,512]{2,1,0:T(8,128)(2,1)S(1)}, bf16[4,64,512]{2,1,0:T(8,128)(2,1)S(1)}, u32[]{:S(2)}, u32[]{:S(2)}) collective-permute-start(bf16[4,64,512]{2,1,0:T(8,128)(2,1)S(1)} %pad_maximum_fusion.6), channel_id=1, source_target_pairs={{0,4},{1,5},{2,6},{3,7},{4,0},{5,1},{6,2},{7,3},{8,12},{9,13},{10,... | collective-permute-start | bytes 786440 | tf_op jit(solution)/shard_map/ppermute | solution.py:17
  24.1 7.4 %collective-permute-start.8 = (bf16[4,64,512]{2,1,0:T(8,128)(2,1)S(1)}, bf16[4,64,512]{2,1,0:T(8,128)(2,1)S(1)}, u32[]{:S(2)}, u32[]{:S(2)}) collective-permute-start(bf16[4,64,512]{2,1,0:T(8,128)(2,1)S(1)} %pad_maximum_fusion.7), channel_id=1, source_target_pairs={{0,1},{1,0},{2,3},{3,2},{4,5},{5,4},{6,7},{7,6},{8,9},{9,8},{10,11... | collective-permute-start | bytes 786440 | tf_op jit(solution)/shard_map/ppermute | solution.py:17
  24.4 8.0 %collective-permute-start.9 = (bf16[4,64,512]{2,1,0:T(8,128)(2,1)S(1)}, bf16[4,64,512]{2,1,0:T(8,128)(2,1)S(1)}, u32[]{:S(2)}, u32[]{:S(2)}) collective-permute-start(bf16[4,64,512]{2,1,0:T(8,128)(2,1)S(1)} %pad_maximum_fusion.8), channel_id=1, source_target_pairs={{0,3},{1,2},{2,1},{3,0},{4,7},{5,6},{6,5},{7,4},{8,11},{9,10},{10,... | collective-permute-start | bytes 786440 | tf_op jit(solution)/shard_map/ppermute | solution.py:17
  25.3 5.2 %collective-permute-start.11 = (f32[1024]{0:T(1024)S(1)}, f32[1024]{0:T(1024)S(1)}, u32[]{:S(2)}, u32[]{:S(2)}) collective-permute-start(f32[1024]{0:T(1024)S(1)} %add.623), channel_id=1, source_target_pairs={{0,32},{8,40},{16,48},{24,56},{32,0},{40,8},{48,16},{56,24},{1,33}... | collective-permute-start | bytes 12296 | tf_op jit(solution)/shard_map/ppermute | solution.py:17
  37.9 3.5 %collective-permute-start.12 = (bf16[128,3072]{1,0:T(8,128)(2,1)S(1)}, bf16[128,3072]{1,0:T(8,128)(2,1)S(1)}, u32[]{:S(2)}, u32[]{:S(2)}) collective-permute-start(bf16[128,3072]{1,0:T(8,128)(2,1)S(1)} %slice.434), channel_id=1, source_target_pairs={{0,8},{8,0},{16,24},{24,16},{32,40},{40,32},{48,56},{56,48},{1,9},... | collective-permute-start | bytes 2359304 | tf_op jit(solution)/shard_map/ppermute | solution.py:17
  40.7 2.5 %collective-permute-start.16 = (bf16[128,3072]{1,0:T(8,128)(2,1)S(1)}, bf16[128,3072]{1,0:T(8,128)(2,1)S(1)}, u32[]{:S(2)}, u32[]{:S(2)}) collective-permute-start(bf16[128,3072]{1,0:T(8,128)(2,1)S(1)} %slice.433), channel_id=1, source_target_pairs={{0,8},{8,0},{16,24},{24,16},{32,40},{40,32},{48,56},{56,48},{1,9},... | collective-permute-start | bytes 2359304 | tf_op jit(solution)/shard_map/ppermute | solution.py:17
  41.6 8.0 %collective-permute-start.13 = (bf16[2,32,3072]{2,1,0:T(8,128)(2,1)S(1)}, bf16[2,32,3072]{2,1,0:T(8,128)(2,1)S(1)}, u32[]{:S(2)}, u32[]{:S(2)}) collective-permute-start(bf16[2,32,3072]{2,1,0:T(8,128)(2,1)S(1)} %bitcast.119), channel_id=1, source_target_pairs={{0,16},{8,56},{16,0},{24,40},{32,48},{40,24},{48,32},{56,8},{1,17}... | collective-permute-start | bytes 1179656 | tf_op jit(solution)/shard_map/ppermute | solution.py:26
  44.8 1.6 %collective-permute-start.18 = (f32[3072]{0:T(1024)S(1)}, f32[3072]{0:T(1024)S(1)}, u32[]{:S(2)}, u32[]{:S(2)}) collective-permute-start(f32[3072]{0:T(1024)S(1)} %add.664), channel_id=1, source_target_pairs={{0,8},{8,0},{16,24},{24,16},{32,40},{40,32},{48,56},{56,48},{1,9},... | collective-permute-start | bytes 36872 | tf_op jit(solution)/shard_map/ppermute | solution.py:17
  45.5 9.6 %slice-start.7 = ((f32[128,3072]{1,0:T(8,128)}), f32[64,3072]{1,0:T(8,128)S(1)}, s32[]{:S(2)}) async-start(f32[128,3072]{1,0:T(8,128)} %copy-done.2), calls=%async_computation.7 | async-start | bytes 1572864 | tf_op jit(solution)/shard_map/slice | solution.py:129
  45.5 9.6 %collective-permute-start.17 = (bf16[2,32,3072]{2,1,0:T(8,128)(2,1)S(1)}, bf16[2,32,3072]{2,1,0:T(8,128)(2,1)S(1)}, u32[]{:S(2)}, u32[]{:S(2)}) collective-permute-start(bf16[2,32,3072]{2,1,0:T(8,128)(2,1)S(1)} %bitcast.120), channel_id=1, source_target_pairs={{0,16},{8,56},{16,0},{24,40},{32,48},{40,24},{48,32},{56,8},{1,17}... | collective-permute-start | bytes 1179656 | tf_op jit(solution)/shard_map/ppermute | solution.py:26
  49.8 9.9 %collective-permute-start.14 = (bf16[1,32,3072]{2,1,0:T(8,128)(2,1)S(1)}, bf16[1,32,3072]{2,1,0:T(8,128)(2,1)S(1)}, u32[]{:S(2)}, u32[]{:S(2)}) collective-permute-start(bf16[1,32,3072]{2,1,0:T(8,128)(2,1)S(1)} %slice.440), channel_id=1, source_target_pairs={{0,48},{8,24},{16,32},{24,8},{32,16},{40,56},{48,0},{56,40},{1,49}... | collective-permute-start | bytes 589832 | tf_op jit(solution)/shard_map/ppermute | solution.py:26
  55.2 8.4 %copy-start.3 = (f32[2,32,3072]{2,1,0:T(8,128)}, f32[2,32,3072]{2,1,0:T(8,128)S(1)}, u32[]{:S(2)}) copy-start(f32[2,32,3072]{2,1,0:T(8,128)S(1)} %convert_add_fusion) | copy-start | bytes 2359300
  55.3 4.5 %collective-permute-start.20 = (f32[3072]{0:T(1024)S(1)}, f32[3072]{0:T(1024)S(1)}, u32[]{:S(2)}, u32[]{:S(2)}) collective-permute-start(f32[3072]{0:T(1024)S(1)} %add.665), channel_id=1, source_target_pairs={{0,16},{8,24},{16,0},{24,8},{32,48},{40,56},{48,32},{56,40},{1,17}... | collective-permute-start | bytes 36872 | tf_op jit(solution)/shard_map/ppermute | solution.py:17
  56.7 6.9 %collective-permute-start.19 = (bf16[1,32,3072]{2,1,0:T(8,128)(2,1)S(1)}, bf16[1,32,3072]{2,1,0:T(8,128)(2,1)S(1)}, u32[]{:S(2)}, u32[]{:S(2)}) collective-permute-start(bf16[1,32,3072]{2,1,0:T(8,128)(2,1)S(1)} %slice.439), channel_id=1, source_target_pairs={{0,48},{8,24},{16,32},{24,8},{32,16},{40,56},{48,0},{56,40},{1,49}... | collective-permute-start | bytes 589832 | tf_op jit(solution)/shard_map/ppermute | solution.py:26
  60.6 12.4 %collective-permute-start.15 = (bf16[32,3072]{1,0:T(8,128)(2,1)}, bf16[32,3072]{1,0:T(8,128)(2,1)}, u32[]{:S(2)}, u32[]{:S(2)}) collective-permute-start(bf16[32,3072]{1,0:T(8,128)(2,1)} %fusion.49), channel_id=1, source_target_pairs={{0,64},{64,0},{1,65},{65,1},{2,66},{66,2},{3,67},{67,3},{4,68},{68... | collective-permute-start | bytes 589832 | tf_op jit(solution)/shard_map/ppermute | solution.py:17
  63.6 36.1 %slice-start.3 = ((s8[9437184]{0:T(1024)(128)(4,1)}), s8[1048576]{0:T(1024)(128)(4,1)S(1)}, s32[]{:S(2)}) async-start(s8[9437184]{0:T(1024)(128)(4,1)} %bitcast.94), calls=%async_computation.3 | async-start | bytes 2097152
  64.4 8.5 %collective-permute-start.25 = (bf16[32,3072]{1,0:T(8,128)(2,1)}, bf16[32,3072]{1,0:T(8,128)(2,1)}, u32[]{:S(2)}, u32[]{:S(2)}) collective-permute-start(bf16[32,3072]{1,0:T(8,128)(2,1)} %fusion.50), channel_id=1, source_target_pairs={{0,64},{64,0},{1,65},{65,1},{2,66},{66,2},{3,67},{67,3},{4,68},{68... | collective-permute-start | bytes 589832 | tf_op jit(solution)/shard_map/ppermute | solution.py:17
  67.8 5.2 %collective-permute-start.21 = (f32[3072]{0:T(1024)S(1)}, f32[3072]{0:T(1024)S(1)}, u32[]{:S(2)}, u32[]{:S(2)}) collective-permute-start(f32[3072]{0:T(1024)S(1)} %add.670), channel_id=1, source_target_pairs={{0,32},{8,40},{16,48},{24,56},{32,0},{40,8},{48,16},{56,24},{1,33}... | collective-permute-start | bytes 36872 | tf_op jit(solution)/shard_map/ppermute | solution.py:17
  77.3 9.1 %collective-permute-start.22 = (bf16[1,32,3200]{2,1,0:T(8,128)(2,1)S(1)}, bf16[1,32,3200]{2,1,0:T(8,128)(2,1)S(1)}, u32[]{:S(2)}, u32[]{:S(2)}) collective-permute-start(bf16[1,32,3200]{2,1,0:T(8,128)(2,1)S(1)} %bitcast.112), channel_id=1, source_target_pairs={{0,48},{8,24},{16,32},{24,8},{32,16},{40,56},{48,0},{56,40},{1,49}... | collective-permute-start | bytes 614408 | tf_op jit(solution)/shard_map/ppermute | solution.py:26
  80.9 13.9 %copy-start.5 = (bf16[256,1536]{1,0:T(8,128)(2,1)S(1)}, bf16[256,1536]{1,0:T(8,128)(2,1)}, u32[]{:S(2)}) copy-start(bf16[256,1536]{1,0:T(8,128)(2,1)} %copy-done.4) | copy-start | bytes 2359300
  80.9 13.9 %copy-start.7 = (bf16[256,1536]{1,0:T(8,128)(2,1)S(1)}, bf16[256,1536]{1,0:T(8,128)(2,1)}, u32[]{:S(2)}) copy-start(bf16[256,1536]{1,0:T(8,128)(2,1)} %copy-done.6) | copy-start | bytes 2359300
  80.9 13.9 %copy-start.8 = (bf16[8,32,1536]{2,1,0:T(8,128)(2,1)S(1)}, bf16[8,32,1536]{2,1,0:T(8,128)(2,1)}, u32[]{:S(2)}) copy-start(bf16[8,32,1536]{2,1,0:T(8,128)(2,1)} %get-tuple-element.110) | copy-start | bytes 2359300
  80.9 13.9 %copy-start.9 = (bf16[8,32,1536]{2,1,0:T(8,128)(2,1)S(1)}, bf16[8,32,1536]{2,1,0:T(8,128)(2,1)}, u32[]{:S(2)}) copy-start(bf16[8,32,1536]{2,1,0:T(8,128)(2,1)} %get-tuple-element.111) | copy-start | bytes 2359300
  80.9 9.9 %collective-permute-start.26 = (bf16[1,32,3200]{2,1,0:T(8,128)(2,1)S(1)}, bf16[1,32,3200]{2,1,0:T(8,128)(2,1)S(1)}, u32[]{:S(2)}, u32[]{:S(2)}) collective-permute-start(bf16[1,32,3200]{2,1,0:T(8,128)(2,1)S(1)} %bitcast.115), channel_id=1, source_target_pairs={{0,48},{8,24},{16,32},{24,8},{32,16},{40,56},{48,0},{56,40},{1,49}... | collective-permute-start | bytes 614408 | tf_op jit(solution)/shard_map/ppermute | solution.py:26
  86.5 8.0 %collective-permute-start.23 = (bf16[2,32,3200]{2,1,0:T(8,128)(2,1)S(1)}, bf16[2,32,3200]{2,1,0:T(8,128)(2,1)S(1)}, u32[]{:S(2)}, u32[]{:S(2)}) collective-permute-start(bf16[2,32,3200]{2,1,0:T(8,128)(2,1)S(1)} %pad_maximum_fusion.4), channel_id=1, source_target_pairs={{0,16},{8,56},{16,0},{24,40},{32,48},{40,24},{48,32},{56,8},{1,17}... | collective-permute-start | bytes 1228808 | tf_op jit(solution)/shard_map/ppermute | solution.py:26
  90.9 8.9 %slice-start.4 = ((s8[9437184]{0:T(1024)(128)(4,1)}), s8[4194304]{0:T(1024)(128)(4,1)S(1)}, s32[]{:S(2)}) async-start(s8[9437184]{0:T(1024)(128)(4,1)} %bitcast.94), calls=%async_computation.4 | async-start | bytes 8388608
  90.9 8.0 %collective-permute-start.27 = (bf16[2,32,3200]{2,1,0:T(8,128)(2,1)S(1)}, bf16[2,32,3200]{2,1,0:T(8,128)(2,1)S(1)}, u32[]{:S(2)}, u32[]{:S(2)}) collective-permute-start(bf16[2,32,3200]{2,1,0:T(8,128)(2,1)S(1)} %pad_maximum_fusion.5), channel_id=1, source_target_pairs={{0,16},{8,56},{16,0},{24,40},{32,48},{40,24},{48,32},{56,8},{1,17}... | collective-permute-start | bytes 1228808 | tf_op jit(solution)/shard_map/ppermute | solution.py:26
  94.6 5.0 %collective-permute-start.24 = (bf16[128,3200]{1,0:T(8,128)(2,1)S(1)}, bf16[128,3200]{1,0:T(8,128)(2,1)S(1)}, u32[]{:S(2)}, u32[]{:S(2)}) collective-permute-start(bf16[128,3200]{1,0:T(8,128)(2,1)S(1)} %bitcast.104), channel_id=1, source_target_pairs={{0,8},{8,0},{16,24},{24,16},{32,40},{40,32},{48,56},{56,48},{1,9},... | collective-permute-start | bytes 2457608 | tf_op jit(solution)/shard_map/ppermute | solution.py:17
  99.0 5.1 %collective-permute-start.28 = (bf16[128,3200]{1,0:T(8,128)(2,1)S(1)}, bf16[128,3200]{1,0:T(8,128)(2,1)S(1)}, u32[]{:S(2)}, u32[]{:S(2)}) collective-permute-start(bf16[128,3200]{1,0:T(8,128)(2,1)S(1)} %bitcast.107), channel_id=1, source_target_pairs={{0,8},{8,0},{16,24},{24,16},{32,40},{40,32},{48,56},{56,48},{1,9},... | collective-permute-start | bytes 2457608 | tf_op jit(solution)/shard_map/ppermute | solution.py:17
  108.2 3.7 %collective-permute-start.29 = (f32[1536]{0:T(1024)S(1)}, f32[1536]{0:T(1024)S(1)}, u32[]{:S(2)}, u32[]{:S(2)}) collective-permute-start(f32[1536]{0:T(1024)S(1)} %div.314), channel_id=1, source_target_pairs={{0,1},{1,0},{2,3},{3,2},{4,5},{5,4},{6,7},{7,6},{8,9},{9,8},{10,11... | collective-permute-start | bytes 18440 | tf_op jit(solution)/shard_map/ppermute | solution.py:17
  109.1 14.8 %collective-permute-start.31 = (bf16[4,32,1664]{2,1,0:T(8,128)(2,1)S(1)}, bf16[4,32,1664]{2,1,0:T(8,128)(2,1)S(1)}, u32[]{:S(2)}, u32[]{:S(2)}) collective-permute-start(bf16[4,32,1664]{2,1,0:T(8,128)(2,1)S(1)} %maximum_maximum_fusion), channel_id=1, source_target_pairs={{0,1},{1,0},{2,3},{3,2},{4,5},{5,4},{6,7},{7,6},{8,11},{9,10},{10,... | collective-permute-start | bytes 1277960 | tf_op jit(solution)/shard_map/ppermute | solution.py:36
  110.3 13.6 %collective-permute-start.30 = (bf16[4,32,1664]{2,1,0:T(8,128)(2,1)S(1)}, bf16[4,32,1664]{2,1,0:T(8,128)(2,1)S(1)}, u32[]{:S(2)}, u32[]{:S(2)}) collective-permute-start(bf16[4,32,1664]{2,1,0:T(8,128)(2,1)S(1)} %maximum_maximum_fusion.1), channel_id=1, source_target_pairs={{0,1},{1,0},{2,3},{3,2},{4,5},{5,4},{6,7},{7,6},{8,11},{9,10},{10,... | collective-permute-start | bytes 1277960 | tf_op jit(solution)/shard_map/ppermute | solution.py:36
  111.9 12.0 %collective-permute-start.33 = (f32[1536]{0:T(1024)S(1)}, f32[1536]{0:T(1024)S(1)}, u32[]{:S(2)}, u32[]{:S(2)}) collective-permute-start(f32[1536]{0:T(1024)S(1)} %add.693), channel_id=1, source_target_pairs={{0,2},{1,3},{2,0},{3,1},{4,6},{5,7},{6,4},{7,5},{8,10},{9,11},{10,... | collective-permute-start | bytes 18440 | tf_op jit(solution)/shard_map/ppermute | solution.py:17
  124.2 7.1 %collective-permute-start.32 = (bf16[2,32,1664]{2,1,0:T(8,128)(2,1)S(1)}, bf16[2,32,1664]{2,1,0:T(8,128)(2,1)S(1)}, u32[]{:S(2)}, u32[]{:S(2)}) collective-permute-start(bf16[2,32,1664]{2,1,0:T(8,128)(2,1)S(1)} %slice.438), channel_id=1, source_target_pairs={{0,3},{1,2},{2,1},{3,0},{4,7},{5,6},{6,5},{7,4},{8,9},{9,8},{10,11... | collective-permute-start | bytes 638984 | tf_op jit(solution)/shard_map/ppermute | solution.py:36
  125.1 8.5 %collective-permute-start.34 = (bf16[2,32,1664]{2,1,0:T(8,128)(2,1)S(1)}, bf16[2,32,1664]{2,1,0:T(8,128)(2,1)S(1)}, u32[]{:S(2)}, u32[]{:S(2)}) collective-permute-start(bf16[2,32,1664]{2,1,0:T(8,128)(2,1)S(1)} %slice.437), channel_id=1, source_target_pairs={{0,3},{1,2},{2,1},{3,0},{4,7},{5,6},{6,5},{7,4},{8,9},{9,8},{10,11... | collective-permute-start | bytes 638984 | tf_op jit(solution)/shard_map/ppermute | solution.py:36
  127.5 3.7 %collective-permute-start.35 = (f32[1536]{0:T(1024)S(1)}, f32[1536]{0:T(1024)S(1)}, u32[]{:S(2)}, u32[]{:S(2)}) collective-permute-start(f32[1536]{0:T(1024)S(1)} %add.696), channel_id=1, source_target_pairs={{0,4},{1,5},{2,6},{3,7},{4,0},{5,1},{6,2},{7,3},{8,12},{9,13},{10,... | collective-permute-start | bytes 18440 | tf_op jit(solution)/shard_map/ppermute | solution.py:17
  133.7 4.8 %collective-permute-start.37 = (bf16[32,1664]{1,0:T(8,128)(2,1)S(1)}, bf16[32,1664]{1,0:T(8,128)(2,1)S(1)}, u32[]{:S(2)}, u32[]{:S(2)}) collective-permute-start(bf16[32,1664]{1,0:T(8,128)(2,1)S(1)} %fusion.59), channel_id=1, source_target_pairs={{0,4},{1,5},{2,6},{3,7},{4,0},{5,1},{6,2},{7,3},{8,12},{9,13},{10,... | collective-permute-start | bytes 319496 | tf_op jit(solution)/shard_map/ppermute | solution.py:17
  134.6 5.0 %collective-permute-start.36 = (bf16[32,1664]{1,0:T(8,128)(2,1)S(1)}, bf16[32,1664]{1,0:T(8,128)(2,1)S(1)}, u32[]{:S(2)}, u32[]{:S(2)}) collective-permute-start(bf16[32,1664]{1,0:T(8,128)(2,1)S(1)} %fusion.58), channel_id=1, source_target_pairs={{0,4},{1,5},{2,6},{3,7},{4,0},{5,1},{6,2},{7,3},{8,12},{9,13},{10,... | collective-permute-start | bytes 319496 | tf_op jit(solution)/shard_map/ppermute | solution.py:17
  (10 other events, 33.2 us)

commit v4 on v3

--- a/solution.py
+++ b/solution.py
@@ -75,7 +75,9 @@
             inputs = tokens.astype(F32)
             sums = jnp.concatenate([jnp.sum(inputs, axis=1), jnp.sum(inputs * inputs, axis=1)])
             sums = sums + exchange(sums, "row", 1)
-            image_start = jnp.sum(weight[:8].astype(F32) * own_vector[:8, None], axis=0)
+            image_start = jnp.sum(
+                weight[:8].astype(F32) * own_vector[:8, None], axis=0, keepdims=True
+            )
         held = [jnp.concatenate([h, g]) for h, g in zip(held, got)]
         relative = [
             rel + [order[step] ^ r for r in rel] for rel, order in zip(relative, COL_ORDERS)
@@ -123,7 +125,7 @@
     send[-1], gain_rows, cots, norms = lax.optimization_barrier((send[-1], gain_rows, cots, norms))
     got = [over_y(s, 0) for s in send]
     gain_image = jnp.dot(gain_rows, weight, preferred_element_type=F32)
-    gain_image = jnp.sum(gain_image, axis=0) + image_start
+    gain_image = jnp.sum(gain_image, axis=0, keepdims=True) + image_start
     gain_image = gain_image + exchange(gain_image, "row", 1)
     left = jnp.concatenate([jnp.where(second, cots[c], norms[c]) for c in chunks])
     both = [b[2:] + g.astype(F32) for b, g in zip(both, got)]
@@ -148,19 +150,21 @@
     own_inv = lax.dynamic_slice_in_dim(inv_std, first_row, block_rows, 0)
     own_inputs = lax.dynamic_slice_in_dim(tokens, first_row, block_rows, 0).astype(F32)
     own_centered = (own_inputs - own_mean[:, None]) * own_inv[:, None]
-    pieces = [
-        jnp.where(second, a, pullbacks[c](a.astype(F32))[0].astype(BF16))
-        for c, a in enumerate(arrived)
-    ]
     held = []
-    for p, m in zip(pieces, mine):
+    columns = lax.broadcasted_iota(jnp.int32, (n, hidden + 128), 1)
+    for c in chunks:
+        a, m = arrived[c], mine[c]
+        p = jnp.where(second, a, pullbacks[c](a.astype(F32))[0].astype(BF16))
+        p, m = lax.optimization_barrier((p, m))
         grads = p.astype(F32)
-        token_sums = [
-            jnp.sum(grads * gain_image, axis=1, keepdims=True),
-            jnp.sum(grads * m, axis=1, keepdims=True),
-        ]
-        token_sums = [t.astype(BF16) for t in token_sums]
-        held.append(jnp.concatenate([p] + token_sums + [jnp.zeros((n, 126), BF16)], axis=1)[None])
+        a_sum = jnp.sum(grads * gain_image, axis=1, keepdims=True)
+        b_sum = jnp.sum(grads * m, axis=1, keepdims=True)
+        wide = jnp.pad(p, ((0, 0), (0, 128))).astype(F32)
+        wide = jnp.where(columns == hidden, a_sum, wide)
+        wide = jnp.where(columns == hidden + 1, b_sum, wide)
+        held.append(wide.astype(BF16)[None])
+        if c + 1 < CHUNKS:
+            arrived[c + 1], _ = lax.optimization_barrier((arrived[c + 1], held[c]))
     got = [over_y(h, 1) for h in held]
     held = [jnp.concatenate([g, h]) for g, h in zip(got, held)]
     held[-1], own_centered, own_inv = lax.optimization_barrier((held[-1], own_centered, own_inv))
@@ -207,15 +211,13 @@
     parts = [p[4:] + g.astype(F32) for p, g in zip(parts, got)]
     send = [p[:2].astype(BF16) for p in parts]
     send[-1], gain_grad = lax.optimization_barrier((send[-1], gain_grad))
-    got = [over_z(s, 1) for s in send]
+    got = [over_z(x, 1) for x in send]
     other_gain = exchange(gain_grad, "col", 4)
-    got, other_gain = lax.optimization_barrier((got, other_gain))
+    parts = [p[2:] + g.astype(F32) for p, g in zip(parts, got)]
+    got = [exchange(p[0].astype(BF16), "col", 4) for p in parts]
+    got[-1], other_gain = lax.optimization_barrier((got[-1], other_gain))
     gain_grad = gain_grad + other_gain
-    parts = [p[2:] + g.astype(F32) for p, g in zip(parts, got)]
-    summed = jnp.concatenate(
-        [p[1] + exchange(p[0].astype(BF16), "col", 4).astype(F32) for p in parts]
-    )
-
+    summed = jnp.concatenate([p[1] + g.astype(F32) for p, g in zip(parts, got)])
     mean_grad = summed[:, features : features + 1] / D
     slope_grad = summed[:, features + 1 : features + 2] / D
     summed = summed[:, :features]

time: 141 us -> 131 us (0.929)
  waiting for transfers between devices: 49.3 us -> 37.4 us
  starting transfers between devices: 48.4 us -> 55.2 us
  local copies, waits for them, and re-layouts: 9.32 us -> 6.44 us
  other arithmetic: 12.6 us -> 10.6 us
    ppermute x26, waiting for transfers between devices: 23.9 us -> 16 us  [exchange(): return lax.ppermute(block, axis, [(i, i ^ mask) for i in ranks])]
    ppermute x8, waiting for transfers between devices: 22.9 us -> 17.4 us  [over_y(): lax.ppermute(block, 'row', [(i, i ^ 2 * mask_of(i % 2, turn)) for i in ra...]
    ppermute x8, starting transfers between devices: 10.7 us -> 14.2 us  [over_y(): lax.ppermute(block, 'row', [(i, i ^ 2 * mask_of(i % 2, turn)) for i in ra...]
    ppermute x26, starting transfers between devices: 32.3 us -> 35.5 us  [exchange(): return lax.ppermute(block, axis, [(i, i ^ mask) for i in ranks])]
    reduce_sum x2 -> x3, other arithmetic: 4.03 us -> 1.29 us  [the longest x1 0.9 us: local(): jnp.sum(weight[:8].astype(F32) * own_vector[:8, None], axis=0, keepdims=T...]
    concatenate x2 -> x0, local copies, waits for them, and re-layouts: 2.06 us -> none  [local(): jnp.concatenate([p] + token_sums + [jnp.zeros((n, 126), BF16)], axis=1)]
    ppermute x4, waiting for transfers between devices: 2.45 us -> 3.96 us  [over_z(): return lax.ppermute(block, ('row', 'col'), route)]
    unnamed x43 -> x35, local copies, waits for them, and re-layouts: 3.46 us -> 2.3 us
  transfers between devices with their start and end apart: 38 -> 38, of which waited for: 23 -> 22; matrix products, arithmetic and copies ran while one was open for 16% -> 18% of each run, Pallas kernels for 0% -> 0%
where the time goes in v4:
time: 131 us
  starting transfers between devices  55.2 us (42%)
  waiting for transfers between devices  37.4 us (29%)
  matrix products  19.4 us (15%)
  other arithmetic  10.6 us (8%)
  local copies, waits for them, and re-layouts  6.44 us (5%)
  between operations  1.79 us (1%)
    ppermute x26, starting transfers between devices, exchange(): return lax.ppermute(block, axis, [(i, i ^ mask) for i in ranks])  35.5 us
    ppermute x8, waiting for transfers between devices, over_y(): lax.ppermute(block, 'row', [(i, i ^ 2 * mask_of(i % 2, turn)) for i in ra...  17.4 us
    ppermute x26, waiting for transfers between devices, exchange(): return lax.ppermute(block, axis, [(i, i ^ mask) for i in ranks])  16 us
    ppermute x8, starting transfers between devices, over_y(): lax.ppermute(block, 'row', [(i, i ^ 2 * mask_of(i % 2, turn)) for i in ra...  14.2 us
    dot_general x1, matrix products, local(): lax.dot_general(left, right, CONTRACT_FIRST, preferred_element_type=F32)  7.55 us
    ppermute x4, starting transfers between devices, over_z(): return lax.ppermute(block, ('row', 'col'), route)  5.42 us
    dot_general x2, matrix products, local(): lax.dot_general(r, weight, CONTRACT_LAST, preferred_element_type=F32)  5.29 us
    dot_general x2, matrix products, local(): partial = jnp.dot(left, weight, preferred_element_type=F32)  5.19 us
  transfers between devices with their start and end apart: 38, of which 22 were waited for; matrix products, arithmetic and copies ran while one was open for 18% of the time, Pallas kernels for 0%

profile of v4, /device:TPU:0, one launch (start us, length us, event | category | flops | bytes accessed | tf_op | source)
XLA Modules:
  0.0 130.8 jit_solution(9261831076408244898)
XLA Ops:
  0.7 1.1 slice_bitcast_fusion.2
  1.7 1.7 %collective-permute-start.2 = (bf16[1,64,512]{2,1,0:T(8,128)(2,1)S(1)}, bf16[1,64,512]{2,1,0:T(8,128)(2,1)S(1)}, u32[]{:S(2)}, u32[]{:S(2)}) collective-permute-start(bf16[1,64,512]{2,1,0:T(8,128)(2,1)S(1)} %get-tuple-element.143), channel_id=1, source_target_pairs={{0,4},{1,5},{2,6},{3,7},{4,0},{5,1},{6,2},{7,3},{8,12},{9,13},{10,... | collective-permute-start | bytes 196616 | tf_op jit(solution)/shard_map/ppermute | solution.py:17
  3.4 1.9 %collective-permute-start = (bf16[1,64,512]{2,1,0:T(8,128)(2,1)S(1)}, bf16[1,64,512]{2,1,0:T(8,128)(2,1)S(1)}, u32[]{:S(2)}, u32[]{:S(2)}) collective-permute-start(bf16[1,64,512]{2,1,0:T(8,128)(2,1)S(1)} %get-tuple-element.144), channel_id=1, source_target_pairs={{0,1},{1,0},{2,3},{3,2},{4,5},{5,4},{6,7},{7,6},{8,9},{9,8},{10,11... | collective-permute-start | bytes 196616 | tf_op jit(solution)/shard_map/ppermute | solution.py:17
  5.3 2.5 %collective-permute-start.1 = (bf16[1,64,512]{2,1,0:T(8,128)(2,1)S(1)}, bf16[1,64,512]{2,1,0:T(8,128)(2,1)S(1)}, u32[]{:S(2)}, u32[]{:S(2)}) collective-permute-start(bf16[1,64,512]{2,1,0:T(8,128)(2,1)S(1)} %get-tuple-element.145), channel_id=1, source_target_pairs={{0,3},{1,2},{2,1},{3,0},{4,7},{5,6},{6,5},{7,4},{8,11},{9,10},{10,... | collective-permute-start | bytes 196616 | tf_op jit(solution)/shard_map/ppermute | solution.py:17
  8.8 1.9 %collective-permute-done.1 = bf16[1,64,512]{2,1,0:T(8,128)(2,1)S(1)} collective-permute-done((bf16[1,64,512]{2,1,0:T(8,128)(2,1)S(1)}, bf16[1,64,512]{2,1,0:T(8,128)(2,1)S(1)}, u32[]{:S(2)}, u32[]{:S(2)}) %collective-permute-start.1) | collective-permute-done | bytes 65568 | tf_op jit(solution)/shard_map/ppermute | solution.py:17
  11.6 2.6 %collective-permute-start.3 = (bf16[2,64,512]{2,1,0:T(8,128)(2,1)S(1)}, bf16[2,64,512]{2,1,0:T(8,128)(2,1)S(1)}, u32[]{:S(2)}, u32[]{:S(2)}) collective-permute-start(bf16[2,64,512]{2,1,0:T(8,128)(2,1)S(1)} %pad_maximum_fusion.9), channel_id=1, source_target_pairs={{0,3},{1,2},{2,1},{3,0},{4,7},{5,6},{6,5},{7,4},{8,11},{9,10},{10,... | collective-permute-start | bytes 393224 | tf_op jit(solution)/shard_map/ppermute | solution.py:17
  15.6 3.1 %collective-permute-done.3 = bf16[2,64,512]{2,1,0:T(8,128)(2,1)S(1)} collective-permute-done((bf16[2,64,512]{2,1,0:T(8,128)(2,1)S(1)}, bf16[2,64,512]{2,1,0:T(8,128)(2,1)S(1)}, u32[]{:S(2)}, u32[]{:S(2)}) %collective-permute-start.3) | collective-permute-done | bytes 131104 | tf_op jit(solution)/shard_map/ppermute | solution.py:17
  18.7 1.0 collective-permute-done.4
  20.0 1.7 %collective-permute-start.10 = (f32[1024]{0:T(1024)S(1)}, f32[1024]{0:T(1024)S(1)}, u32[]{:S(2)}, u32[]{:S(2)}) collective-permute-start(f32[1024]{0:T(1024)S(1)} %fusion.80), channel_id=1, source_target_pairs={{0,16},{8,24},{16,0},{24,8},{32,48},{40,56},{48,32},{56,40},{1,17}... | collective-permute-start | bytes 12296 | tf_op jit(solution)/shard_map/ppermute | solution.py:17
  21.6 1.5 %collective-permute-start.7 = (bf16[4,64,512]{2,1,0:T(8,128)(2,1)S(1)}, bf16[4,64,512]{2,1,0:T(8,128)(2,1)S(1)}, u32[]{:S(2)}, u32[]{:S(2)}) collective-permute-start(bf16[4,64,512]{2,1,0:T(8,128)(2,1)S(1)} %pad_maximum_fusion.6), channel_id=1, source_target_pairs={{0,4},{1,5},{2,6},{3,7},{4,0},{5,1},{6,2},{7,3},{8,12},{9,13},{10,... | collective-permute-start | bytes 786440 | tf_op jit(solution)/shard_map/ppermute | solution.py:17
  24.4 3.0 %collective-permute-start.11 = (f32[1024]{0:T(1024)S(1)}, f32[1024]{0:T(1024)S(1)}, u32[]{:S(2)}, u32[]{:S(2)}) collective-permute-start(f32[1024]{0:T(1024)S(1)} %add.627), channel_id=1, source_target_pairs={{0,32},{8,40},{16,48},{24,56},{32,0},{40,8},{48,16},{56,24},{1,33}... | collective-permute-start | bytes 12296 | tf_op jit(solution)/shard_map/ppermute | solution.py:17
  27.3 2.2 %collective-permute-done.11 = f32[1024]{0:T(1024)S(1)} collective-permute-done((f32[1024]{0:T(1024)S(1)}, f32[1024]{0:T(1024)S(1)}, u32[]{:S(2)}, u32[]{:S(2)}) %collective-permute-start.11) | collective-permute-done | bytes 4128 | tf_op jit(solution)/shard_map/ppermute | solution.py:17
  31.4 1.4 %broadcast_select_fusion.3 = (bf16[8,32,1536]{2,1,0:T(8,128)(2,1)S(1)}, bf16[8,32,1536]{2,1,0:T(8,128)(2,1)}, bf16[8,32,1536]{2,1,0:T(8,128)(2,1)}, bf16[8,32,1536]{2,1,0:T(8,128)(2,1)S(1)}) fusion(bf16[8,32,1536]{2,1,0:T(8,128)(2,1)S(1)} %bitcast.83, pred[]{:T(512)S(6)} %eq.227, bf16[8,64,1536]{2,1,0:T(8,128)(2,1)S(1)} %slice_dynamic-update-slice_fusion, ...), kind=kLoop, calls=%fused_computation.45 | loop fusion | flops 786432 | bytes 6291457 | tf_op jit(solution)/shard_map/jit(_where)/select_n | solution.py:114
  32.8 1.2 slice-done.2
  34.1 2.6 %fusion.8 = f32[256,3072]{1,0:T(8,128)S(1)} fusion(bf16[256,1536]{1,0:T(8,128)(2,1)S(1)} %bitcast.94, bf16[1,1536,3072]{2,1,0:T(8,128)(2,1)S(1)} %bitcast.74), kind=kOutput, calls=%fused_computation.9 | convolution fusion | flops 2415919104 | bytes 13369344 | tf_op jit(solution)/shard_map/dot_general | solution.py:115
  36.9 2.6 %fusion.6 = f32[256,3072]{1,0:T(8,128)S(1)} fusion(bf16[256,1536]{1,0:T(8,128)(2,1)S(1)} %bitcast.93, bf16[1,1536,3072]{2,1,0:T(8,128)(2,1)S(1)} %bitcast.74), kind=kOutput, calls=%fused_computation.7 | convolution fusion | flops 2415919104 | bytes 13369344 | tf_op jit(solution)/shard_map/dot_general | solution.py:115
  40.4 1.1 collective-permute-start.13
  42.3 1.3 %fusion.21 = f32[3072]{0:T(1024)S(1)} fusion(bf16[8,1536]{1,0:T(8,128)(2,1)S(1)} %maximum_maximum_fusion.2, bf16[1,1536,3072]{2,1,0:T(8,128)(2,1)S(1)} %bitcast.74), kind=kOutput, calls=%fused_computation.33 | convolution fusion | flops 75518976 | bytes 9474048 | tf_op jit(solution)/shard_map/dot_general | solution.py:127
  45.2 3.3 %collective-permute-done.13 = bf16[2,32,3072]{2,1,0:T(8,128)(2,1)S(1)} collective-permute-done((bf16[2,32,3072]{2,1,0:T(8,128)(2,1)S(1)}, bf16[2,32,3072]{2,1,0:T(8,128)(2,1)S(1)}, u32[]{:S(2)}, u32[]{:S(2)}) %collective-permute-start.13) | collective-permute-done | bytes 393248 | tf_op jit(solution)/shard_map/ppermute | solution.py:26
  49.4 2.3 %collective-permute-start.14 = (bf16[1,32,3072]{2,1,0:T(8,128)(2,1)}, bf16[1,32,3072]{2,1,0:T(8,128)(2,1)}, u32[]{:S(2)}, u32[]{:S(2)}) collective-permute-start(bf16[1,32,3072]{2,1,0:T(8,128)(2,1)} %slice.428), channel_id=1, source_target_pairs={{0,48},{8,24},{16,32},{24,8},{32,16},{40,56},{48,0},{56,40},{1,49}... | collective-permute-start | bytes 589832 | tf_op jit(solution)/shard_map/ppermute | solution.py:26
  51.6 1.4 %collective-permute-done.17 = bf16[2,32,3072]{2,1,0:T(8,128)(2,1)S(1)} collective-permute-done((bf16[2,32,3072]{2,1,0:T(8,128)(2,1)S(1)}, bf16[2,32,3072]{2,1,0:T(8,128)(2,1)S(1)}, u32[]{:S(2)}, u32[]{:S(2)}) %collective-permute-start.17) | collective-permute-done | bytes 393248 | tf_op jit(solution)/shard_map/ppermute | solution.py:26
  53.2 1.5 %collective-permute-start.20 = (f32[1,3072]{1,0:T(1,128)S(1)}, f32[1,3072]{1,0:T(1,128)S(1)}, u32[]{:S(2)}, u32[]{:S(2)}) collective-permute-start(f32[1,3072]{1,0:T(1,128)S(1)} %add.669), channel_id=1, source_target_pairs={{0,16},{8,24},{16,0},{24,8},{32,48},{40,56},{48,32},{56,40},{1,17}... | collective-permute-start | bytes 36872 | tf_op jit(solution)/shard_map/ppermute | solution.py:17
  54.6 3.0 %collective-permute-start.19 = (bf16[1,32,3072]{2,1,0:T(8,128)(2,1)S(1)}, bf16[1,32,3072]{2,1,0:T(8,128)(2,1)S(1)}, u32[]{:S(2)}, u32[]{:S(2)}) collective-permute-start(bf16[1,32,3072]{2,1,0:T(8,128)(2,1)S(1)} %slice.427), channel_id=1, source_target_pairs={{0,48},{8,24},{16,32},{24,8},{32,16},{40,56},{48,0},{56,40},{1,49}... | collective-permute-start | bytes 589832 | tf_op jit(solution)/shard_map/ppermute | solution.py:26
  57.7 1.3 fusion.49
  59.0 2.5 %collective-permute-start.15 = (bf16[32,3072]{1,0:T(8,128)(2,1)S(1)}, bf16[32,3072]{1,0:T(8,128)(2,1)S(1)}, u32[]{:S(2)}, u32[]{:S(2)}) collective-permute-start(bf16[32,3072]{1,0:T(8,128)(2,1)S(1)} %get-tuple-element.103), channel_id=1, source_target_pairs={{0,64},{64,0},{1,65},{65,1},{2,66},{66,2},{3,67},{67,3},{4,68},{68... | collective-permute-start | bytes 589832 | tf_op jit(solution)/shard_map/ppermute | solution.py:17
  61.9 3.2 %collective-permute-start.21 = (f32[1,3072]{1,0:T(1,128)S(1)}, f32[1,3072]{1,0:T(1,128)S(1)}, u32[]{:S(2)}, u32[]{:S(2)}) collective-permute-start(f32[1,3072]{1,0:T(1,128)S(1)} %add.674), channel_id=1, source_target_pairs={{0,32},{8,40},{16,48},{24,56},{32,0},{40,8},{48,16},{56,24},{1,33}... | collective-permute-start | bytes 36872 | tf_op jit(solution)/shard_map/ppermute | solution.py:17
  65.1 1.2 collective-permute-start.25
  67.7 3.1 %collective-permute-start.22 = (bf16[1,32,3200]{2,1,0:T(8,128)(2,1)S(1)}, bf16[1,32,3200]{2,1,0:T(8,128)(2,1)S(1)}, u32[]{:S(2)}, u32[]{:S(2)}) collective-permute-start(bf16[1,32,3200]{2,1,0:T(8,128)(2,1)S(1)} %fusion.57), channel_id=1, source_target_pairs={{0,48},{8,24},{16,32},{24,8},{32,16},{40,56},{48,0},{56,40},{1,49}... | collective-permute-start | bytes 614408 | tf_op jit(solution)/shard_map/ppermute | solution.py:26
  70.8 1.4 %collective-permute-done.25 = bf16[32,3072]{1,0:T(8,128)(2,1)S(1)} collective-permute-done((bf16[32,3072]{1,0:T(8,128)(2,1)S(1)}, bf16[32,3072]{1,0:T(8,128)(2,1)S(1)}, u32[]{:S(2)}, u32[]{:S(2)}) %collective-permute-start.25) | collective-permute-done | bytes 196640 | tf_op jit(solution)/shard_map/ppermute | solution.py:17
  72.9 1.3 collective-permute-start.26
  74.2 1.6 %collective-permute-done.22 = bf16[1,32,3200]{2,1,0:T(8,128)(2,1)S(1)} collective-permute-done((bf16[1,32,3200]{2,1,0:T(8,128)(2,1)S(1)}, bf16[1,32,3200]{2,1,0:T(8,128)(2,1)S(1)}, u32[]{:S(2)}, u32[]{:S(2)}) %collective-permute-start.22) | collective-permute-done | bytes 204832 | tf_op jit(solution)/shard_map/ppermute | solution.py:26
  75.8 2.5 %collective-permute-start.23 = (bf16[2,32,3200]{2,1,0:T(8,128)(2,1)S(1)}, bf16[2,32,3200]{2,1,0:T(8,128)(2,1)S(1)}, u32[]{:S(2)}, u32[]{:S(2)}) collective-permute-start(bf16[2,32,3200]{2,1,0:T(8,128)(2,1)S(1)} %pad_maximum_fusion.4), channel_id=1, source_target_pairs={{0,16},{8,56},{16,0},{24,40},{32,48},{40,24},{48,32},{56,8},{1,17}... | collective-permute-start | bytes 1228808 | tf_op jit(solution)/shard_map/ppermute | solution.py:26
  78.3 3.9 %collective-permute-done.26 = bf16[1,32,3200]{2,1,0:T(8,128)(2,1)S(1)} collective-permute-done((bf16[1,32,3200]{2,1,0:T(8,128)(2,1)S(1)}, bf16[1,32,3200]{2,1,0:T(8,128)(2,1)S(1)}, u32[]{:S(2)}, u32[]{:S(2)}) %collective-permute-start.26) | collective-permute-done | bytes 204832 | tf_op jit(solution)/shard_map/ppermute | solution.py:26
  82.7 1.5 %collective-permute-done.23 = bf16[2,32,3200]{2,1,0:T(8,128)(2,1)S(1)} collective-permute-done((bf16[2,32,3200]{2,1,0:T(8,128)(2,1)S(1)}, bf16[2,32,3200]{2,1,0:T(8,128)(2,1)S(1)}, u32[]{:S(2)}, u32[]{:S(2)}) %collective-permute-start.23) | collective-permute-done | bytes 409632 | tf_op jit(solution)/shard_map/ppermute | solution.py:26
  84.7 5.6 %collective-permute-done.27 = bf16[2,32,3200]{2,1,0:T(8,128)(2,1)S(1)} collective-permute-done((bf16[2,32,3200]{2,1,0:T(8,128)(2,1)S(1)}, bf16[2,32,3200]{2,1,0:T(8,128)(2,1)S(1)}, u32[]{:S(2)}, u32[]{:S(2)}) %collective-permute-start.27) | collective-permute-done | bytes 409632 | tf_op jit(solution)/shard_map/ppermute | solution.py:26
  91.9 2.6 %fusion.2 = f32[256,1536]{1,0:T(8,128)S(1)} fusion(bf16[1,1536,3072]{2,1,0:T(8,128)(2,1)S(1)} %bitcast.76, bf16[128,3072]{1,0:T(8,128)(2,1)S(1)} %slice.312, bf16[128,3072]{1,0:T(8,128)(2,1)S(1)} %slice.311), kind=kOutput, calls=%fused_computation.3 | convolution fusion | flops 2419064832 | bytes 12582912 | tf_op jit(solution)/shard_map/dot_general | solution.py:178
  94.7 2.6 %fusion = f32[256,1536]{1,0:T(8,128)S(1)} fusion(bf16[1,1536,3072]{2,1,0:T(8,128)(2,1)S(1)} %bitcast.76, bf16[128,3072]{1,0:T(8,128)(2,1)S(1)} %slice.316, bf16[128,3072]{1,0:T(8,128)(2,1)S(1)} %slice.315), kind=kOutput, calls=%fused_computation.1 | convolution fusion | flops 2419064832 | bytes 12582912 | tf_op jit(solution)/shard_map/dot_general | solution.py:178
  98.4 1.6 %collective-permute-start.29 = (f32[1536]{0:T(1024)S(1)}, f32[1536]{0:T(1024)S(1)}, u32[]{:S(2)}, u32[]{:S(2)}) collective-permute-start(f32[1536]{0:T(1024)S(1)} %div.314), channel_id=1, source_target_pairs={{0,1},{1,0},{2,3},{3,2},{4,5},{5,4},{6,7},{7,6},{8,9},{9,8},{10,11... | collective-permute-start | bytes 18440 | tf_op jit(solution)/shard_map/ppermute | solution.py:17
  100.8 1.5 %collective-permute-start.31 = (bf16[4,32,1664]{2,1,0:T(8,128)(2,1)S(1)}, bf16[4,32,1664]{2,1,0:T(8,128)(2,1)S(1)}, u32[]{:S(2)}, u32[]{:S(2)}) collective-permute-start(bf16[4,32,1664]{2,1,0:T(8,128)(2,1)S(1)} %maximum_maximum_fusion), channel_id=1, source_target_pairs={{0,1},{1,0},{2,3},{3,2},{4,5},{5,4},{6,7},{7,6},{8,11},{9,10},{10,... | collective-permute-start | bytes 1277960 | tf_op jit(solution)/shard_map/ppermute | solution.py:36
  102.3 3.3 %collective-permute-start.34 = (f32[1536]{0:T(1024)S(1)}, f32[1536]{0:T(1024)S(1)}, u32[]{:S(2)}, u32[]{:S(2)}) collective-permute-start(f32[1536]{0:T(1024)S(1)} %add.697), channel_id=1, source_target_pairs={{0,2},{1,3},{2,0},{3,1},{4,6},{5,7},{6,4},{7,5},{8,10},{9,11},{10,... | collective-permute-start | bytes 18440 | tf_op jit(solution)/shard_map/ppermute | solution.py:17
  105.6 7.5 %convolution_convert_fusion = bf16[1536,3072]{1,0:T(8,128)(2,1)} fusion(bf16[512,1536]{1,0:T(8,128)(2,1)S(1)} %pad_maximum_fusion.1, bf16[512,3072]{1,0:T(8,128)(2,1)S(1)} %pad_maximum_fusion), kind=kOutput, calls=%fused_computation | convolution fusion | flops 4836556800 | bytes 14155776 | tf_op jit(solution)/shard_map/dot_general | solution.py:207
  113.2 1.9 %collective-permute-done.34 = f32[1536]{0:T(1024)S(1)} collective-permute-done((f32[1536]{0:T(1024)S(1)}, f32[1536]{0:T(1024)S(1)}, u32[]{:S(2)}, u32[]{:S(2)}) %collective-permute-start.34) | collective-permute-done | bytes 6176 | tf_op jit(solution)/shard_map/ppermute | solution.py:17
  115.6 1.0 collective-permute-start.35
  116.7 2.3 %collective-permute-start.32 = (bf16[2,32,1664]{2,1,0:T(8,128)(2,1)S(1)}, bf16[2,32,1664]{2,1,0:T(8,128)(2,1)S(1)}, u32[]{:S(2)}, u32[]{:S(2)}) collective-permute-start(bf16[2,32,1664]{2,1,0:T(8,128)(2,1)S(1)} %slice.426), channel_id=1, source_target_pairs={{0,3},{1,2},{2,1},{3,0},{4,7},{5,6},{6,5},{7,4},{8,9},{9,8},{10,11... | collective-permute-start | bytes 638984 | tf_op jit(solution)/shard_map/ppermute | solution.py:36
  119.0 3.6 %collective-permute-done.35 = bf16[2,32,1664]{2,1,0:T(8,128)(2,1)S(1)} collective-permute-done((bf16[2,32,1664]{2,1,0:T(8,128)(2,1)S(1)}, bf16[2,32,1664]{2,1,0:T(8,128)(2,1)S(1)}, u32[]{:S(2)}, u32[]{:S(2)}) %collective-permute-start.35) | collective-permute-done | bytes 213024 | tf_op jit(solution)/shard_map/ppermute | solution.py:36
  122.7 1.9 %collective-permute-start.36 = (bf16[32,1664]{1,0:T(8,128)(2,1)S(1)}, bf16[32,1664]{1,0:T(8,128)(2,1)S(1)}, u32[]{:S(2)}, u32[]{:S(2)}) collective-permute-start(bf16[32,1664]{1,0:T(8,128)(2,1)S(1)} %fusion.61), channel_id=1, source_target_pairs={{0,4},{1,5},{2,6},{3,7},{4,0},{5,1},{6,2},{7,3},{8,12},{9,13},{10,... | collective-permute-start | bytes 319496 | tf_op jit(solution)/shard_map/ppermute | solution.py:17
  125.0 1.9 %collective-permute-start.33 = (bf16[32,1664]{1,0:T(8,128)(2,1)S(1)}, bf16[32,1664]{1,0:T(8,128)(2,1)S(1)}, u32[]{:S(2)}, u32[]{:S(2)}) collective-permute-start(bf16[32,1664]{1,0:T(8,128)(2,1)S(1)} %fusion.60), channel_id=1, source_target_pairs={{0,4},{1,5},{2,6},{3,7},{4,0},{5,1},{6,2},{7,3},{8,12},{9,13},{10,... | collective-permute-start | bytes 319496 | tf_op jit(solution)/shard_map/ppermute | solution.py:17
  128.1 1.6 %collective-permute-done.33 = bf16[32,1664]{1,0:T(8,128)(2,1)S(1)} collective-permute-done((bf16[32,1664]{1,0:T(8,128)(2,1)S(1)}, bf16[32,1664]{1,0:T(8,128)(2,1)S(1)}, u32[]{:S(2)}, u32[]{:S(2)}) %collective-permute-start.33) | collective-permute-done | bytes 106528 | tf_op jit(solution)/shard_map/ppermute | solution.py:17
  (198 shorter events, 20.7 us)
Async XLA Ops:
  0.6 10.2 %copy-start = (bf16[512,1536]{1,0:T(8,128)(2,1)S(1)}, bf16[512,1536]{1,0:T(8,128)(2,1)}, u32[]{:S(2)}) copy-start(bf16[512,1536]{1,0:T(8,128)(2,1)} %param.4) | copy-start | bytes 4718596
  0.6 32.2 %slice-start = ((s8[9437184]{0:T(1024)(128)(4,1)}), s8[1048576]{0:T(1024)(128)(4,1)S(1)}, s32[]{:S(2)}) async-start(s8[9437184]{0:T(1024)(128)(4,1)} %bitcast.73), calls=%async_computation | async-start | bytes 2097152
  1.7 7.0 %collective-permute-start.2 = (bf16[1,64,512]{2,1,0:T(8,128)(2,1)S(1)}, bf16[1,64,512]{2,1,0:T(8,128)(2,1)S(1)}, u32[]{:S(2)}, u32[]{:S(2)}) collective-permute-start(bf16[1,64,512]{2,1,0:T(8,128)(2,1)S(1)} %get-tuple-element.143), channel_id=1, source_target_pairs={{0,4},{1,5},{2,6},{3,7},{4,0},{5,1},{6,2},{7,3},{8,12},{9,13},{10,... | collective-permute-start | bytes 196616 | tf_op jit(solution)/shard_map/ppermute | solution.py:17
  3.4 5.4 %collective-permute-start = (bf16[1,64,512]{2,1,0:T(8,128)(2,1)S(1)}, bf16[1,64,512]{2,1,0:T(8,128)(2,1)S(1)}, u32[]{:S(2)}, u32[]{:S(2)}) collective-permute-start(bf16[1,64,512]{2,1,0:T(8,128)(2,1)S(1)} %get-tuple-element.144), channel_id=1, source_target_pairs={{0,1},{1,0},{2,3},{3,2},{4,5},{5,4},{6,7},{7,6},{8,9},{9,8},{10,11... | collective-permute-start | bytes 196616 | tf_op jit(solution)/shard_map/ppermute | solution.py:17
  5.3 5.5 %collective-permute-start.1 = (bf16[1,64,512]{2,1,0:T(8,128)(2,1)S(1)}, bf16[1,64,512]{2,1,0:T(8,128)(2,1)S(1)}, u32[]{:S(2)}, u32[]{:S(2)}) collective-permute-start(bf16[1,64,512]{2,1,0:T(8,128)(2,1)S(1)} %get-tuple-element.145), channel_id=1, source_target_pairs={{0,3},{1,2},{2,1},{3,0},{4,7},{5,6},{6,5},{7,4},{8,11},{9,10},{10,... | collective-permute-start | bytes 196616 | tf_op jit(solution)/shard_map/ppermute | solution.py:17
  11.5 4.1 %collective-permute-start.6 = (f32[1024]{0:T(1024)S(1)}, f32[1024]{0:T(1024)S(1)}, u32[]{:S(2)}, u32[]{:S(2)}) collective-permute-start(f32[1024]{0:T(1024)S(1)} %pad_maximum_fusion.15), channel_id=1, source_target_pairs={{0,8},{8,0},{16,24},{24,16},{32,40},{40,32},{48,56},{56,48},{1,9},... | collective-permute-start | bytes 12296 | tf_op jit(solution)/shard_map/ppermute | solution.py:17
  11.6 7.1 %collective-permute-start.3 = (bf16[2,64,512]{2,1,0:T(8,128)(2,1)S(1)}, bf16[2,64,512]{2,1,0:T(8,128)(2,1)S(1)}, u32[]{:S(2)}, u32[]{:S(2)}) collective-permute-start(bf16[2,64,512]{2,1,0:T(8,128)(2,1)S(1)} %pad_maximum_fusion.9), channel_id=1, source_target_pairs={{0,3},{1,2},{2,1},{3,0},{4,7},{5,6},{6,5},{7,4},{8,11},{9,10},{10,... | collective-permute-start | bytes 393224 | tf_op jit(solution)/shard_map/ppermute | solution.py:17
  14.2 5.6 %collective-permute-start.4 = (bf16[2,64,512]{2,1,0:T(8,128)(2,1)S(1)}, bf16[2,64,512]{2,1,0:T(8,128)(2,1)S(1)}, u32[]{:S(2)}, u32[]{:S(2)}) collective-permute-start(bf16[2,64,512]{2,1,0:T(8,128)(2,1)S(1)} %pad_maximum_fusion.10), channel_id=1, source_target_pairs={{0,4},{1,5},{2,6},{3,7},{4,0},{5,1},{6,2},{7,3},{8,12},{9,13},{10,... | collective-permute-start | bytes 393224 | tf_op jit(solution)/shard_map/ppermute | solution.py:17
  14.7 5.3 %collective-permute-start.5 = (bf16[2,64,512]{2,1,0:T(8,128)(2,1)S(1)}, bf16[2,64,512]{2,1,0:T(8,128)(2,1)S(1)}, u32[]{:S(2)}, u32[]{:S(2)}) collective-permute-start(bf16[2,64,512]{2,1,0:T(8,128)(2,1)S(1)} %pad_maximum_fusion.11), channel_id=1, source_target_pairs={{0,1},{1,0},{2,3},{3,2},{4,5},{5,4},{6,7},{7,6},{8,9},{9,8},{10,11... | collective-permute-start | bytes 393224 | tf_op jit(solution)/shard_map/ppermute | solution.py:17
  20.0 4.3 %collective-permute-start.10 = (f32[1024]{0:T(1024)S(1)}, f32[1024]{0:T(1024)S(1)}, u32[]{:S(2)}, u32[]{:S(2)}) collective-permute-start(f32[1024]{0:T(1024)S(1)} %fusion.80), channel_id=1, source_target_pairs={{0,16},{8,24},{16,0},{24,8},{32,48},{40,56},{48,32},{56,40},{1,17}... | collective-permute-start | bytes 12296 | tf_op jit(solution)/shard_map/ppermute | solution.py:17
  21.6 8.7 %collective-permute-start.7 = (bf16[4,64,512]{2,1,0:T(8,128)(2,1)S(1)}, bf16[4,64,512]{2,1,0:T(8,128)(2,1)S(1)}, u32[]{:S(2)}, u32[]{:S(2)}) collective-permute-start(bf16[4,64,512]{2,1,0:T(8,128)(2,1)S(1)} %pad_maximum_fusion.6), channel_id=1, source_target_pairs={{0,4},{1,5},{2,6},{3,7},{4,0},{5,1},{6,2},{7,3},{8,12},{9,13},{10,... | collective-permute-start | bytes 786440 | tf_op jit(solution)/shard_map/ppermute | solution.py:17
  23.1 7.4 %collective-permute-start.8 = (bf16[4,64,512]{2,1,0:T(8,128)(2,1)S(1)}, bf16[4,64,512]{2,1,0:T(8,128)(2,1)S(1)}, u32[]{:S(2)}, u32[]{:S(2)}) collective-permute-start(bf16[4,64,512]{2,1,0:T(8,128)(2,1)S(1)} %pad_maximum_fusion.7), channel_id=1, source_target_pairs={{0,1},{1,0},{2,3},{3,2},{4,5},{5,4},{6,7},{7,6},{8,9},{9,8},{10,11... | collective-permute-start | bytes 786440 | tf_op jit(solution)/shard_map/ppermute | solution.py:17
  23.4 7.9 %collective-permute-start.9 = (bf16[4,64,512]{2,1,0:T(8,128)(2,1)S(1)}, bf16[4,64,512]{2,1,0:T(8,128)(2,1)S(1)}, u32[]{:S(2)}, u32[]{:S(2)}) collective-permute-start(bf16[4,64,512]{2,1,0:T(8,128)(2,1)S(1)} %pad_maximum_fusion.8), channel_id=1, source_target_pairs={{0,3},{1,2},{2,1},{3,0},{4,7},{5,6},{6,5},{7,4},{8,11},{9,10},{10,... | collective-permute-start | bytes 786440 | tf_op jit(solution)/shard_map/ppermute | solution.py:17
  24.4 5.2 %collective-permute-start.11 = (f32[1024]{0:T(1024)S(1)}, f32[1024]{0:T(1024)S(1)}, u32[]{:S(2)}, u32[]{:S(2)}) collective-permute-start(f32[1024]{0:T(1024)S(1)} %add.627), channel_id=1, source_target_pairs={{0,32},{8,40},{16,48},{24,56},{32,0},{40,8},{48,16},{56,24},{1,33}... | collective-permute-start | bytes 12296 | tf_op jit(solution)/shard_map/ppermute | solution.py:17
  36.8 3.5 %collective-permute-start.12 = (bf16[128,3072]{1,0:T(8,128)(2,1)S(1)}, bf16[128,3072]{1,0:T(8,128)(2,1)S(1)}, u32[]{:S(2)}, u32[]{:S(2)}) collective-permute-start(bf16[128,3072]{1,0:T(8,128)(2,1)S(1)} %slice.422), channel_id=1, source_target_pairs={{0,8},{8,0},{16,24},{24,16},{32,40},{40,32},{48,56},{56,48},{1,9},... | collective-permute-start | bytes 2359304 | tf_op jit(solution)/shard_map/ppermute | solution.py:17
  39.6 2.5 %collective-permute-start.16 = (bf16[128,3072]{1,0:T(8,128)(2,1)S(1)}, bf16[128,3072]{1,0:T(8,128)(2,1)S(1)}, u32[]{:S(2)}, u32[]{:S(2)}) collective-permute-start(bf16[128,3072]{1,0:T(8,128)(2,1)S(1)} %slice.421), channel_id=1, source_target_pairs={{0,8},{8,0},{16,24},{24,16},{32,40},{40,32},{48,56},{56,48},{1,9},... | collective-permute-start | bytes 2359304 | tf_op jit(solution)/shard_map/ppermute | solution.py:17
  40.4 8.0 %collective-permute-start.13 = (bf16[2,32,3072]{2,1,0:T(8,128)(2,1)S(1)}, bf16[2,32,3072]{2,1,0:T(8,128)(2,1)S(1)}, u32[]{:S(2)}, u32[]{:S(2)}) collective-permute-start(bf16[2,32,3072]{2,1,0:T(8,128)(2,1)S(1)} %bitcast.95), channel_id=1, source_target_pairs={{0,16},{8,56},{16,0},{24,40},{32,48},{40,24},{48,32},{56,8},{1,17}... | collective-permute-start | bytes 1179656 | tf_op jit(solution)/shard_map/ppermute | solution.py:26
  43.6 1.6 %collective-permute-start.18 = (f32[1,3072]{1,0:T(1,128)S(1)}, f32[1,3072]{1,0:T(1,128)S(1)}, u32[]{:S(2)}, u32[]{:S(2)}) collective-permute-start(f32[1,3072]{1,0:T(1,128)S(1)} %add.668), channel_id=1, source_target_pairs={{0,8},{8,0},{16,24},{24,16},{32,40},{40,32},{48,56},{56,48},{1,9},... | collective-permute-start | bytes 36872 | tf_op jit(solution)/shard_map/ppermute | solution.py:17
  44.4 4.1 %slice-start.6 = ((f32[128,3072]{1,0:T(8,128)}), f32[64,3072]{1,0:T(8,128)S(1)}, s32[]{:S(2)}) async-start(f32[128,3072]{1,0:T(8,128)} %copy-done.1), calls=%async_computation.6 | async-start | bytes 1572864 | tf_op jit(solution)/shard_map/slice | solution.py:131
  44.4 8.7 %slice-start.7 = ((f32[128,3072]{1,0:T(8,128)}), f32[64,3072]{1,0:T(8,128)S(1)}, s32[]{:S(2)}) async-start(f32[128,3072]{1,0:T(8,128)} %copy-done.2), calls=%async_computation.7 | async-start | bytes 1572864 | tf_op jit(solution)/shard_map/slice | solution.py:131
  44.4 8.7 %collective-permute-start.17 = (bf16[2,32,3072]{2,1,0:T(8,128)(2,1)S(1)}, bf16[2,32,3072]{2,1,0:T(8,128)(2,1)S(1)}, u32[]{:S(2)}, u32[]{:S(2)}) collective-permute-start(bf16[2,32,3072]{2,1,0:T(8,128)(2,1)S(1)} %bitcast.96), channel_id=1, source_target_pairs={{0,16},{8,56},{16,0},{24,40},{32,48},{40,24},{48,32},{56,8},{1,17}... | collective-permute-start | bytes 1179656 | tf_op jit(solution)/shard_map/ppermute | solution.py:26
  48.6 4.6 %copy-start.7 = (f32[2,32,3072]{2,1,0:T(8,128)}, f32[2,32,3072]{2,1,0:T(8,128)S(1)}, u32[]{:S(2)}) copy-start(f32[2,32,3072]{2,1,0:T(8,128)S(1)} %convert_add_fusion.1) | copy-start | bytes 2359300
  49.4 8.3 %collective-permute-start.14 = (bf16[1,32,3072]{2,1,0:T(8,128)(2,1)}, bf16[1,32,3072]{2,1,0:T(8,128)(2,1)}, u32[]{:S(2)}, u32[]{:S(2)}) collective-permute-start(bf16[1,32,3072]{2,1,0:T(8,128)(2,1)} %slice.428), channel_id=1, source_target_pairs={{0,48},{8,24},{16,32},{24,8},{32,16},{40,56},{48,0},{56,40},{1,49}... | collective-permute-start | bytes 589832 | tf_op jit(solution)/shard_map/ppermute | solution.py:26
  53.2 4.5 %collective-permute-start.20 = (f32[1,3072]{1,0:T(1,128)S(1)}, f32[1,3072]{1,0:T(1,128)S(1)}, u32[]{:S(2)}, u32[]{:S(2)}) collective-permute-start(f32[1,3072]{1,0:T(1,128)S(1)} %add.669), channel_id=1, source_target_pairs={{0,16},{8,24},{16,0},{24,8},{32,48},{40,56},{48,32},{56,40},{1,17}... | collective-permute-start | bytes 36872 | tf_op jit(solution)/shard_map/ppermute | solution.py:17
  54.6 6.9 %collective-permute-start.19 = (bf16[1,32,3072]{2,1,0:T(8,128)(2,1)S(1)}, bf16[1,32,3072]{2,1,0:T(8,128)(2,1)S(1)}, u32[]{:S(2)}, u32[]{:S(2)}) collective-permute-start(bf16[1,32,3072]{2,1,0:T(8,128)(2,1)S(1)} %slice.427), channel_id=1, source_target_pairs={{0,48},{8,24},{16,32},{24,8},{32,16},{40,56},{48,0},{56,40},{1,49}... | collective-permute-start | bytes 589832 | tf_op jit(solution)/shard_map/ppermute | solution.py:26
  59.0 8.1 %collective-permute-start.15 = (bf16[32,3072]{1,0:T(8,128)(2,1)S(1)}, bf16[32,3072]{1,0:T(8,128)(2,1)S(1)}, u32[]{:S(2)}, u32[]{:S(2)}) collective-permute-start(bf16[32,3072]{1,0:T(8,128)(2,1)S(1)} %get-tuple-element.103), channel_id=1, source_target_pairs={{0,64},{64,0},{1,65},{65,1},{2,66},{66,2},{3,67},{67,3},{4,68},{68... | collective-permute-start | bytes 589832 | tf_op jit(solution)/shard_map/ppermute | solution.py:17
  61.5 29.6 %slice-start.3 = ((s8[9437184]{0:T(1024)(128)(4,1)}), s8[4194304]{0:T(1024)(128)(4,1)S(1)}, s32[]{:S(2)}) async-start(s8[9437184]{0:T(1024)(128)(4,1)} %bitcast.75), calls=%async_computation.3 | async-start | bytes 8388608
  61.9 5.2 %collective-permute-start.21 = (f32[1,3072]{1,0:T(1,128)S(1)}, f32[1,3072]{1,0:T(1,128)S(1)}, u32[]{:S(2)}, u32[]{:S(2)}) collective-permute-start(f32[1,3072]{1,0:T(1,128)S(1)} %add.674), channel_id=1, source_target_pairs={{0,32},{8,40},{16,48},{24,56},{32,0},{40,8},{48,16},{56,24},{1,33}... | collective-permute-start | bytes 36872 | tf_op jit(solution)/shard_map/ppermute | solution.py:17
  65.1 7.2 %collective-permute-start.25 = (bf16[32,3072]{1,0:T(8,128)(2,1)S(1)}, bf16[32,3072]{1,0:T(8,128)(2,1)S(1)}, u32[]{:S(2)}, u32[]{:S(2)}) collective-permute-start(bf16[32,3072]{1,0:T(8,128)(2,1)S(1)} %get-tuple-element.65), channel_id=1, source_target_pairs={{0,64},{64,0},{1,65},{65,1},{2,66},{66,2},{3,67},{67,3},{4,68},{68... | collective-permute-start | bytes 589832 | tf_op jit(solution)/shard_map/ppermute | solution.py:17
  67.7 8.0 %collective-permute-start.22 = (bf16[1,32,3200]{2,1,0:T(8,128)(2,1)S(1)}, bf16[1,32,3200]{2,1,0:T(8,128)(2,1)S(1)}, u32[]{:S(2)}, u32[]{:S(2)}) collective-permute-start(bf16[1,32,3200]{2,1,0:T(8,128)(2,1)S(1)} %fusion.57), channel_id=1, source_target_pairs={{0,48},{8,24},{16,32},{24,8},{32,16},{40,56},{48,0},{56,40},{1,49}... | collective-permute-start | bytes 614408 | tf_op jit(solution)/shard_map/ppermute | solution.py:26
  72.9 11.6 %copy-start.4 = (bf16[256,1536]{1,0:T(8,128)(2,1)S(1)}, bf16[256,1536]{1,0:T(8,128)(2,1)}, u32[]{:S(2)}) copy-start(bf16[256,1536]{1,0:T(8,128)(2,1)} %copy-done.3) | copy-start | bytes 2359300
  72.9 11.6 %copy-start.5 = (bf16[8,32,1536]{2,1,0:T(8,128)(2,1)S(1)}, bf16[8,32,1536]{2,1,0:T(8,128)(2,1)}, u32[]{:S(2)}) copy-start(bf16[8,32,1536]{2,1,0:T(8,128)(2,1)} %get-tuple-element.124) | copy-start | bytes 2359300
  72.9 11.6 %copy-start.6 = (bf16[8,32,1536]{2,1,0:T(8,128)(2,1)S(1)}, bf16[8,32,1536]{2,1,0:T(8,128)(2,1)}, u32[]{:S(2)}) copy-start(bf16[8,32,1536]{2,1,0:T(8,128)(2,1)} %get-tuple-element.125) | copy-start | bytes 2359300
  72.9 9.3 %collective-permute-start.26 = (bf16[1,32,3200]{2,1,0:T(8,128)(2,1)S(1)}, bf16[1,32,3200]{2,1,0:T(8,128)(2,1)S(1)}, u32[]{:S(2)}, u32[]{:S(2)}) collective-permute-start(bf16[1,32,3200]{2,1,0:T(8,128)(2,1)S(1)} %fusion.58), channel_id=1, source_target_pairs={{0,48},{8,24},{16,32},{24,8},{32,16},{40,56},{48,0},{56,40},{1,49}... | collective-permute-start | bytes 614408 | tf_op jit(solution)/shard_map/ppermute | solution.py:26
  75.8 8.4 %collective-permute-start.23 = (bf16[2,32,3200]{2,1,0:T(8,128)(2,1)S(1)}, bf16[2,32,3200]{2,1,0:T(8,128)(2,1)S(1)}, u32[]{:S(2)}, u32[]{:S(2)}) collective-permute-start(bf16[2,32,3200]{2,1,0:T(8,128)(2,1)S(1)} %pad_maximum_fusion.4), channel_id=1, source_target_pairs={{0,16},{8,56},{16,0},{24,40},{32,48},{40,24},{48,32},{56,8},{1,17}... | collective-permute-start | bytes 1228808 | tf_op jit(solution)/shard_map/ppermute | solution.py:26
  82.3 8.9 %slice-start.4 = ((s8[9437184]{0:T(1024)(128)(4,1)}), s8[4194304]{0:T(1024)(128)(4,1)S(1)}, s32[]{:S(2)}) async-start(s8[9437184]{0:T(1024)(128)(4,1)} %bitcast.75), calls=%async_computation.4 | async-start | bytes 8388608
  82.3 8.0 %collective-permute-start.27 = (bf16[2,32,3200]{2,1,0:T(8,128)(2,1)S(1)}, bf16[2,32,3200]{2,1,0:T(8,128)(2,1)S(1)}, u32[]{:S(2)}, u32[]{:S(2)}) collective-permute-start(bf16[2,32,3200]{2,1,0:T(8,128)(2,1)S(1)} %pad_maximum_fusion.5), channel_id=1, source_target_pairs={{0,16},{8,56},{16,0},{24,40},{32,48},{40,24},{48,32},{56,8},{1,17}... | collective-permute-start | bytes 1228808 | tf_op jit(solution)/shard_map/ppermute | solution.py:26
  84.3 6.7 %collective-permute-start.24 = (bf16[128,3200]{1,0:T(8,128)(2,1)S(1)}, bf16[128,3200]{1,0:T(8,128)(2,1)S(1)}, u32[]{:S(2)}, u32[]{:S(2)}) collective-permute-start(bf16[128,3200]{1,0:T(8,128)(2,1)S(1)} %bitcast.85), channel_id=1, source_target_pairs={{0,8},{8,0},{16,24},{24,16},{32,40},{40,32},{48,56},{56,48},{1,9},... | collective-permute-start | bytes 2457608 | tf_op jit(solution)/shard_map/ppermute | solution.py:17
  90.4 4.2 %collective-permute-start.28 = (bf16[128,3200]{1,0:T(8,128)(2,1)S(1)}, bf16[128,3200]{1,0:T(8,128)(2,1)S(1)}, u32[]{:S(2)}, u32[]{:S(2)}) collective-permute-start(bf16[128,3200]{1,0:T(8,128)(2,1)S(1)} %bitcast.88), channel_id=1, source_target_pairs={{0,8},{8,0},{16,24},{24,16},{32,40},{40,32},{48,56},{56,48},{1,9},... | collective-permute-start | bytes 2457608 | tf_op jit(solution)/shard_map/ppermute | solution.py:17
  98.4 3.9 %collective-permute-start.29 = (f32[1536]{0:T(1024)S(1)}, f32[1536]{0:T(1024)S(1)}, u32[]{:S(2)}, u32[]{:S(2)}) collective-permute-start(f32[1536]{0:T(1024)S(1)} %div.314), channel_id=1, source_target_pairs={{0,1},{1,0},{2,3},{3,2},{4,5},{5,4},{6,7},{7,6},{8,9},{9,8},{10,11... | collective-permute-start | bytes 18440 | tf_op jit(solution)/shard_map/ppermute | solution.py:17
  100.2 14.9 %collective-permute-start.30 = (bf16[4,32,1664]{2,1,0:T(8,128)(2,1)S(1)}, bf16[4,32,1664]{2,1,0:T(8,128)(2,1)S(1)}, u32[]{:S(2)}, u32[]{:S(2)}) collective-permute-start(bf16[4,32,1664]{2,1,0:T(8,128)(2,1)S(1)} %maximum_maximum_fusion.1), channel_id=1, source_target_pairs={{0,1},{1,0},{2,3},{3,2},{4,5},{5,4},{6,7},{7,6},{8,11},{9,10},{10,... | collective-permute-start | bytes 1277960 | tf_op jit(solution)/shard_map/ppermute | solution.py:36
  100.8 14.3 %collective-permute-start.31 = (bf16[4,32,1664]{2,1,0:T(8,128)(2,1)S(1)}, bf16[4,32,1664]{2,1,0:T(8,128)(2,1)S(1)}, u32[]{:S(2)}, u32[]{:S(2)}) collective-permute-start(bf16[4,32,1664]{2,1,0:T(8,128)(2,1)S(1)} %maximum_maximum_fusion), channel_id=1, source_target_pairs={{0,1},{1,0},{2,3},{3,2},{4,5},{5,4},{6,7},{7,6},{8,11},{9,10},{10,... | collective-permute-start | bytes 1277960 | tf_op jit(solution)/shard_map/ppermute | solution.py:36
  102.3 12.8 %collective-permute-start.34 = (f32[1536]{0:T(1024)S(1)}, f32[1536]{0:T(1024)S(1)}, u32[]{:S(2)}, u32[]{:S(2)}) collective-permute-start(f32[1536]{0:T(1024)S(1)} %add.697), channel_id=1, source_target_pairs={{0,2},{1,3},{2,0},{3,1},{4,6},{5,7},{6,4},{7,5},{8,10},{9,11},{10,... | collective-permute-start | bytes 18440 | tf_op jit(solution)/shard_map/ppermute | solution.py:17
  115.3 11.6 %collective-permute-start.37 = (f32[1536]{0:T(1024)S(1)}, f32[1536]{0:T(1024)S(1)}, u32[]{:S(2)}, u32[]{:S(2)}) collective-permute-start(f32[1536]{0:T(1024)S(1)} %add.702), channel_id=1, source_target_pairs={{0,4},{1,5},{2,6},{3,7},{4,0},{5,1},{6,2},{7,3},{8,12},{9,13},{10,... | collective-permute-start | bytes 18440 | tf_op jit(solution)/shard_map/ppermute | solution.py:17
  115.6 7.1 %collective-permute-start.35 = (bf16[2,32,1664]{2,1,0:T(8,128)(2,1)S(1)}, bf16[2,32,1664]{2,1,0:T(8,128)(2,1)S(1)}, u32[]{:S(2)}, u32[]{:S(2)}) collective-permute-start(bf16[2,32,1664]{2,1,0:T(8,128)(2,1)S(1)} %slice.425), channel_id=1, source_target_pairs={{0,3},{1,2},{2,1},{3,0},{4,7},{5,6},{6,5},{7,4},{8,9},{9,8},{10,11... | collective-permute-start | bytes 638984 | tf_op jit(solution)/shard_map/ppermute | solution.py:36
  116.7 8.2 %collective-permute-start.32 = (bf16[2,32,1664]{2,1,0:T(8,128)(2,1)S(1)}, bf16[2,32,1664]{2,1,0:T(8,128)(2,1)S(1)}, u32[]{:S(2)}, u32[]{:S(2)}) collective-permute-start(bf16[2,32,1664]{2,1,0:T(8,128)(2,1)S(1)} %slice.426), channel_id=1, source_target_pairs={{0,3},{1,2},{2,1},{3,0},{4,7},{5,6},{6,5},{7,4},{8,9},{9,8},{10,11... | collective-permute-start | bytes 638984 | tf_op jit(solution)/shard_map/ppermute | solution.py:36
  122.7 4.8 %collective-permute-start.36 = (bf16[32,1664]{1,0:T(8,128)(2,1)S(1)}, bf16[32,1664]{1,0:T(8,128)(2,1)S(1)}, u32[]{:S(2)}, u32[]{:S(2)}) collective-permute-start(bf16[32,1664]{1,0:T(8,128)(2,1)S(1)} %fusion.61), channel_id=1, source_target_pairs={{0,4},{1,5},{2,6},{3,7},{4,0},{5,1},{6,2},{7,3},{8,12},{9,13},{10,... | collective-permute-start | bytes 319496 | tf_op jit(solution)/shard_map/ppermute | solution.py:17
  125.0 4.8 %collective-permute-start.33 = (bf16[32,1664]{1,0:T(8,128)(2,1)S(1)}, bf16[32,1664]{1,0:T(8,128)(2,1)S(1)}, u32[]{:S(2)}, u32[]{:S(2)}) collective-permute-start(bf16[32,1664]{1,0:T(8,128)(2,1)S(1)} %fusion.60), channel_id=1, source_target_pairs={{0,4},{1,5},{2,6},{3,7},{4,0},{5,1},{6,2},{7,3},{8,12},{9,13},{10,... | collective-permute-start | bytes 319496 | tf_op jit(solution)/shard_map/ppermute | solution.py:17
  (6 other events, 16.6 us)

commit v5 on v4

--- a/solution.py
+++ b/solution.py
@@ -210,8 +210,8 @@
     weight_grads, got = lax.optimization_barrier((weight_grads, got))
     parts = [p[4:] + g.astype(F32) for p, g in zip(parts, got)]
     send = [p[:2].astype(BF16) for p in parts]
-    send[-1], gain_grad = lax.optimization_barrier((send[-1], gain_grad))
     got = [over_z(x, 1) for x in send]
+    gain_grad, _ = lax.optimization_barrier((gain_grad, send))
     other_gain = exchange(gain_grad, "col", 4)
     parts = [p[2:] + g.astype(F32) for p, g in zip(parts, got)]
     got = [exchange(p[0].astype(BF16), "col", 4) for p in parts]

time: 131 us -> 131 us (level)
  starting transfers between devices: 55.2 us -> 52 us
  waiting for transfers between devices: 37.4 us -> 40.4 us
    ppermute x26, starting transfers between devices: 35.5 us -> 32.3 us  [exchange(): return lax.ppermute(block, axis, [(i, i ^ mask) for i in ranks])]
    ppermute x26, waiting for transfers between devices: 16 us -> 17.6 us  [exchange(): return lax.ppermute(block, axis, [(i, i ^ mask) for i in ranks])]
    ppermute x4, waiting for transfers between devices: 3.96 us -> 5.32 us  [over_z(): return lax.ppermute(block, ('row', 'col'), route)]
where the time goes in v5:
time: 131 us
  starting transfers between devices  52 us (40%)
  waiting for transfers between devices  40.4 us (31%)
  matrix products  19.4 us (15%)
  other arithmetic  10.6 us (8%)
  local copies, waits for them, and re-layouts  6.44 us (5%)
  between operations  1.79 us (1%)
    ppermute x26, starting transfers between devices, exchange(): return lax.ppermute(block, axis, [(i, i ^ mask) for i in ranks])  32.3 us
    ppermute x26, waiting for transfers between devices, exchange(): return lax.ppermute(block, axis, [(i, i ^ mask) for i in ranks])  17.6 us
    ppermute x8, waiting for transfers between devices, over_y(): lax.ppermute(block, 'row', [(i, i ^ 2 * mask_of(i % 2, turn)) for i in ra...  17.4 us
    ppermute x8, starting transfers between devices, over_y(): lax.ppermute(block, 'row', [(i, i ^ 2 * mask_of(i % 2, turn)) for i in ra...  14.2 us
    dot_general x1, matrix products, local(): lax.dot_general(left, right, CONTRACT_FIRST, preferred_element_type=F32)  7.55 us
    ppermute x4, starting transfers between devices, over_z(): return lax.ppermute(block, ('row', 'col'), route)  5.5 us
    ppermute x4, waiting for transfers between devices, over_z(): return lax.ppermute(block, ('row', 'col'), route)  5.32 us
    dot_general x2, matrix products, local(): lax.dot_general(r, weight, CONTRACT_LAST, preferred_element_type=F32)  5.29 us
  transfers between devices with their start and end apart: 38, of which 22 were waited for; matrix products, arithmetic and copies ran while one was open for 18% of the time, Pallas kernels for 0%

profile of v5, /device:TPU:0, one launch (start us, length us, event | category | flops | bytes accessed | tf_op | source)
XLA Modules:
  0.0 130.6 jit_solution(16351375140058209499)
XLA Ops:
  0.7 1.1 slice_bitcast_fusion.2
  1.7 1.7 %collective-permute-start.2 = (bf16[1,64,512]{2,1,0:T(8,128)(2,1)S(1)}, bf16[1,64,512]{2,1,0:T(8,128)(2,1)S(1)}, u32[]{:S(2)}, u32[]{:S(2)}) collective-permute-start(bf16[1,64,512]{2,1,0:T(8,128)(2,1)S(1)} %get-tuple-element.141), channel_id=1, source_target_pairs={{0,4},{1,5},{2,6},{3,7},{4,0},{5,1},{6,2},{7,3},{8,12},{9,13},{10,... | collective-permute-start | bytes 196616 | tf_op jit(solution)/shard_map/ppermute | solution.py:17
  3.4 1.9 %collective-permute-start = (bf16[1,64,512]{2,1,0:T(8,128)(2,1)S(1)}, bf16[1,64,512]{2,1,0:T(8,128)(2,1)S(1)}, u32[]{:S(2)}, u32[]{:S(2)}) collective-permute-start(bf16[1,64,512]{2,1,0:T(8,128)(2,1)S(1)} %get-tuple-element.142), channel_id=1, source_target_pairs={{0,1},{1,0},{2,3},{3,2},{4,5},{5,4},{6,7},{7,6},{8,9},{9,8},{10,11... | collective-permute-start | bytes 196616 | tf_op jit(solution)/shard_map/ppermute | solution.py:17
  5.3 2.5 %collective-permute-start.1 = (bf16[1,64,512]{2,1,0:T(8,128)(2,1)S(1)}, bf16[1,64,512]{2,1,0:T(8,128)(2,1)S(1)}, u32[]{:S(2)}, u32[]{:S(2)}) collective-permute-start(bf16[1,64,512]{2,1,0:T(8,128)(2,1)S(1)} %get-tuple-element.143), channel_id=1, source_target_pairs={{0,3},{1,2},{2,1},{3,0},{4,7},{5,6},{6,5},{7,4},{8,11},{9,10},{10,... | collective-permute-start | bytes 196616 | tf_op jit(solution)/shard_map/ppermute | solution.py:17
  8.8 1.9 %collective-permute-done.1 = bf16[1,64,512]{2,1,0:T(8,128)(2,1)S(1)} collective-permute-done((bf16[1,64,512]{2,1,0:T(8,128)(2,1)S(1)}, bf16[1,64,512]{2,1,0:T(8,128)(2,1)S(1)}, u32[]{:S(2)}, u32[]{:S(2)}) %collective-permute-start.1) | collective-permute-done | bytes 65568 | tf_op jit(solution)/shard_map/ppermute | solution.py:17
  11.6 2.6 %collective-permute-start.3 = (bf16[2,64,512]{2,1,0:T(8,128)(2,1)S(1)}, bf16[2,64,512]{2,1,0:T(8,128)(2,1)S(1)}, u32[]{:S(2)}, u32[]{:S(2)}) collective-permute-start(bf16[2,64,512]{2,1,0:T(8,128)(2,1)S(1)} %pad_maximum_fusion.9), channel_id=1, source_target_pairs={{0,3},{1,2},{2,1},{3,0},{4,7},{5,6},{6,5},{7,4},{8,11},{9,10},{10,... | collective-permute-start | bytes 393224 | tf_op jit(solution)/shard_map/ppermute | solution.py:17
  14.7 0.9 fusion.62
  15.6 3.1 %collective-permute-done.3 = bf16[2,64,512]{2,1,0:T(8,128)(2,1)S(1)} collective-permute-done((bf16[2,64,512]{2,1,0:T(8,128)(2,1)S(1)}, bf16[2,64,512]{2,1,0:T(8,128)(2,1)S(1)}, u32[]{:S(2)}, u32[]{:S(2)}) %collective-permute-start.3) | collective-permute-done | bytes 131104 | tf_op jit(solution)/shard_map/ppermute | solution.py:17
  18.7 1.0 collective-permute-done.4
  20.0 1.7 %collective-permute-start.10 = (f32[1024]{0:T(1024)S(1)}, f32[1024]{0:T(1024)S(1)}, u32[]{:S(2)}, u32[]{:S(2)}) collective-permute-start(f32[1024]{0:T(1024)S(1)} %fusion.80), channel_id=1, source_target_pairs={{0,16},{8,24},{16,0},{24,8},{32,48},{40,56},{48,32},{56,40},{1,17}... | collective-permute-start | bytes 12296 | tf_op jit(solution)/shard_map/ppermute | solution.py:17
  21.6 1.5 %collective-permute-start.7 = (bf16[4,64,512]{2,1,0:T(8,128)(2,1)S(1)}, bf16[4,64,512]{2,1,0:T(8,128)(2,1)S(1)}, u32[]{:S(2)}, u32[]{:S(2)}) collective-permute-start(bf16[4,64,512]{2,1,0:T(8,128)(2,1)S(1)} %pad_maximum_fusion.6), channel_id=1, source_target_pairs={{0,4},{1,5},{2,6},{3,7},{4,0},{5,1},{6,2},{7,3},{8,12},{9,13},{10,... | collective-permute-start | bytes 786440 | tf_op jit(solution)/shard_map/ppermute | solution.py:17
  24.4 3.0 %collective-permute-start.11 = (f32[1024]{0:T(1024)S(1)}, f32[1024]{0:T(1024)S(1)}, u32[]{:S(2)}, u32[]{:S(2)}) collective-permute-start(f32[1024]{0:T(1024)S(1)} %add.627), channel_id=1, source_target_pairs={{0,32},{8,40},{16,48},{24,56},{32,0},{40,8},{48,16},{56,24},{1,33}... | collective-permute-start | bytes 12296 | tf_op jit(solution)/shard_map/ppermute | solution.py:17
  27.3 2.2 %collective-permute-done.11 = f32[1024]{0:T(1024)S(1)} collective-permute-done((f32[1024]{0:T(1024)S(1)}, f32[1024]{0:T(1024)S(1)}, u32[]{:S(2)}, u32[]{:S(2)}) %collective-permute-start.11) | collective-permute-done | bytes 4128 | tf_op jit(solution)/shard_map/ppermute | solution.py:17
  31.4 1.4 %broadcast_select_fusion.3 = (bf16[8,32,1536]{2,1,0:T(8,128)(2,1)S(1)}, bf16[8,32,1536]{2,1,0:T(8,128)(2,1)}, bf16[8,32,1536]{2,1,0:T(8,128)(2,1)}, bf16[8,32,1536]{2,1,0:T(8,128)(2,1)S(1)}) fusion(bf16[8,32,1536]{2,1,0:T(8,128)(2,1)S(1)} %bitcast.83, pred[]{:T(512)S(6)} %eq.227, bf16[8,64,1536]{2,1,0:T(8,128)(2,1)S(1)} %slice_dynamic-update-slice_fusion, ...), kind=kLoop, calls=%fused_computation.45 | loop fusion | flops 786432 | bytes 6291457 | tf_op jit(solution)/shard_map/jit(_where)/select_n | solution.py:114
  32.8 1.2 slice-done.2
  34.1 2.6 %fusion.8 = f32[256,3072]{1,0:T(8,128)S(1)} fusion(bf16[256,1536]{1,0:T(8,128)(2,1)S(1)} %bitcast.94, bf16[1,1536,3072]{2,1,0:T(8,128)(2,1)S(1)} %bitcast.74), kind=kOutput, calls=%fused_computation.9 | convolution fusion | flops 2415919104 | bytes 13369344 | tf_op jit(solution)/shard_map/dot_general | solution.py:115
  36.9 2.6 %fusion.6 = f32[256,3072]{1,0:T(8,128)S(1)} fusion(bf16[256,1536]{1,0:T(8,128)(2,1)S(1)} %bitcast.93, bf16[1,1536,3072]{2,1,0:T(8,128)(2,1)S(1)} %bitcast.74), kind=kOutput, calls=%fused_computation.7 | convolution fusion | flops 2415919104 | bytes 13369344 | tf_op jit(solution)/shard_map/dot_general | solution.py:115
  40.4 1.1 collective-permute-start.13
  42.3 1.3 %fusion.21 = f32[3072]{0:T(1024)S(1)} fusion(bf16[8,1536]{1,0:T(8,128)(2,1)S(1)} %maximum_maximum_fusion.2, bf16[1,1536,3072]{2,1,0:T(8,128)(2,1)S(1)} %bitcast.74), kind=kOutput, calls=%fused_computation.33 | convolution fusion | flops 75518976 | bytes 9474048 | tf_op jit(solution)/shard_map/dot_general | solution.py:127
  45.2 3.3 %collective-permute-done.13 = bf16[2,32,3072]{2,1,0:T(8,128)(2,1)S(1)} collective-permute-done((bf16[2,32,3072]{2,1,0:T(8,128)(2,1)S(1)}, bf16[2,32,3072]{2,1,0:T(8,128)(2,1)S(1)}, u32[]{:S(2)}, u32[]{:S(2)}) %collective-permute-start.13) | collective-permute-done | bytes 393248 | tf_op jit(solution)/shard_map/ppermute | solution.py:26
  49.4 2.3 %collective-permute-start.14 = (bf16[1,32,3072]{2,1,0:T(8,128)(2,1)}, bf16[1,32,3072]{2,1,0:T(8,128)(2,1)}, u32[]{:S(2)}, u32[]{:S(2)}) collective-permute-start(bf16[1,32,3072]{2,1,0:T(8,128)(2,1)} %slice.428), channel_id=1, source_target_pairs={{0,48},{8,24},{16,32},{24,8},{32,16},{40,56},{48,0},{56,40},{1,49}... | collective-permute-start | bytes 589832 | tf_op jit(solution)/shard_map/ppermute | solution.py:26
  51.6 1.4 %collective-permute-done.17 = bf16[2,32,3072]{2,1,0:T(8,128)(2,1)S(1)} collective-permute-done((bf16[2,32,3072]{2,1,0:T(8,128)(2,1)S(1)}, bf16[2,32,3072]{2,1,0:T(8,128)(2,1)S(1)}, u32[]{:S(2)}, u32[]{:S(2)}) %collective-permute-start.17) | collective-permute-done | bytes 393248 | tf_op jit(solution)/shard_map/ppermute | solution.py:26
  53.2 1.5 %collective-permute-start.20 = (f32[1,3072]{1,0:T(1,128)S(1)}, f32[1,3072]{1,0:T(1,128)S(1)}, u32[]{:S(2)}, u32[]{:S(2)}) collective-permute-start(f32[1,3072]{1,0:T(1,128)S(1)} %add.669), channel_id=1, source_target_pairs={{0,16},{8,24},{16,0},{24,8},{32,48},{40,56},{48,32},{56,40},{1,17}... | collective-permute-start | bytes 36872 | tf_op jit(solution)/shard_map/ppermute | solution.py:17
  54.6 3.0 %collective-permute-start.19 = (bf16[1,32,3072]{2,1,0:T(8,128)(2,1)S(1)}, bf16[1,32,3072]{2,1,0:T(8,128)(2,1)S(1)}, u32[]{:S(2)}, u32[]{:S(2)}) collective-permute-start(bf16[1,32,3072]{2,1,0:T(8,128)(2,1)S(1)} %slice.427), channel_id=1, source_target_pairs={{0,48},{8,24},{16,32},{24,8},{32,16},{40,56},{48,0},{56,40},{1,49}... | collective-permute-start | bytes 589832 | tf_op jit(solution)/shard_map/ppermute | solution.py:26
  57.7 1.3 fusion.49
  59.0 2.5 %collective-permute-start.15 = (bf16[32,3072]{1,0:T(8,128)(2,1)S(1)}, bf16[32,3072]{1,0:T(8,128)(2,1)S(1)}, u32[]{:S(2)}, u32[]{:S(2)}) collective-permute-start(bf16[32,3072]{1,0:T(8,128)(2,1)S(1)} %get-tuple-element.101), channel_id=1, source_target_pairs={{0,64},{64,0},{1,65},{65,1},{2,66},{66,2},{3,67},{67,3},{4,68},{68... | collective-permute-start | bytes 589832 | tf_op jit(solution)/shard_map/ppermute | solution.py:17
  61.9 3.2 %collective-permute-start.21 = (f32[1,3072]{1,0:T(1,128)S(1)}, f32[1,3072]{1,0:T(1,128)S(1)}, u32[]{:S(2)}, u32[]{:S(2)}) collective-permute-start(f32[1,3072]{1,0:T(1,128)S(1)} %add.674), channel_id=1, source_target_pairs={{0,32},{8,40},{16,48},{24,56},{32,0},{40,8},{48,16},{56,24},{1,33}... | collective-permute-start | bytes 36872 | tf_op jit(solution)/shard_map/ppermute | solution.py:17
  65.1 1.2 collective-permute-start.25
  67.7 3.1 %collective-permute-start.22 = (bf16[1,32,3200]{2,1,0:T(8,128)(2,1)S(1)}, bf16[1,32,3200]{2,1,0:T(8,128)(2,1)S(1)}, u32[]{:S(2)}, u32[]{:S(2)}) collective-permute-start(bf16[1,32,3200]{2,1,0:T(8,128)(2,1)S(1)} %fusion.57), channel_id=1, source_target_pairs={{0,48},{8,24},{16,32},{24,8},{32,16},{40,56},{48,0},{56,40},{1,49}... | collective-permute-start | bytes 614408 | tf_op jit(solution)/shard_map/ppermute | solution.py:26
  70.8 1.4 %collective-permute-done.25 = bf16[32,3072]{1,0:T(8,128)(2,1)S(1)} collective-permute-done((bf16[32,3072]{1,0:T(8,128)(2,1)S(1)}, bf16[32,3072]{1,0:T(8,128)(2,1)S(1)}, u32[]{:S(2)}, u32[]{:S(2)}) %collective-permute-start.25) | collective-permute-done | bytes 196640 | tf_op jit(solution)/shard_map/ppermute | solution.py:17
  72.9 1.3 collective-permute-start.26
  74.2 1.6 %collective-permute-done.22 = bf16[1,32,3200]{2,1,0:T(8,128)(2,1)S(1)} collective-permute-done((bf16[1,32,3200]{2,1,0:T(8,128)(2,1)S(1)}, bf16[1,32,3200]{2,1,0:T(8,128)(2,1)S(1)}, u32[]{:S(2)}, u32[]{:S(2)}) %collective-permute-start.22) | collective-permute-done | bytes 204832 | tf_op jit(solution)/shard_map/ppermute | solution.py:26
  75.8 2.5 %collective-permute-start.23 = (bf16[2,32,3200]{2,1,0:T(8,128)(2,1)S(1)}, bf16[2,32,3200]{2,1,0:T(8,128)(2,1)S(1)}, u32[]{:S(2)}, u32[]{:S(2)}) collective-permute-start(bf16[2,32,3200]{2,1,0:T(8,128)(2,1)S(1)} %pad_maximum_fusion.4), channel_id=1, source_target_pairs={{0,16},{8,56},{16,0},{24,40},{32,48},{40,24},{48,32},{56,8},{1,17}... | collective-permute-start | bytes 1228808 | tf_op jit(solution)/shard_map/ppermute | solution.py:26
  78.3 3.9 %collective-permute-done.26 = bf16[1,32,3200]{2,1,0:T(8,128)(2,1)S(1)} collective-permute-done((bf16[1,32,3200]{2,1,0:T(8,128)(2,1)S(1)}, bf16[1,32,3200]{2,1,0:T(8,128)(2,1)S(1)}, u32[]{:S(2)}, u32[]{:S(2)}) %collective-permute-start.26) | collective-permute-done | bytes 204832 | tf_op jit(solution)/shard_map/ppermute | solution.py:26
  82.7 1.5 %collective-permute-done.23 = bf16[2,32,3200]{2,1,0:T(8,128)(2,1)S(1)} collective-permute-done((bf16[2,32,3200]{2,1,0:T(8,128)(2,1)S(1)}, bf16[2,32,3200]{2,1,0:T(8,128)(2,1)S(1)}, u32[]{:S(2)}, u32[]{:S(2)}) %collective-permute-start.23) | collective-permute-done | bytes 409632 | tf_op jit(solution)/shard_map/ppermute | solution.py:26
  84.7 5.6 %collective-permute-done.27 = bf16[2,32,3200]{2,1,0:T(8,128)(2,1)S(1)} collective-permute-done((bf16[2,32,3200]{2,1,0:T(8,128)(2,1)S(1)}, bf16[2,32,3200]{2,1,0:T(8,128)(2,1)S(1)}, u32[]{:S(2)}, u32[]{:S(2)}) %collective-permute-start.27) | collective-permute-done | bytes 409632 | tf_op jit(solution)/shard_map/ppermute | solution.py:26
  91.9 2.6 %fusion.2 = f32[256,1536]{1,0:T(8,128)S(1)} fusion(bf16[1,1536,3072]{2,1,0:T(8,128)(2,1)S(1)} %bitcast.76, bf16[128,3072]{1,0:T(8,128)(2,1)S(1)} %slice.312, bf16[128,3072]{1,0:T(8,128)(2,1)S(1)} %slice.311), kind=kOutput, calls=%fused_computation.3 | convolution fusion | flops 2419064832 | bytes 12582912 | tf_op jit(solution)/shard_map/dot_general | solution.py:178
  94.7 2.6 %fusion = f32[256,1536]{1,0:T(8,128)S(1)} fusion(bf16[1,1536,3072]{2,1,0:T(8,128)(2,1)S(1)} %bitcast.76, bf16[128,3072]{1,0:T(8,128)(2,1)S(1)} %slice.316, bf16[128,3072]{1,0:T(8,128)(2,1)S(1)} %slice.315), kind=kOutput, calls=%fused_computation.1 | convolution fusion | flops 2419064832 | bytes 12582912 | tf_op jit(solution)/shard_map/dot_general | solution.py:178
  98.4 1.6 %collective-permute-start.29 = (f32[1536]{0:T(1024)S(1)}, f32[1536]{0:T(1024)S(1)}, u32[]{:S(2)}, u32[]{:S(2)}) collective-permute-start(f32[1536]{0:T(1024)S(1)} %div.314), channel_id=1, source_target_pairs={{0,1},{1,0},{2,3},{3,2},{4,5},{5,4},{6,7},{7,6},{8,9},{9,8},{10,11... | collective-permute-start | bytes 18440 | tf_op jit(solution)/shard_map/ppermute | solution.py:17
  100.8 1.5 %collective-permute-start.31 = (bf16[4,32,1664]{2,1,0:T(8,128)(2,1)S(1)}, bf16[4,32,1664]{2,1,0:T(8,128)(2,1)S(1)}, u32[]{:S(2)}, u32[]{:S(2)}) collective-permute-start(bf16[4,32,1664]{2,1,0:T(8,128)(2,1)S(1)} %maximum_maximum_fusion), channel_id=1, source_target_pairs={{0,1},{1,0},{2,3},{3,2},{4,5},{5,4},{6,7},{7,6},{8,11},{9,10},{10,... | collective-permute-start | bytes 1277960 | tf_op jit(solution)/shard_map/ppermute | solution.py:36
  102.3 3.3 %collective-permute-start.36 = (f32[1536]{0:T(1024)S(1)}, f32[1536]{0:T(1024)S(1)}, u32[]{:S(2)}, u32[]{:S(2)}) collective-permute-start(f32[1536]{0:T(1024)S(1)} %add.697), channel_id=1, source_target_pairs={{0,2},{1,3},{2,0},{3,1},{4,6},{5,7},{6,4},{7,5},{8,10},{9,11},{10,... | collective-permute-start | bytes 18440 | tf_op jit(solution)/shard_map/ppermute | solution.py:17
  105.6 7.5 %convolution_convert_fusion = bf16[1536,3072]{1,0:T(8,128)(2,1)} fusion(bf16[512,1536]{1,0:T(8,128)(2,1)S(1)} %pad_maximum_fusion.1, bf16[512,3072]{1,0:T(8,128)(2,1)S(1)} %pad_maximum_fusion), kind=kOutput, calls=%fused_computation | convolution fusion | flops 4836556800 | bytes 14155776 | tf_op jit(solution)/shard_map/dot_general | solution.py:207
  113.2 1.9 %collective-permute-done.36 = f32[1536]{0:T(1024)S(1)} collective-permute-done((f32[1536]{0:T(1024)S(1)}, f32[1536]{0:T(1024)S(1)}, u32[]{:S(2)}, u32[]{:S(2)}) %collective-permute-start.36) | collective-permute-done | bytes 6176 | tf_op jit(solution)/shard_map/ppermute | solution.py:17
  116.3 2.5 %collective-permute-start.32 = (bf16[2,32,1664]{2,1,0:T(8,128)(2,1)S(1)}, bf16[2,32,1664]{2,1,0:T(8,128)(2,1)S(1)}, u32[]{:S(2)}, u32[]{:S(2)}) collective-permute-start(bf16[2,32,1664]{2,1,0:T(8,128)(2,1)S(1)} %slice.426), channel_id=1, source_target_pairs={{0,3},{1,2},{2,1},{3,0},{4,7},{5,6},{6,5},{7,4},{8,9},{9,8},{10,11... | collective-permute-start | bytes 638984 | tf_op jit(solution)/shard_map/ppermute | solution.py:36
  119.0 3.4 %collective-permute-done.34 = bf16[2,32,1664]{2,1,0:T(8,128)(2,1)S(1)} collective-permute-done((bf16[2,32,1664]{2,1,0:T(8,128)(2,1)S(1)}, bf16[2,32,1664]{2,1,0:T(8,128)(2,1)S(1)}, u32[]{:S(2)}, u32[]{:S(2)}) %collective-permute-start.34) | collective-permute-done | bytes 213024 | tf_op jit(solution)/shard_map/ppermute | solution.py:36
  122.8 1.9 %collective-permute-done.32 = bf16[2,32,1664]{2,1,0:T(8,128)(2,1)S(1)} collective-permute-done((bf16[2,32,1664]{2,1,0:T(8,128)(2,1)S(1)}, bf16[2,32,1664]{2,1,0:T(8,128)(2,1)S(1)}, u32[]{:S(2)}, u32[]{:S(2)}) %collective-permute-start.32) | collective-permute-done | bytes 213024 | tf_op jit(solution)/shard_map/ppermute | solution.py:36
  125.1 2.2 %collective-permute-done.35 = bf16[32,1664]{1,0:T(8,128)(2,1)S(1)} collective-permute-done((bf16[32,1664]{1,0:T(8,128)(2,1)S(1)}, bf16[32,1664]{1,0:T(8,128)(2,1)S(1)}, u32[]{:S(2)}, u32[]{:S(2)}) %collective-permute-start.35) | collective-permute-done | bytes 106528 | tf_op jit(solution)/shard_map/ppermute | solution.py:17
  127.9 1.6 %collective-permute-done.33 = bf16[32,1664]{1,0:T(8,128)(2,1)S(1)} collective-permute-done((bf16[32,1664]{1,0:T(8,128)(2,1)S(1)}, bf16[32,1664]{1,0:T(8,128)(2,1)S(1)}, u32[]{:S(2)}, u32[]{:S(2)}) %collective-permute-start.33) | collective-permute-done | bytes 106528 | tf_op jit(solution)/shard_map/ppermute | solution.py:17
  (198 shorter events, 20.2 us)
Async XLA Ops:
  0.6 10.2 %copy-start = (bf16[512,1536]{1,0:T(8,128)(2,1)S(1)}, bf16[512,1536]{1,0:T(8,128)(2,1)}, u32[]{:S(2)}) copy-start(bf16[512,1536]{1,0:T(8,128)(2,1)} %param.4) | copy-start | bytes 4718596
  0.6 32.2 %slice-start = ((s8[9437184]{0:T(1024)(128)(4,1)}), s8[1048576]{0:T(1024)(128)(4,1)S(1)}, s32[]{:S(2)}) async-start(s8[9437184]{0:T(1024)(128)(4,1)} %bitcast.73), calls=%async_computation | async-start | bytes 2097152
  1.7 7.0 %collective-permute-start.2 = (bf16[1,64,512]{2,1,0:T(8,128)(2,1)S(1)}, bf16[1,64,512]{2,1,0:T(8,128)(2,1)S(1)}, u32[]{:S(2)}, u32[]{:S(2)}) collective-permute-start(bf16[1,64,512]{2,1,0:T(8,128)(2,1)S(1)} %get-tuple-element.141), channel_id=1, source_target_pairs={{0,4},{1,5},{2,6},{3,7},{4,0},{5,1},{6,2},{7,3},{8,12},{9,13},{10,... | collective-permute-start | bytes 196616 | tf_op jit(solution)/shard_map/ppermute | solution.py:17
  3.4 5.4 %collective-permute-start = (bf16[1,64,512]{2,1,0:T(8,128)(2,1)S(1)}, bf16[1,64,512]{2,1,0:T(8,128)(2,1)S(1)}, u32[]{:S(2)}, u32[]{:S(2)}) collective-permute-start(bf16[1,64,512]{2,1,0:T(8,128)(2,1)S(1)} %get-tuple-element.142), channel_id=1, source_target_pairs={{0,1},{1,0},{2,3},{3,2},{4,5},{5,4},{6,7},{7,6},{8,9},{9,8},{10,11... | collective-permute-start | bytes 196616 | tf_op jit(solution)/shard_map/ppermute | solution.py:17
  5.3 5.5 %collective-permute-start.1 = (bf16[1,64,512]{2,1,0:T(8,128)(2,1)S(1)}, bf16[1,64,512]{2,1,0:T(8,128)(2,1)S(1)}, u32[]{:S(2)}, u32[]{:S(2)}) collective-permute-start(bf16[1,64,512]{2,1,0:T(8,128)(2,1)S(1)} %get-tuple-element.143), channel_id=1, source_target_pairs={{0,3},{1,2},{2,1},{3,0},{4,7},{5,6},{6,5},{7,4},{8,11},{9,10},{10,... | collective-permute-start | bytes 196616 | tf_op jit(solution)/shard_map/ppermute | solution.py:17
  11.5 4.1 %collective-permute-start.6 = (f32[1024]{0:T(1024)S(1)}, f32[1024]{0:T(1024)S(1)}, u32[]{:S(2)}, u32[]{:S(2)}) collective-permute-start(f32[1024]{0:T(1024)S(1)} %pad_maximum_fusion.15), channel_id=1, source_target_pairs={{0,8},{8,0},{16,24},{24,16},{32,40},{40,32},{48,56},{56,48},{1,9},... | collective-permute-start | bytes 12296 | tf_op jit(solution)/shard_map/ppermute | solution.py:17
  11.6 7.1 %collective-permute-start.3 = (bf16[2,64,512]{2,1,0:T(8,128)(2,1)S(1)}, bf16[2,64,512]{2,1,0:T(8,128)(2,1)S(1)}, u32[]{:S(2)}, u32[]{:S(2)}) collective-permute-start(bf16[2,64,512]{2,1,0:T(8,128)(2,1)S(1)} %pad_maximum_fusion.9), channel_id=1, source_target_pairs={{0,3},{1,2},{2,1},{3,0},{4,7},{5,6},{6,5},{7,4},{8,11},{9,10},{10,... | collective-permute-start | bytes 393224 | tf_op jit(solution)/shard_map/ppermute | solution.py:17
  14.2 5.6 %collective-permute-start.4 = (bf16[2,64,512]{2,1,0:T(8,128)(2,1)S(1)}, bf16[2,64,512]{2,1,0:T(8,128)(2,1)S(1)}, u32[]{:S(2)}, u32[]{:S(2)}) collective-permute-start(bf16[2,64,512]{2,1,0:T(8,128)(2,1)S(1)} %pad_maximum_fusion.10), channel_id=1, source_target_pairs={{0,4},{1,5},{2,6},{3,7},{4,0},{5,1},{6,2},{7,3},{8,12},{9,13},{10,... | collective-permute-start | bytes 393224 | tf_op jit(solution)/shard_map/ppermute | solution.py:17
  14.7 5.3 %collective-permute-start.5 = (bf16[2,64,512]{2,1,0:T(8,128)(2,1)S(1)}, bf16[2,64,512]{2,1,0:T(8,128)(2,1)S(1)}, u32[]{:S(2)}, u32[]{:S(2)}) collective-permute-start(bf16[2,64,512]{2,1,0:T(8,128)(2,1)S(1)} %pad_maximum_fusion.11), channel_id=1, source_target_pairs={{0,1},{1,0},{2,3},{3,2},{4,5},{5,4},{6,7},{7,6},{8,9},{9,8},{10,11... | collective-permute-start | bytes 393224 | tf_op jit(solution)/shard_map/ppermute | solution.py:17
  20.0 4.3 %collective-permute-start.10 = (f32[1024]{0:T(1024)S(1)}, f32[1024]{0:T(1024)S(1)}, u32[]{:S(2)}, u32[]{:S(2)}) collective-permute-start(f32[1024]{0:T(1024)S(1)} %fusion.80), channel_id=1, source_target_pairs={{0,16},{8,24},{16,0},{24,8},{32,48},{40,56},{48,32},{56,40},{1,17}... | collective-permute-start | bytes 12296 | tf_op jit(solution)/shard_map/ppermute | solution.py:17
  21.6 8.7 %collective-permute-start.7 = (bf16[4,64,512]{2,1,0:T(8,128)(2,1)S(1)}, bf16[4,64,512]{2,1,0:T(8,128)(2,1)S(1)}, u32[]{:S(2)}, u32[]{:S(2)}) collective-permute-start(bf16[4,64,512]{2,1,0:T(8,128)(2,1)S(1)} %pad_maximum_fusion.6), channel_id=1, source_target_pairs={{0,4},{1,5},{2,6},{3,7},{4,0},{5,1},{6,2},{7,3},{8,12},{9,13},{10,... | collective-permute-start | bytes 786440 | tf_op jit(solution)/shard_map/ppermute | solution.py:17
  23.1 7.4 %collective-permute-start.8 = (bf16[4,64,512]{2,1,0:T(8,128)(2,1)S(1)}, bf16[4,64,512]{2,1,0:T(8,128)(2,1)S(1)}, u32[]{:S(2)}, u32[]{:S(2)}) collective-permute-start(bf16[4,64,512]{2,1,0:T(8,128)(2,1)S(1)} %pad_maximum_fusion.7), channel_id=1, source_target_pairs={{0,1},{1,0},{2,3},{3,2},{4,5},{5,4},{6,7},{7,6},{8,9},{9,8},{10,11... | collective-permute-start | bytes 786440 | tf_op jit(solution)/shard_map/ppermute | solution.py:17
  23.4 7.9 %collective-permute-start.9 = (bf16[4,64,512]{2,1,0:T(8,128)(2,1)S(1)}, bf16[4,64,512]{2,1,0:T(8,128)(2,1)S(1)}, u32[]{:S(2)}, u32[]{:S(2)}) collective-permute-start(bf16[4,64,512]{2,1,0:T(8,128)(2,1)S(1)} %pad_maximum_fusion.8), channel_id=1, source_target_pairs={{0,3},{1,2},{2,1},{3,0},{4,7},{5,6},{6,5},{7,4},{8,11},{9,10},{10,... | collective-permute-start | bytes 786440 | tf_op jit(solution)/shard_map/ppermute | solution.py:17
  24.4 5.2 %collective-permute-start.11 = (f32[1024]{0:T(1024)S(1)}, f32[1024]{0:T(1024)S(1)}, u32[]{:S(2)}, u32[]{:S(2)}) collective-permute-start(f32[1024]{0:T(1024)S(1)} %add.627), channel_id=1, source_target_pairs={{0,32},{8,40},{16,48},{24,56},{32,0},{40,8},{48,16},{56,24},{1,33}... | collective-permute-start | bytes 12296 | tf_op jit(solution)/shard_map/ppermute | solution.py:17
  36.8 3.5 %collective-permute-start.12 = (bf16[128,3072]{1,0:T(8,128)(2,1)S(1)}, bf16[128,3072]{1,0:T(8,128)(2,1)S(1)}, u32[]{:S(2)}, u32[]{:S(2)}) collective-permute-start(bf16[128,3072]{1,0:T(8,128)(2,1)S(1)} %slice.422), channel_id=1, source_target_pairs={{0,8},{8,0},{16,24},{24,16},{32,40},{40,32},{48,56},{56,48},{1,9},... | collective-permute-start | bytes 2359304 | tf_op jit(solution)/shard_map/ppermute | solution.py:17
  39.6 2.5 %collective-permute-start.16 = (bf16[128,3072]{1,0:T(8,128)(2,1)S(1)}, bf16[128,3072]{1,0:T(8,128)(2,1)S(1)}, u32[]{:S(2)}, u32[]{:S(2)}) collective-permute-start(bf16[128,3072]{1,0:T(8,128)(2,1)S(1)} %slice.421), channel_id=1, source_target_pairs={{0,8},{8,0},{16,24},{24,16},{32,40},{40,32},{48,56},{56,48},{1,9},... | collective-permute-start | bytes 2359304 | tf_op jit(solution)/shard_map/ppermute | solution.py:17
  40.4 8.0 %collective-permute-start.13 = (bf16[2,32,3072]{2,1,0:T(8,128)(2,1)S(1)}, bf16[2,32,3072]{2,1,0:T(8,128)(2,1)S(1)}, u32[]{:S(2)}, u32[]{:S(2)}) collective-permute-start(bf16[2,32,3072]{2,1,0:T(8,128)(2,1)S(1)} %bitcast.95), channel_id=1, source_target_pairs={{0,16},{8,56},{16,0},{24,40},{32,48},{40,24},{48,32},{56,8},{1,17}... | collective-permute-start | bytes 1179656 | tf_op jit(solution)/shard_map/ppermute | solution.py:26
  43.6 1.6 %collective-permute-start.18 = (f32[1,3072]{1,0:T(1,128)S(1)}, f32[1,3072]{1,0:T(1,128)S(1)}, u32[]{:S(2)}, u32[]{:S(2)}) collective-permute-start(f32[1,3072]{1,0:T(1,128)S(1)} %add.668), channel_id=1, source_target_pairs={{0,8},{8,0},{16,24},{24,16},{32,40},{40,32},{48,56},{56,48},{1,9},... | collective-permute-start | bytes 36872 | tf_op jit(solution)/shard_map/ppermute | solution.py:17
  44.4 4.1 %slice-start.6 = ((f32[128,3072]{1,0:T(8,128)}), f32[64,3072]{1,0:T(8,128)S(1)}, s32[]{:S(2)}) async-start(f32[128,3072]{1,0:T(8,128)} %copy-done.1), calls=%async_computation.6 | async-start | bytes 1572864 | tf_op jit(solution)/shard_map/slice | solution.py:131
  44.4 8.7 %slice-start.7 = ((f32[128,3072]{1,0:T(8,128)}), f32[64,3072]{1,0:T(8,128)S(1)}, s32[]{:S(2)}) async-start(f32[128,3072]{1,0:T(8,128)} %copy-done.2), calls=%async_computation.7 | async-start | bytes 1572864 | tf_op jit(solution)/shard_map/slice | solution.py:131
  44.4 8.7 %collective-permute-start.17 = (bf16[2,32,3072]{2,1,0:T(8,128)(2,1)S(1)}, bf16[2,32,3072]{2,1,0:T(8,128)(2,1)S(1)}, u32[]{:S(2)}, u32[]{:S(2)}) collective-permute-start(bf16[2,32,3072]{2,1,0:T(8,128)(2,1)S(1)} %bitcast.96), channel_id=1, source_target_pairs={{0,16},{8,56},{16,0},{24,40},{32,48},{40,24},{48,32},{56,8},{1,17}... | collective-permute-start | bytes 1179656 | tf_op jit(solution)/shard_map/ppermute | solution.py:26
  48.6 4.6 %copy-start.7 = (f32[2,32,3072]{2,1,0:T(8,128)}, f32[2,32,3072]{2,1,0:T(8,128)S(1)}, u32[]{:S(2)}) copy-start(f32[2,32,3072]{2,1,0:T(8,128)S(1)} %convert_add_fusion.1) | copy-start | bytes 2359300
  49.4 8.3 %collective-permute-start.14 = (bf16[1,32,3072]{2,1,0:T(8,128)(2,1)}, bf16[1,32,3072]{2,1,0:T(8,128)(2,1)}, u32[]{:S(2)}, u32[]{:S(2)}) collective-permute-start(bf16[1,32,3072]{2,1,0:T(8,128)(2,1)} %slice.428), channel_id=1, source_target_pairs={{0,48},{8,24},{16,32},{24,8},{32,16},{40,56},{48,0},{56,40},{1,49}... | collective-permute-start | bytes 589832 | tf_op jit(solution)/shard_map/ppermute | solution.py:26
  53.2 4.5 %collective-permute-start.20 = (f32[1,3072]{1,0:T(1,128)S(1)}, f32[1,3072]{1,0:T(1,128)S(1)}, u32[]{:S(2)}, u32[]{:S(2)}) collective-permute-start(f32[1,3072]{1,0:T(1,128)S(1)} %add.669), channel_id=1, source_target_pairs={{0,16},{8,24},{16,0},{24,8},{32,48},{40,56},{48,32},{56,40},{1,17}... | collective-permute-start | bytes 36872 | tf_op jit(solution)/shard_map/ppermute | solution.py:17
  54.6 6.9 %collective-permute-start.19 = (bf16[1,32,3072]{2,1,0:T(8,128)(2,1)S(1)}, bf16[1,32,3072]{2,1,0:T(8,128)(2,1)S(1)}, u32[]{:S(2)}, u32[]{:S(2)}) collective-permute-start(bf16[1,32,3072]{2,1,0:T(8,128)(2,1)S(1)} %slice.427), channel_id=1, source_target_pairs={{0,48},{8,24},{16,32},{24,8},{32,16},{40,56},{48,0},{56,40},{1,49}... | collective-permute-start | bytes 589832 | tf_op jit(solution)/shard_map/ppermute | solution.py:26
  59.0 8.1 %collective-permute-start.15 = (bf16[32,3072]{1,0:T(8,128)(2,1)S(1)}, bf16[32,3072]{1,0:T(8,128)(2,1)S(1)}, u32[]{:S(2)}, u32[]{:S(2)}) collective-permute-start(bf16[32,3072]{1,0:T(8,128)(2,1)S(1)} %get-tuple-element.101), channel_id=1, source_target_pairs={{0,64},{64,0},{1,65},{65,1},{2,66},{66,2},{3,67},{67,3},{4,68},{68... | collective-permute-start | bytes 589832 | tf_op jit(solution)/shard_map/ppermute | solution.py:17
  61.5 29.6 %slice-start.3 = ((s8[9437184]{0:T(1024)(128)(4,1)}), s8[4194304]{0:T(1024)(128)(4,1)S(1)}, s32[]{:S(2)}) async-start(s8[9437184]{0:T(1024)(128)(4,1)} %bitcast.75), calls=%async_computation.3 | async-start | bytes 8388608
  61.9 5.2 %collective-permute-start.21 = (f32[1,3072]{1,0:T(1,128)S(1)}, f32[1,3072]{1,0:T(1,128)S(1)}, u32[]{:S(2)}, u32[]{:S(2)}) collective-permute-start(f32[1,3072]{1,0:T(1,128)S(1)} %add.674), channel_id=1, source_target_pairs={{0,32},{8,40},{16,48},{24,56},{32,0},{40,8},{48,16},{56,24},{1,33}... | collective-permute-start | bytes 36872 | tf_op jit(solution)/shard_map/ppermute | solution.py:17
  65.1 7.2 %collective-permute-start.25 = (bf16[32,3072]{1,0:T(8,128)(2,1)S(1)}, bf16[32,3072]{1,0:T(8,128)(2,1)S(1)}, u32[]{:S(2)}, u32[]{:S(2)}) collective-permute-start(bf16[32,3072]{1,0:T(8,128)(2,1)S(1)} %get-tuple-element.64), channel_id=1, source_target_pairs={{0,64},{64,0},{1,65},{65,1},{2,66},{66,2},{3,67},{67,3},{4,68},{68... | collective-permute-start | bytes 589832 | tf_op jit(solution)/shard_map/ppermute | solution.py:17
  67.7 8.0 %collective-permute-start.22 = (bf16[1,32,3200]{2,1,0:T(8,128)(2,1)S(1)}, bf16[1,32,3200]{2,1,0:T(8,128)(2,1)S(1)}, u32[]{:S(2)}, u32[]{:S(2)}) collective-permute-start(bf16[1,32,3200]{2,1,0:T(8,128)(2,1)S(1)} %fusion.57), channel_id=1, source_target_pairs={{0,48},{8,24},{16,32},{24,8},{32,16},{40,56},{48,0},{56,40},{1,49}... | collective-permute-start | bytes 614408 | tf_op jit(solution)/shard_map/ppermute | solution.py:26
  72.9 11.6 %copy-start.4 = (bf16[256,1536]{1,0:T(8,128)(2,1)S(1)}, bf16[256,1536]{1,0:T(8,128)(2,1)}, u32[]{:S(2)}) copy-start(bf16[256,1536]{1,0:T(8,128)(2,1)} %copy-done.3) | copy-start | bytes 2359300
  72.9 11.6 %copy-start.5 = (bf16[8,32,1536]{2,1,0:T(8,128)(2,1)S(1)}, bf16[8,32,1536]{2,1,0:T(8,128)(2,1)}, u32[]{:S(2)}) copy-start(bf16[8,32,1536]{2,1,0:T(8,128)(2,1)} %get-tuple-element.122) | copy-start | bytes 2359300
  72.9 11.6 %copy-start.6 = (bf16[8,32,1536]{2,1,0:T(8,128)(2,1)S(1)}, bf16[8,32,1536]{2,1,0:T(8,128)(2,1)}, u32[]{:S(2)}) copy-start(bf16[8,32,1536]{2,1,0:T(8,128)(2,1)} %get-tuple-element.123) | copy-start | bytes 2359300
  72.9 9.3 %collective-permute-start.26 = (bf16[1,32,3200]{2,1,0:T(8,128)(2,1)S(1)}, bf16[1,32,3200]{2,1,0:T(8,128)(2,1)S(1)}, u32[]{:S(2)}, u32[]{:S(2)}) collective-permute-start(bf16[1,32,3200]{2,1,0:T(8,128)(2,1)S(1)} %fusion.58), channel_id=1, source_target_pairs={{0,48},{8,24},{16,32},{24,8},{32,16},{40,56},{48,0},{56,40},{1,49}... | collective-permute-start | bytes 614408 | tf_op jit(solution)/shard_map/ppermute | solution.py:26
  75.8 8.4 %collective-permute-start.23 = (bf16[2,32,3200]{2,1,0:T(8,128)(2,1)S(1)}, bf16[2,32,3200]{2,1,0:T(8,128)(2,1)S(1)}, u32[]{:S(2)}, u32[]{:S(2)}) collective-permute-start(bf16[2,32,3200]{2,1,0:T(8,128)(2,1)S(1)} %pad_maximum_fusion.4), channel_id=1, source_target_pairs={{0,16},{8,56},{16,0},{24,40},{32,48},{40,24},{48,32},{56,8},{1,17}... | collective-permute-start | bytes 1228808 | tf_op jit(solution)/shard_map/ppermute | solution.py:26
  82.3 8.9 %slice-start.4 = ((s8[9437184]{0:T(1024)(128)(4,1)}), s8[4194304]{0:T(1024)(128)(4,1)S(1)}, s32[]{:S(2)}) async-start(s8[9437184]{0:T(1024)(128)(4,1)} %bitcast.75), calls=%async_computation.4 | async-start | bytes 8388608
  82.3 8.0 %collective-permute-start.27 = (bf16[2,32,3200]{2,1,0:T(8,128)(2,1)S(1)}, bf16[2,32,3200]{2,1,0:T(8,128)(2,1)S(1)}, u32[]{:S(2)}, u32[]{:S(2)}) collective-permute-start(bf16[2,32,3200]{2,1,0:T(8,128)(2,1)S(1)} %pad_maximum_fusion.5), channel_id=1, source_target_pairs={{0,16},{8,56},{16,0},{24,40},{32,48},{40,24},{48,32},{56,8},{1,17}... | collective-permute-start | bytes 1228808 | tf_op jit(solution)/shard_map/ppermute | solution.py:26
  84.3 6.7 %collective-permute-start.24 = (bf16[128,3200]{1,0:T(8,128)(2,1)S(1)}, bf16[128,3200]{1,0:T(8,128)(2,1)S(1)}, u32[]{:S(2)}, u32[]{:S(2)}) collective-permute-start(bf16[128,3200]{1,0:T(8,128)(2,1)S(1)} %bitcast.85), channel_id=1, source_target_pairs={{0,8},{8,0},{16,24},{24,16},{32,40},{40,32},{48,56},{56,48},{1,9},... | collective-permute-start | bytes 2457608 | tf_op jit(solution)/shard_map/ppermute | solution.py:17
  90.4 4.2 %collective-permute-start.28 = (bf16[128,3200]{1,0:T(8,128)(2,1)S(1)}, bf16[128,3200]{1,0:T(8,128)(2,1)S(1)}, u32[]{:S(2)}, u32[]{:S(2)}) collective-permute-start(bf16[128,3200]{1,0:T(8,128)(2,1)S(1)} %bitcast.88), channel_id=1, source_target_pairs={{0,8},{8,0},{16,24},{24,16},{32,40},{40,32},{48,56},{56,48},{1,9},... | collective-permute-start | bytes 2457608 | tf_op jit(solution)/shard_map/ppermute | solution.py:17
  98.4 3.9 %collective-permute-start.29 = (f32[1536]{0:T(1024)S(1)}, f32[1536]{0:T(1024)S(1)}, u32[]{:S(2)}, u32[]{:S(2)}) collective-permute-start(f32[1536]{0:T(1024)S(1)} %div.314), channel_id=1, source_target_pairs={{0,1},{1,0},{2,3},{3,2},{4,5},{5,4},{6,7},{7,6},{8,9},{9,8},{10,11... | collective-permute-start | bytes 18440 | tf_op jit(solution)/shard_map/ppermute | solution.py:17
  100.2 14.9 %collective-permute-start.30 = (bf16[4,32,1664]{2,1,0:T(8,128)(2,1)S(1)}, bf16[4,32,1664]{2,1,0:T(8,128)(2,1)S(1)}, u32[]{:S(2)}, u32[]{:S(2)}) collective-permute-start(bf16[4,32,1664]{2,1,0:T(8,128)(2,1)S(1)} %maximum_maximum_fusion.1), channel_id=1, source_target_pairs={{0,1},{1,0},{2,3},{3,2},{4,5},{5,4},{6,7},{7,6},{8,11},{9,10},{10,... | collective-permute-start | bytes 1277960 | tf_op jit(solution)/shard_map/ppermute | solution.py:36
  100.8 14.3 %collective-permute-start.31 = (bf16[4,32,1664]{2,1,0:T(8,128)(2,1)S(1)}, bf16[4,32,1664]{2,1,0:T(8,128)(2,1)S(1)}, u32[]{:S(2)}, u32[]{:S(2)}) collective-permute-start(bf16[4,32,1664]{2,1,0:T(8,128)(2,1)S(1)} %maximum_maximum_fusion), channel_id=1, source_target_pairs={{0,1},{1,0},{2,3},{3,2},{4,5},{5,4},{6,7},{7,6},{8,11},{9,10},{10,... | collective-permute-start | bytes 1277960 | tf_op jit(solution)/shard_map/ppermute | solution.py:36
  102.3 12.8 %collective-permute-start.36 = (f32[1536]{0:T(1024)S(1)}, f32[1536]{0:T(1024)S(1)}, u32[]{:S(2)}, u32[]{:S(2)}) collective-permute-start(f32[1536]{0:T(1024)S(1)} %add.697), channel_id=1, source_target_pairs={{0,2},{1,3},{2,0},{3,1},{4,6},{5,7},{6,4},{7,5},{8,10},{9,11},{10,... | collective-permute-start | bytes 18440 | tf_op jit(solution)/shard_map/ppermute | solution.py:17
  115.3 7.1 %collective-permute-start.34 = (bf16[2,32,1664]{2,1,0:T(8,128)(2,1)S(1)}, bf16[2,32,1664]{2,1,0:T(8,128)(2,1)S(1)}, u32[]{:S(2)}, u32[]{:S(2)}) collective-permute-start(bf16[2,32,1664]{2,1,0:T(8,128)(2,1)S(1)} %slice.425), channel_id=1, source_target_pairs={{0,3},{1,2},{2,1},{3,0},{4,7},{5,6},{6,5},{7,4},{8,9},{9,8},{10,11... | collective-permute-start | bytes 638984 | tf_op jit(solution)/shard_map/ppermute | solution.py:36
  116.3 8.4 %collective-permute-start.32 = (bf16[2,32,1664]{2,1,0:T(8,128)(2,1)S(1)}, bf16[2,32,1664]{2,1,0:T(8,128)(2,1)S(1)}, u32[]{:S(2)}, u32[]{:S(2)}) collective-permute-start(bf16[2,32,1664]{2,1,0:T(8,128)(2,1)S(1)} %slice.426), channel_id=1, source_target_pairs={{0,3},{1,2},{2,1},{3,0},{4,7},{5,6},{6,5},{7,4},{8,9},{9,8},{10,11... | collective-permute-start | bytes 638984 | tf_op jit(solution)/shard_map/ppermute | solution.py:36
  118.8 6.3 %collective-permute-start.37 = (f32[1536]{0:T(1024)S(1)}, f32[1536]{0:T(1024)S(1)}, u32[]{:S(2)}, u32[]{:S(2)}) collective-permute-start(f32[1536]{0:T(1024)S(1)} %add.703), channel_id=1, source_target_pairs={{0,4},{1,5},{2,6},{3,7},{4,0},{5,1},{6,2},{7,3},{8,12},{9,13},{10,... | collective-permute-start | bytes 18440 | tf_op jit(solution)/shard_map/ppermute | solution.py:17
  122.5 4.8 %collective-permute-start.35 = (bf16[32,1664]{1,0:T(8,128)(2,1)S(1)}, bf16[32,1664]{1,0:T(8,128)(2,1)S(1)}, u32[]{:S(2)}, u32[]{:S(2)}) collective-permute-start(bf16[32,1664]{1,0:T(8,128)(2,1)S(1)} %fusion.61), channel_id=1, source_target_pairs={{0,4},{1,5},{2,6},{3,7},{4,0},{5,1},{6,2},{7,3},{8,12},{9,13},{10,... | collective-permute-start | bytes 319496 | tf_op jit(solution)/shard_map/ppermute | solution.py:17
  124.7 4.8 %collective-permute-start.33 = (bf16[32,1664]{1,0:T(8,128)(2,1)S(1)}, bf16[32,1664]{1,0:T(8,128)(2,1)S(1)}, u32[]{:S(2)}, u32[]{:S(2)}) collective-permute-start(bf16[32,1664]{1,0:T(8,128)(2,1)S(1)} %fusion.60), channel_id=1, source_target_pairs={{0,4},{1,5},{2,6},{3,7},{4,0},{5,1},{6,2},{7,3},{8,12},{9,13},{10,... | collective-permute-start | bytes 319496 | tf_op jit(solution)/shard_map/ppermute | solution.py:17
  (6 other events, 16.6 us)

commit v6 on v5

--- a/solution.py
+++ b/solution.py
@@ -122,7 +122,7 @@
     high = later.astype(BF16)
     low = (later - high.astype(F32)).astype(BF16)
     gain_rows = jnp.stack([high, low] + [jnp.zeros_like(high)] * 6)
-    send[-1], gain_rows, cots, norms = lax.optimization_barrier((send[-1], gain_rows, cots, norms))
+    gain_rows, cots, norms, _ = lax.optimization_barrier((gain_rows, cots, norms, send))
     got = [over_y(s, 0) for s in send]
     gain_image = jnp.dot(gain_rows, weight, preferred_element_type=F32)
     gain_image = jnp.sum(gain_image, axis=0, keepdims=True) + image_start
@@ -130,7 +130,7 @@
     left = jnp.concatenate([jnp.where(second, cots[c], norms[c]) for c in chunks])
     both = [b[2:] + g.astype(F32) for b, g in zip(both, got)]
     send = [b[:1].astype(BF16) for b in both]
-    send[-1], gain_image = lax.optimization_barrier((send[-1], gain_image))
+    gain_image, _ = lax.optimization_barrier((gain_image, send))
     got = [over_y(s, 1) for s in send]
     gain_image = gain_image + exchange(gain_image, "row", 2)
     mine = [b[1] + g[0].astype(F32) for b, g in zip(both, got)]

time: 131 us -> 131 us (level)
  no operation moved by 1% of the time
where the time goes in v6:
time: 131 us
  starting transfers between devices  52 us (40%)
  waiting for transfers between devices  40.4 us (31%)
  matrix products  19.4 us (15%)
  other arithmetic  10.6 us (8%)
  local copies, waits for them, and re-layouts  6.44 us (5%)
  between operations  1.79 us (1%)
    ppermute x26, starting transfers between devices, exchange(): return lax.ppermute(block, axis, [(i, i ^ mask) for i in ranks])  32.3 us
    ppermute x26, waiting for transfers between devices, exchange(): return lax.ppermute(block, axis, [(i, i ^ mask) for i in ranks])  17.6 us
    ppermute x8, waiting for transfers between devices, over_y(): lax.ppermute(block, 'row', [(i, i ^ 2 * mask_of(i % 2, turn)) for i in ra...  17.4 us
    ppermute x8, starting transfers between devices, over_y(): lax.ppermute(block, 'row', [(i, i ^ 2 * mask_of(i % 2, turn)) for i in ra...  14.2 us
    dot_general x1, matrix products, local(): lax.dot_general(left, right, CONTRACT_FIRST, preferred_element_type=F32)  7.55 us
    ppermute x4, starting transfers between devices, over_z(): return lax.ppermute(block, ('row', 'col'), route)  5.5 us
    ppermute x4, waiting for transfers between devices, over_z(): return lax.ppermute(block, ('row', 'col'), route)  5.32 us
    dot_general x2, matrix products, local(): lax.dot_general(r, weight, CONTRACT_LAST, preferred_element_type=F32)  5.29 us
  transfers between devices with their start and end apart: 38, of which 22 were waited for; matrix products, arithmetic and copies ran while one was open for 18% of the time, Pallas kernels for 0%

profile of v6, /device:TPU:0, one launch (start us, length us, event | category | flops | bytes accessed | tf_op | source)
XLA Modules:
  0.0 130.6 jit_solution(16351375140058209499)
XLA Ops:
  0.7 1.1 slice_bitcast_fusion.2
  1.7 1.7 %collective-permute-start.2 = (bf16[1,64,512]{2,1,0:T(8,128)(2,1)S(1)}, bf16[1,64,512]{2,1,0:T(8,128)(2,1)S(1)}, u32[]{:S(2)}, u32[]{:S(2)}) collective-permute-start(bf16[1,64,512]{2,1,0:T(8,128)(2,1)S(1)} %get-tuple-element.137), channel_id=1, source_target_pairs={{0,4},{1,5},{2,6},{3,7},{4,0},{5,1},{6,2},{7,3},{8,12},{9,13},{10,... | collective-permute-start | bytes 196616 | tf_op jit(solution)/shard_map/ppermute | solution.py:17
  3.4 1.9 %collective-permute-start = (bf16[1,64,512]{2,1,0:T(8,128)(2,1)S(1)}, bf16[1,64,512]{2,1,0:T(8,128)(2,1)S(1)}, u32[]{:S(2)}, u32[]{:S(2)}) collective-permute-start(bf16[1,64,512]{2,1,0:T(8,128)(2,1)S(1)} %get-tuple-element.138), channel_id=1, source_target_pairs={{0,1},{1,0},{2,3},{3,2},{4,5},{5,4},{6,7},{7,6},{8,9},{9,8},{10,11... | collective-permute-start | bytes 196616 | tf_op jit(solution)/shard_map/ppermute | solution.py:17
  5.3 2.5 %collective-permute-start.1 = (bf16[1,64,512]{2,1,0:T(8,128)(2,1)S(1)}, bf16[1,64,512]{2,1,0:T(8,128)(2,1)S(1)}, u32[]{:S(2)}, u32[]{:S(2)}) collective-permute-start(bf16[1,64,512]{2,1,0:T(8,128)(2,1)S(1)} %get-tuple-element.139), channel_id=1, source_target_pairs={{0,3},{1,2},{2,1},{3,0},{4,7},{5,6},{6,5},{7,4},{8,11},{9,10},{10,... | collective-permute-start | bytes 196616 | tf_op jit(solution)/shard_map/ppermute | solution.py:17
  8.8 1.9 %collective-permute-done.1 = bf16[1,64,512]{2,1,0:T(8,128)(2,1)S(1)} collective-permute-done((bf16[1,64,512]{2,1,0:T(8,128)(2,1)S(1)}, bf16[1,64,512]{2,1,0:T(8,128)(2,1)S(1)}, u32[]{:S(2)}, u32[]{:S(2)}) %collective-permute-start.1) | collective-permute-done | bytes 65568 | tf_op jit(solution)/shard_map/ppermute | solution.py:17
  11.6 2.6 %collective-permute-start.3 = (bf16[2,64,512]{2,1,0:T(8,128)(2,1)S(1)}, bf16[2,64,512]{2,1,0:T(8,128)(2,1)S(1)}, u32[]{:S(2)}, u32[]{:S(2)}) collective-permute-start(bf16[2,64,512]{2,1,0:T(8,128)(2,1)S(1)} %pad_maximum_fusion.9), channel_id=1, source_target_pairs={{0,3},{1,2},{2,1},{3,0},{4,7},{5,6},{6,5},{7,4},{8,11},{9,10},{10,... | collective-permute-start | bytes 393224 | tf_op jit(solution)/shard_map/ppermute | solution.py:17
  14.7 0.9 fusion.62
  15.6 3.1 %collective-permute-done.3 = bf16[2,64,512]{2,1,0:T(8,128)(2,1)S(1)} collective-permute-done((bf16[2,64,512]{2,1,0:T(8,128)(2,1)S(1)}, bf16[2,64,512]{2,1,0:T(8,128)(2,1)S(1)}, u32[]{:S(2)}, u32[]{:S(2)}) %collective-permute-start.3) | collective-permute-done | bytes 131104 | tf_op jit(solution)/shard_map/ppermute | solution.py:17
  18.7 1.0 collective-permute-done.4
  20.0 1.7 %collective-permute-start.10 = (f32[1024]{0:T(1024)S(1)}, f32[1024]{0:T(1024)S(1)}, u32[]{:S(2)}, u32[]{:S(2)}) collective-permute-start(f32[1024]{0:T(1024)S(1)} %fusion.80), channel_id=1, source_target_pairs={{0,16},{8,24},{16,0},{24,8},{32,48},{40,56},{48,32},{56,40},{1,17}... | collective-permute-start | bytes 12296 | tf_op jit(solution)/shard_map/ppermute | solution.py:17
  21.6 1.5 %collective-permute-start.7 = (bf16[4,64,512]{2,1,0:T(8,128)(2,1)S(1)}, bf16[4,64,512]{2,1,0:T(8,128)(2,1)S(1)}, u32[]{:S(2)}, u32[]{:S(2)}) collective-permute-start(bf16[4,64,512]{2,1,0:T(8,128)(2,1)S(1)} %pad_maximum_fusion.6), channel_id=1, source_target_pairs={{0,4},{1,5},{2,6},{3,7},{4,0},{5,1},{6,2},{7,3},{8,12},{9,13},{10,... | collective-permute-start | bytes 786440 | tf_op jit(solution)/shard_map/ppermute | solution.py:17
  24.4 3.0 %collective-permute-start.11 = (f32[1024]{0:T(1024)S(1)}, f32[1024]{0:T(1024)S(1)}, u32[]{:S(2)}, u32[]{:S(2)}) collective-permute-start(f32[1024]{0:T(1024)S(1)} %add.627), channel_id=1, source_target_pairs={{0,32},{8,40},{16,48},{24,56},{32,0},{40,8},{48,16},{56,24},{1,33}... | collective-permute-start | bytes 12296 | tf_op jit(solution)/shard_map/ppermute | solution.py:17
  27.3 2.2 %collective-permute-done.11 = f32[1024]{0:T(1024)S(1)} collective-permute-done((f32[1024]{0:T(1024)S(1)}, f32[1024]{0:T(1024)S(1)}, u32[]{:S(2)}, u32[]{:S(2)}) %collective-permute-start.11) | collective-permute-done | bytes 4128 | tf_op jit(solution)/shard_map/ppermute | solution.py:17
  31.4 1.4 %broadcast_select_fusion.3 = (bf16[8,32,1536]{2,1,0:T(8,128)(2,1)S(1)}, bf16[8,32,1536]{2,1,0:T(8,128)(2,1)}, bf16[8,32,1536]{2,1,0:T(8,128)(2,1)}, bf16[8,32,1536]{2,1,0:T(8,128)(2,1)S(1)}) fusion(bf16[8,32,1536]{2,1,0:T(8,128)(2,1)S(1)} %bitcast.83, pred[]{:T(512)S(6)} %eq.227, bf16[8,64,1536]{2,1,0:T(8,128)(2,1)S(1)} %slice_dynamic-update-slice_fusion, ...), kind=kLoop, calls=%fused_computation.45 | loop fusion | flops 786432 | bytes 6291457 | tf_op jit(solution)/shard_map/jit(_where)/select_n | solution.py:114
  32.8 1.2 slice-done.2
  34.1 2.6 %fusion.8 = f32[256,3072]{1,0:T(8,128)S(1)} fusion(bf16[256,1536]{1,0:T(8,128)(2,1)S(1)} %bitcast.94, bf16[1,1536,3072]{2,1,0:T(8,128)(2,1)S(1)} %bitcast.74), kind=kOutput, calls=%fused_computation.9 | convolution fusion | flops 2415919104 | bytes 13369344 | tf_op jit(solution)/shard_map/dot_general | solution.py:115
  36.9 2.6 %fusion.6 = f32[256,3072]{1,0:T(8,128)S(1)} fusion(bf16[256,1536]{1,0:T(8,128)(2,1)S(1)} %bitcast.93, bf16[1,1536,3072]{2,1,0:T(8,128)(2,1)S(1)} %bitcast.74), kind=kOutput, calls=%fused_computation.7 | convolution fusion | flops 2415919104 | bytes 13369344 | tf_op jit(solution)/shard_map/dot_general | solution.py:115
  40.4 1.1 collective-permute-start.13
  42.3 1.3 %fusion.21 = f32[3072]{0:T(1024)S(1)} fusion(bf16[8,1536]{1,0:T(8,128)(2,1)S(1)} %maximum_maximum_fusion.2, bf16[1,1536,3072]{2,1,0:T(8,128)(2,1)S(1)} %bitcast.74), kind=kOutput, calls=%fused_computation.33 | convolution fusion | flops 75518976 | bytes 9474048 | tf_op jit(solution)/shard_map/dot_general | solution.py:127
  45.2 3.3 %collective-permute-done.13 = bf16[2,32,3072]{2,1,0:T(8,128)(2,1)S(1)} collective-permute-done((bf16[2,32,3072]{2,1,0:T(8,128)(2,1)S(1)}, bf16[2,32,3072]{2,1,0:T(8,128)(2,1)S(1)}, u32[]{:S(2)}, u32[]{:S(2)}) %collective-permute-start.13) | collective-permute-done | bytes 393248 | tf_op jit(solution)/shard_map/ppermute | solution.py:26
  49.4 2.3 %collective-permute-start.14 = (bf16[1,32,3072]{2,1,0:T(8,128)(2,1)}, bf16[1,32,3072]{2,1,0:T(8,128)(2,1)}, u32[]{:S(2)}, u32[]{:S(2)}) collective-permute-start(bf16[1,32,3072]{2,1,0:T(8,128)(2,1)} %slice.428), channel_id=1, source_target_pairs={{0,48},{8,24},{16,32},{24,8},{32,16},{40,56},{48,0},{56,40},{1,49}... | collective-permute-start | bytes 589832 | tf_op jit(solution)/shard_map/ppermute | solution.py:26
  51.6 1.4 %collective-permute-done.17 = bf16[2,32,3072]{2,1,0:T(8,128)(2,1)S(1)} collective-permute-done((bf16[2,32,3072]{2,1,0:T(8,128)(2,1)S(1)}, bf16[2,32,3072]{2,1,0:T(8,128)(2,1)S(1)}, u32[]{:S(2)}, u32[]{:S(2)}) %collective-permute-start.17) | collective-permute-done | bytes 393248 | tf_op jit(solution)/shard_map/ppermute | solution.py:26
  53.2 1.5 %collective-permute-start.20 = (f32[1,3072]{1,0:T(1,128)S(1)}, f32[1,3072]{1,0:T(1,128)S(1)}, u32[]{:S(2)}, u32[]{:S(2)}) collective-permute-start(f32[1,3072]{1,0:T(1,128)S(1)} %add.673), channel_id=1, source_target_pairs={{0,16},{8,24},{16,0},{24,8},{32,48},{40,56},{48,32},{56,40},{1,17}... | collective-permute-start | bytes 36872 | tf_op jit(solution)/shard_map/ppermute | solution.py:17
  54.6 3.0 %collective-permute-start.18 = (bf16[1,32,3072]{2,1,0:T(8,128)(2,1)S(1)}, bf16[1,32,3072]{2,1,0:T(8,128)(2,1)S(1)}, u32[]{:S(2)}, u32[]{:S(2)}) collective-permute-start(bf16[1,32,3072]{2,1,0:T(8,128)(2,1)S(1)} %slice.427), channel_id=1, source_target_pairs={{0,48},{8,24},{16,32},{24,8},{32,16},{40,56},{48,0},{56,40},{1,49}... | collective-permute-start | bytes 589832 | tf_op jit(solution)/shard_map/ppermute | solution.py:26
  57.7 1.3 fusion.49
  59.0 2.5 %collective-permute-start.15 = (bf16[32,3072]{1,0:T(8,128)(2,1)S(1)}, bf16[32,3072]{1,0:T(8,128)(2,1)S(1)}, u32[]{:S(2)}, u32[]{:S(2)}) collective-permute-start(bf16[32,3072]{1,0:T(8,128)(2,1)S(1)} %get-tuple-element.97), channel_id=1, source_target_pairs={{0,64},{64,0},{1,65},{65,1},{2,66},{66,2},{3,67},{67,3},{4,68},{68... | collective-permute-start | bytes 589832 | tf_op jit(solution)/shard_map/ppermute | solution.py:17
  61.9 3.2 %collective-permute-start.21 = (f32[1,3072]{1,0:T(1,128)S(1)}, f32[1,3072]{1,0:T(1,128)S(1)}, u32[]{:S(2)}, u32[]{:S(2)}) collective-permute-start(f32[1,3072]{1,0:T(1,128)S(1)} %add.674), channel_id=1, source_target_pairs={{0,32},{8,40},{16,48},{24,56},{32,0},{40,8},{48,16},{56,24},{1,33}... | collective-permute-start | bytes 36872 | tf_op jit(solution)/shard_map/ppermute | solution.py:17
  65.1 1.2 collective-permute-start.25
  67.7 3.1 %collective-permute-start.22 = (bf16[1,32,3200]{2,1,0:T(8,128)(2,1)S(1)}, bf16[1,32,3200]{2,1,0:T(8,128)(2,1)S(1)}, u32[]{:S(2)}, u32[]{:S(2)}) collective-permute-start(bf16[1,32,3200]{2,1,0:T(8,128)(2,1)S(1)} %fusion.57), channel_id=1, source_target_pairs={{0,48},{8,24},{16,32},{24,8},{32,16},{40,56},{48,0},{56,40},{1,49}... | collective-permute-start | bytes 614408 | tf_op jit(solution)/shard_map/ppermute | solution.py:26
  70.8 1.4 %collective-permute-done.25 = bf16[32,3072]{1,0:T(8,128)(2,1)S(1)} collective-permute-done((bf16[32,3072]{1,0:T(8,128)(2,1)S(1)}, bf16[32,3072]{1,0:T(8,128)(2,1)S(1)}, u32[]{:S(2)}, u32[]{:S(2)}) %collective-permute-start.25) | collective-permute-done | bytes 196640 | tf_op jit(solution)/shard_map/ppermute | solution.py:17
  72.9 1.3 collective-permute-start.26
  74.2 1.6 %collective-permute-done.22 = bf16[1,32,3200]{2,1,0:T(8,128)(2,1)S(1)} collective-permute-done((bf16[1,32,3200]{2,1,0:T(8,128)(2,1)S(1)}, bf16[1,32,3200]{2,1,0:T(8,128)(2,1)S(1)}, u32[]{:S(2)}, u32[]{:S(2)}) %collective-permute-start.22) | collective-permute-done | bytes 204832 | tf_op jit(solution)/shard_map/ppermute | solution.py:26
  75.8 2.5 %collective-permute-start.23 = (bf16[2,32,3200]{2,1,0:T(8,128)(2,1)S(1)}, bf16[2,32,3200]{2,1,0:T(8,128)(2,1)S(1)}, u32[]{:S(2)}, u32[]{:S(2)}) collective-permute-start(bf16[2,32,3200]{2,1,0:T(8,128)(2,1)S(1)} %pad_maximum_fusion.4), channel_id=1, source_target_pairs={{0,16},{8,56},{16,0},{24,40},{32,48},{40,24},{48,32},{56,8},{1,17}... | collective-permute-start | bytes 1228808 | tf_op jit(solution)/shard_map/ppermute | solution.py:26
  78.3 3.9 %collective-permute-done.26 = bf16[1,32,3200]{2,1,0:T(8,128)(2,1)S(1)} collective-permute-done((bf16[1,32,3200]{2,1,0:T(8,128)(2,1)S(1)}, bf16[1,32,3200]{2,1,0:T(8,128)(2,1)S(1)}, u32[]{:S(2)}, u32[]{:S(2)}) %collective-permute-start.26) | collective-permute-done | bytes 204832 | tf_op jit(solution)/shard_map/ppermute | solution.py:26
  82.7 1.5 %collective-permute-done.23 = bf16[2,32,3200]{2,1,0:T(8,128)(2,1)S(1)} collective-permute-done((bf16[2,32,3200]{2,1,0:T(8,128)(2,1)S(1)}, bf16[2,32,3200]{2,1,0:T(8,128)(2,1)S(1)}, u32[]{:S(2)}, u32[]{:S(2)}) %collective-permute-start.23) | collective-permute-done | bytes 409632 | tf_op jit(solution)/shard_map/ppermute | solution.py:26
  84.7 5.6 %collective-permute-done.27 = bf16[2,32,3200]{2,1,0:T(8,128)(2,1)S(1)} collective-permute-done((bf16[2,32,3200]{2,1,0:T(8,128)(2,1)S(1)}, bf16[2,32,3200]{2,1,0:T(8,128)(2,1)S(1)}, u32[]{:S(2)}, u32[]{:S(2)}) %collective-permute-start.27) | collective-permute-done | bytes 409632 | tf_op jit(solution)/shard_map/ppermute | solution.py:26
  91.9 2.6 %fusion.2 = f32[256,1536]{1,0:T(8,128)S(1)} fusion(bf16[1,1536,3072]{2,1,0:T(8,128)(2,1)S(1)} %bitcast.76, bf16[128,3072]{1,0:T(8,128)(2,1)S(1)} %slice.312, bf16[128,3072]{1,0:T(8,128)(2,1)S(1)} %slice.311), kind=kOutput, calls=%fused_computation.3 | convolution fusion | flops 2419064832 | bytes 12582912 | tf_op jit(solution)/shard_map/dot_general | solution.py:178
  94.7 2.6 %fusion = f32[256,1536]{1,0:T(8,128)S(1)} fusion(bf16[1,1536,3072]{2,1,0:T(8,128)(2,1)S(1)} %bitcast.76, bf16[128,3072]{1,0:T(8,128)(2,1)S(1)} %slice.316, bf16[128,3072]{1,0:T(8,128)(2,1)S(1)} %slice.315), kind=kOutput, calls=%fused_computation.1 | convolution fusion | flops 2419064832 | bytes 12582912 | tf_op jit(solution)/shard_map/dot_general | solution.py:178
  98.4 1.6 %collective-permute-start.29 = (f32[1536]{0:T(1024)S(1)}, f32[1536]{0:T(1024)S(1)}, u32[]{:S(2)}, u32[]{:S(2)}) collective-permute-start(f32[1536]{0:T(1024)S(1)} %div.314), channel_id=1, source_target_pairs={{0,1},{1,0},{2,3},{3,2},{4,5},{5,4},{6,7},{7,6},{8,9},{9,8},{10,11... | collective-permute-start | bytes 18440 | tf_op jit(solution)/shard_map/ppermute | solution.py:17
  100.8 1.5 %collective-permute-start.31 = (bf16[4,32,1664]{2,1,0:T(8,128)(2,1)S(1)}, bf16[4,32,1664]{2,1,0:T(8,128)(2,1)S(1)}, u32[]{:S(2)}, u32[]{:S(2)}) collective-permute-start(bf16[4,32,1664]{2,1,0:T(8,128)(2,1)S(1)} %maximum_maximum_fusion), channel_id=1, source_target_pairs={{0,1},{1,0},{2,3},{3,2},{4,5},{5,4},{6,7},{7,6},{8,11},{9,10},{10,... | collective-permute-start | bytes 1277960 | tf_op jit(solution)/shard_map/ppermute | solution.py:36
  102.3 3.3 %collective-permute-start.36 = (f32[1536]{0:T(1024)S(1)}, f32[1536]{0:T(1024)S(1)}, u32[]{:S(2)}, u32[]{:S(2)}) collective-permute-start(f32[1536]{0:T(1024)S(1)} %add.697), channel_id=1, source_target_pairs={{0,2},{1,3},{2,0},{3,1},{4,6},{5,7},{6,4},{7,5},{8,10},{9,11},{10,... | collective-permute-start | bytes 18440 | tf_op jit(solution)/shard_map/ppermute | solution.py:17
  105.6 7.5 %convolution_convert_fusion = bf16[1536,3072]{1,0:T(8,128)(2,1)} fusion(bf16[512,1536]{1,0:T(8,128)(2,1)S(1)} %pad_maximum_fusion.1, bf16[512,3072]{1,0:T(8,128)(2,1)S(1)} %pad_maximum_fusion), kind=kOutput, calls=%fused_computation | convolution fusion | flops 4836556800 | bytes 14155776 | tf_op jit(solution)/shard_map/dot_general | solution.py:207
  113.2 1.9 %collective-permute-done.36 = f32[1536]{0:T(1024)S(1)} collective-permute-done((f32[1536]{0:T(1024)S(1)}, f32[1536]{0:T(1024)S(1)}, u32[]{:S(2)}, u32[]{:S(2)}) %collective-permute-start.36) | collective-permute-done | bytes 6176 | tf_op jit(solution)/shard_map/ppermute | solution.py:17
  116.3 2.5 %collective-permute-start.32 = (bf16[2,32,1664]{2,1,0:T(8,128)(2,1)S(1)}, bf16[2,32,1664]{2,1,0:T(8,128)(2,1)S(1)}, u32[]{:S(2)}, u32[]{:S(2)}) collective-permute-start(bf16[2,32,1664]{2,1,0:T(8,128)(2,1)S(1)} %slice.426), channel_id=1, source_target_pairs={{0,3},{1,2},{2,1},{3,0},{4,7},{5,6},{6,5},{7,4},{8,9},{9,8},{10,11... | collective-permute-start | bytes 638984 | tf_op jit(solution)/shard_map/ppermute | solution.py:36
  119.0 3.4 %collective-permute-done.34 = bf16[2,32,1664]{2,1,0:T(8,128)(2,1)S(1)} collective-permute-done((bf16[2,32,1664]{2,1,0:T(8,128)(2,1)S(1)}, bf16[2,32,1664]{2,1,0:T(8,128)(2,1)S(1)}, u32[]{:S(2)}, u32[]{:S(2)}) %collective-permute-start.34) | collective-permute-done | bytes 213024 | tf_op jit(solution)/shard_map/ppermute | solution.py:36
  122.8 1.9 %collective-permute-done.32 = bf16[2,32,1664]{2,1,0:T(8,128)(2,1)S(1)} collective-permute-done((bf16[2,32,1664]{2,1,0:T(8,128)(2,1)S(1)}, bf16[2,32,1664]{2,1,0:T(8,128)(2,1)S(1)}, u32[]{:S(2)}, u32[]{:S(2)}) %collective-permute-start.32) | collective-permute-done | bytes 213024 | tf_op jit(solution)/shard_map/ppermute | solution.py:36
  125.1 2.2 %collective-permute-done.35 = bf16[32,1664]{1,0:T(8,128)(2,1)S(1)} collective-permute-done((bf16[32,1664]{1,0:T(8,128)(2,1)S(1)}, bf16[32,1664]{1,0:T(8,128)(2,1)S(1)}, u32[]{:S(2)}, u32[]{:S(2)}) %collective-permute-start.35) | collective-permute-done | bytes 106528 | tf_op jit(solution)/shard_map/ppermute | solution.py:17
  127.9 1.6 %collective-permute-done.33 = bf16[32,1664]{1,0:T(8,128)(2,1)S(1)} collective-permute-done((bf16[32,1664]{1,0:T(8,128)(2,1)S(1)}, bf16[32,1664]{1,0:T(8,128)(2,1)S(1)}, u32[]{:S(2)}, u32[]{:S(2)}) %collective-permute-start.33) | collective-permute-done | bytes 106528 | tf_op jit(solution)/shard_map/ppermute | solution.py:17
  (198 shorter events, 20.2 us)
Async XLA Ops:
  0.6 10.2 %copy-start = (bf16[512,1536]{1,0:T(8,128)(2,1)S(1)}, bf16[512,1536]{1,0:T(8,128)(2,1)}, u32[]{:S(2)}) copy-start(bf16[512,1536]{1,0:T(8,128)(2,1)} %param.4) | copy-start | bytes 4718596
  0.6 32.2 %slice-start = ((s8[9437184]{0:T(1024)(128)(4,1)}), s8[1048576]{0:T(1024)(128)(4,1)S(1)}, s32[]{:S(2)}) async-start(s8[9437184]{0:T(1024)(128)(4,1)} %bitcast.73), calls=%async_computation | async-start | bytes 2097152
  1.7 7.0 %collective-permute-start.2 = (bf16[1,64,512]{2,1,0:T(8,128)(2,1)S(1)}, bf16[1,64,512]{2,1,0:T(8,128)(2,1)S(1)}, u32[]{:S(2)}, u32[]{:S(2)}) collective-permute-start(bf16[1,64,512]{2,1,0:T(8,128)(2,1)S(1)} %get-tuple-element.137), channel_id=1, source_target_pairs={{0,4},{1,5},{2,6},{3,7},{4,0},{5,1},{6,2},{7,3},{8,12},{9,13},{10,... | collective-permute-start | bytes 196616 | tf_op jit(solution)/shard_map/ppermute | solution.py:17
  3.4 5.4 %collective-permute-start = (bf16[1,64,512]{2,1,0:T(8,128)(2,1)S(1)}, bf16[1,64,512]{2,1,0:T(8,128)(2,1)S(1)}, u32[]{:S(2)}, u32[]{:S(2)}) collective-permute-start(bf16[1,64,512]{2,1,0:T(8,128)(2,1)S(1)} %get-tuple-element.138), channel_id=1, source_target_pairs={{0,1},{1,0},{2,3},{3,2},{4,5},{5,4},{6,7},{7,6},{8,9},{9,8},{10,11... | collective-permute-start | bytes 196616 | tf_op jit(solution)/shard_map/ppermute | solution.py:17
  5.3 5.5 %collective-permute-start.1 = (bf16[1,64,512]{2,1,0:T(8,128)(2,1)S(1)}, bf16[1,64,512]{2,1,0:T(8,128)(2,1)S(1)}, u32[]{:S(2)}, u32[]{:S(2)}) collective-permute-start(bf16[1,64,512]{2,1,0:T(8,128)(2,1)S(1)} %get-tuple-element.139), channel_id=1, source_target_pairs={{0,3},{1,2},{2,1},{3,0},{4,7},{5,6},{6,5},{7,4},{8,11},{9,10},{10,... | collective-permute-start | bytes 196616 | tf_op jit(solution)/shard_map/ppermute | solution.py:17
  11.5 4.1 %collective-permute-start.6 = (f32[1024]{0:T(1024)S(1)}, f32[1024]{0:T(1024)S(1)}, u32[]{:S(2)}, u32[]{:S(2)}) collective-permute-start(f32[1024]{0:T(1024)S(1)} %pad_maximum_fusion.15), channel_id=1, source_target_pairs={{0,8},{8,0},{16,24},{24,16},{32,40},{40,32},{48,56},{56,48},{1,9},... | collective-permute-start | bytes 12296 | tf_op jit(solution)/shard_map/ppermute | solution.py:17
  11.6 7.1 %collective-permute-start.3 = (bf16[2,64,512]{2,1,0:T(8,128)(2,1)S(1)}, bf16[2,64,512]{2,1,0:T(8,128)(2,1)S(1)}, u32[]{:S(2)}, u32[]{:S(2)}) collective-permute-start(bf16[2,64,512]{2,1,0:T(8,128)(2,1)S(1)} %pad_maximum_fusion.9), channel_id=1, source_target_pairs={{0,3},{1,2},{2,1},{3,0},{4,7},{5,6},{6,5},{7,4},{8,11},{9,10},{10,... | collective-permute-start | bytes 393224 | tf_op jit(solution)/shard_map/ppermute | solution.py:17
  14.2 5.6 %collective-permute-start.4 = (bf16[2,64,512]{2,1,0:T(8,128)(2,1)S(1)}, bf16[2,64,512]{2,1,0:T(8,128)(2,1)S(1)}, u32[]{:S(2)}, u32[]{:S(2)}) collective-permute-start(bf16[2,64,512]{2,1,0:T(8,128)(2,1)S(1)} %pad_maximum_fusion.10), channel_id=1, source_target_pairs={{0,4},{1,5},{2,6},{3,7},{4,0},{5,1},{6,2},{7,3},{8,12},{9,13},{10,... | collective-permute-start | bytes 393224 | tf_op jit(solution)/shard_map/ppermute | solution.py:17
  14.7 5.3 %collective-permute-start.5 = (bf16[2,64,512]{2,1,0:T(8,128)(2,1)S(1)}, bf16[2,64,512]{2,1,0:T(8,128)(2,1)S(1)}, u32[]{:S(2)}, u32[]{:S(2)}) collective-permute-start(bf16[2,64,512]{2,1,0:T(8,128)(2,1)S(1)} %pad_maximum_fusion.11), channel_id=1, source_target_pairs={{0,1},{1,0},{2,3},{3,2},{4,5},{5,4},{6,7},{7,6},{8,9},{9,8},{10,11... | collective-permute-start | bytes 393224 | tf_op jit(solution)/shard_map/ppermute | solution.py:17
  20.0 4.3 %collective-permute-start.10 = (f32[1024]{0:T(1024)S(1)}, f32[1024]{0:T(1024)S(1)}, u32[]{:S(2)}, u32[]{:S(2)}) collective-permute-start(f32[1024]{0:T(1024)S(1)} %fusion.80), channel_id=1, source_target_pairs={{0,16},{8,24},{16,0},{24,8},{32,48},{40,56},{48,32},{56,40},{1,17}... | collective-permute-start | bytes 12296 | tf_op jit(solution)/shard_map/ppermute | solution.py:17
  21.6 8.7 %collective-permute-start.7 = (bf16[4,64,512]{2,1,0:T(8,128)(2,1)S(1)}, bf16[4,64,512]{2,1,0:T(8,128)(2,1)S(1)}, u32[]{:S(2)}, u32[]{:S(2)}) collective-permute-start(bf16[4,64,512]{2,1,0:T(8,128)(2,1)S(1)} %pad_maximum_fusion.6), channel_id=1, source_target_pairs={{0,4},{1,5},{2,6},{3,7},{4,0},{5,1},{6,2},{7,3},{8,12},{9,13},{10,... | collective-permute-start | bytes 786440 | tf_op jit(solution)/shard_map/ppermute | solution.py:17
  23.1 7.4 %collective-permute-start.8 = (bf16[4,64,512]{2,1,0:T(8,128)(2,1)S(1)}, bf16[4,64,512]{2,1,0:T(8,128)(2,1)S(1)}, u32[]{:S(2)}, u32[]{:S(2)}) collective-permute-start(bf16[4,64,512]{2,1,0:T(8,128)(2,1)S(1)} %pad_maximum_fusion.7), channel_id=1, source_target_pairs={{0,1},{1,0},{2,3},{3,2},{4,5},{5,4},{6,7},{7,6},{8,9},{9,8},{10,11... | collective-permute-start | bytes 786440 | tf_op jit(solution)/shard_map/ppermute | solution.py:17
  23.4 7.9 %collective-permute-start.9 = (bf16[4,64,512]{2,1,0:T(8,128)(2,1)S(1)}, bf16[4,64,512]{2,1,0:T(8,128)(2,1)S(1)}, u32[]{:S(2)}, u32[]{:S(2)}) collective-permute-start(bf16[4,64,512]{2,1,0:T(8,128)(2,1)S(1)} %pad_maximum_fusion.8), channel_id=1, source_target_pairs={{0,3},{1,2},{2,1},{3,0},{4,7},{5,6},{6,5},{7,4},{8,11},{9,10},{10,... | collective-permute-start | bytes 786440 | tf_op jit(solution)/shard_map/ppermute | solution.py:17
  24.4 5.2 %collective-permute-start.11 = (f32[1024]{0:T(1024)S(1)}, f32[1024]{0:T(1024)S(1)}, u32[]{:S(2)}, u32[]{:S(2)}) collective-permute-start(f32[1024]{0:T(1024)S(1)} %add.627), channel_id=1, source_target_pairs={{0,32},{8,40},{16,48},{24,56},{32,0},{40,8},{48,16},{56,24},{1,33}... | collective-permute-start | bytes 12296 | tf_op jit(solution)/shard_map/ppermute | solution.py:17
  36.8 3.5 %collective-permute-start.12 = (bf16[128,3072]{1,0:T(8,128)(2,1)S(1)}, bf16[128,3072]{1,0:T(8,128)(2,1)S(1)}, u32[]{:S(2)}, u32[]{:S(2)}) collective-permute-start(bf16[128,3072]{1,0:T(8,128)(2,1)S(1)} %slice.422), channel_id=1, source_target_pairs={{0,8},{8,0},{16,24},{24,16},{32,40},{40,32},{48,56},{56,48},{1,9},... | collective-permute-start | bytes 2359304 | tf_op jit(solution)/shard_map/ppermute | solution.py:17
  39.6 2.5 %collective-permute-start.16 = (bf16[128,3072]{1,0:T(8,128)(2,1)S(1)}, bf16[128,3072]{1,0:T(8,128)(2,1)S(1)}, u32[]{:S(2)}, u32[]{:S(2)}) collective-permute-start(bf16[128,3072]{1,0:T(8,128)(2,1)S(1)} %slice.421), channel_id=1, source_target_pairs={{0,8},{8,0},{16,24},{24,16},{32,40},{40,32},{48,56},{56,48},{1,9},... | collective-permute-start | bytes 2359304 | tf_op jit(solution)/shard_map/ppermute | solution.py:17
  40.4 8.0 %collective-permute-start.13 = (bf16[2,32,3072]{2,1,0:T(8,128)(2,1)S(1)}, bf16[2,32,3072]{2,1,0:T(8,128)(2,1)S(1)}, u32[]{:S(2)}, u32[]{:S(2)}) collective-permute-start(bf16[2,32,3072]{2,1,0:T(8,128)(2,1)S(1)} %bitcast.95), channel_id=1, source_target_pairs={{0,16},{8,56},{16,0},{24,40},{32,48},{40,24},{48,32},{56,8},{1,17}... | collective-permute-start | bytes 1179656 | tf_op jit(solution)/shard_map/ppermute | solution.py:26
  43.6 1.6 %collective-permute-start.19 = (f32[1,3072]{1,0:T(1,128)S(1)}, f32[1,3072]{1,0:T(1,128)S(1)}, u32[]{:S(2)}, u32[]{:S(2)}) collective-permute-start(f32[1,3072]{1,0:T(1,128)S(1)} %add.672), channel_id=1, source_target_pairs={{0,8},{8,0},{16,24},{24,16},{32,40},{40,32},{48,56},{56,48},{1,9},... | collective-permute-start | bytes 36872 | tf_op jit(solution)/shard_map/ppermute | solution.py:17
  44.4 4.1 %slice-start.6 = ((f32[128,3072]{1,0:T(8,128)}), f32[64,3072]{1,0:T(8,128)S(1)}, s32[]{:S(2)}) async-start(f32[128,3072]{1,0:T(8,128)} %copy-done.1), calls=%async_computation.6 | async-start | bytes 1572864 | tf_op jit(solution)/shard_map/slice | solution.py:131
  44.4 8.7 %slice-start.7 = ((f32[128,3072]{1,0:T(8,128)}), f32[64,3072]{1,0:T(8,128)S(1)}, s32[]{:S(2)}) async-start(f32[128,3072]{1,0:T(8,128)} %copy-done.2), calls=%async_computation.7 | async-start | bytes 1572864 | tf_op jit(solution)/shard_map/slice | solution.py:131
  44.4 8.7 %collective-permute-start.17 = (bf16[2,32,3072]{2,1,0:T(8,128)(2,1)S(1)}, bf16[2,32,3072]{2,1,0:T(8,128)(2,1)S(1)}, u32[]{:S(2)}, u32[]{:S(2)}) collective-permute-start(bf16[2,32,3072]{2,1,0:T(8,128)(2,1)S(1)} %bitcast.96), channel_id=1, source_target_pairs={{0,16},{8,56},{16,0},{24,40},{32,48},{40,24},{48,32},{56,8},{1,17}... | collective-permute-start | bytes 1179656 | tf_op jit(solution)/shard_map/ppermute | solution.py:26
  48.6 4.6 %copy-start.7 = (f32[2,32,3072]{2,1,0:T(8,128)}, f32[2,32,3072]{2,1,0:T(8,128)S(1)}, u32[]{:S(2)}) copy-start(f32[2,32,3072]{2,1,0:T(8,128)S(1)} %convert_add_fusion.1) | copy-start | bytes 2359300
  49.4 8.3 %collective-permute-start.14 = (bf16[1,32,3072]{2,1,0:T(8,128)(2,1)}, bf16[1,32,3072]{2,1,0:T(8,128)(2,1)}, u32[]{:S(2)}, u32[]{:S(2)}) collective-permute-start(bf16[1,32,3072]{2,1,0:T(8,128)(2,1)} %slice.428), channel_id=1, source_target_pairs={{0,48},{8,24},{16,32},{24,8},{32,16},{40,56},{48,0},{56,40},{1,49}... | collective-permute-start | bytes 589832 | tf_op jit(solution)/shard_map/ppermute | solution.py:26
  53.2 4.5 %collective-permute-start.20 = (f32[1,3072]{1,0:T(1,128)S(1)}, f32[1,3072]{1,0:T(1,128)S(1)}, u32[]{:S(2)}, u32[]{:S(2)}) collective-permute-start(f32[1,3072]{1,0:T(1,128)S(1)} %add.673), channel_id=1, source_target_pairs={{0,16},{8,24},{16,0},{24,8},{32,48},{40,56},{48,32},{56,40},{1,17}... | collective-permute-start | bytes 36872 | tf_op jit(solution)/shard_map/ppermute | solution.py:17
  54.6 6.9 %collective-permute-start.18 = (bf16[1,32,3072]{2,1,0:T(8,128)(2,1)S(1)}, bf16[1,32,3072]{2,1,0:T(8,128)(2,1)S(1)}, u32[]{:S(2)}, u32[]{:S(2)}) collective-permute-start(bf16[1,32,3072]{2,1,0:T(8,128)(2,1)S(1)} %slice.427), channel_id=1, source_target_pairs={{0,48},{8,24},{16,32},{24,8},{32,16},{40,56},{48,0},{56,40},{1,49}... | collective-permute-start | bytes 589832 | tf_op jit(solution)/shard_map/ppermute | solution.py:26
  59.0 8.1 %collective-permute-start.15 = (bf16[32,3072]{1,0:T(8,128)(2,1)S(1)}, bf16[32,3072]{1,0:T(8,128)(2,1)S(1)}, u32[]{:S(2)}, u32[]{:S(2)}) collective-permute-start(bf16[32,3072]{1,0:T(8,128)(2,1)S(1)} %get-tuple-element.97), channel_id=1, source_target_pairs={{0,64},{64,0},{1,65},{65,1},{2,66},{66,2},{3,67},{67,3},{4,68},{68... | collective-permute-start | bytes 589832 | tf_op jit(solution)/shard_map/ppermute | solution.py:17
  61.5 29.6 %slice-start.3 = ((s8[9437184]{0:T(1024)(128)(4,1)}), s8[4194304]{0:T(1024)(128)(4,1)S(1)}, s32[]{:S(2)}) async-start(s8[9437184]{0:T(1024)(128)(4,1)} %bitcast.75), calls=%async_computation.3 | async-start | bytes 8388608
  61.9 5.2 %collective-permute-start.21 = (f32[1,3072]{1,0:T(1,128)S(1)}, f32[1,3072]{1,0:T(1,128)S(1)}, u32[]{:S(2)}, u32[]{:S(2)}) collective-permute-start(f32[1,3072]{1,0:T(1,128)S(1)} %add.674), channel_id=1, source_target_pairs={{0,32},{8,40},{16,48},{24,56},{32,0},{40,8},{48,16},{56,24},{1,33}... | collective-permute-start | bytes 36872 | tf_op jit(solution)/shard_map/ppermute | solution.py:17
  65.1 7.2 %collective-permute-start.25 = (bf16[32,3072]{1,0:T(8,128)(2,1)S(1)}, bf16[32,3072]{1,0:T(8,128)(2,1)S(1)}, u32[]{:S(2)}, u32[]{:S(2)}) collective-permute-start(bf16[32,3072]{1,0:T(8,128)(2,1)S(1)} %get-tuple-element.60), channel_id=1, source_target_pairs={{0,64},{64,0},{1,65},{65,1},{2,66},{66,2},{3,67},{67,3},{4,68},{68... | collective-permute-start | bytes 589832 | tf_op jit(solution)/shard_map/ppermute | solution.py:17
  67.7 8.0 %collective-permute-start.22 = (bf16[1,32,3200]{2,1,0:T(8,128)(2,1)S(1)}, bf16[1,32,3200]{2,1,0:T(8,128)(2,1)S(1)}, u32[]{:S(2)}, u32[]{:S(2)}) collective-permute-start(bf16[1,32,3200]{2,1,0:T(8,128)(2,1)S(1)} %fusion.57), channel_id=1, source_target_pairs={{0,48},{8,24},{16,32},{24,8},{32,16},{40,56},{48,0},{56,40},{1,49}... | collective-permute-start | bytes 614408 | tf_op jit(solution)/shard_map/ppermute | solution.py:26
  72.9 11.6 %copy-start.4 = (bf16[256,1536]{1,0:T(8,128)(2,1)S(1)}, bf16[256,1536]{1,0:T(8,128)(2,1)}, u32[]{:S(2)}) copy-start(bf16[256,1536]{1,0:T(8,128)(2,1)} %copy-done.3) | copy-start | bytes 2359300
  72.9 11.6 %copy-start.5 = (bf16[8,32,1536]{2,1,0:T(8,128)(2,1)S(1)}, bf16[8,32,1536]{2,1,0:T(8,128)(2,1)}, u32[]{:S(2)}) copy-start(bf16[8,32,1536]{2,1,0:T(8,128)(2,1)} %get-tuple-element.118) | copy-start | bytes 2359300
  72.9 11.6 %copy-start.6 = (bf16[8,32,1536]{2,1,0:T(8,128)(2,1)S(1)}, bf16[8,32,1536]{2,1,0:T(8,128)(2,1)}, u32[]{:S(2)}) copy-start(bf16[8,32,1536]{2,1,0:T(8,128)(2,1)} %get-tuple-element.119) | copy-start | bytes 2359300
  72.9 9.3 %collective-permute-start.26 = (bf16[1,32,3200]{2,1,0:T(8,128)(2,1)S(1)}, bf16[1,32,3200]{2,1,0:T(8,128)(2,1)S(1)}, u32[]{:S(2)}, u32[]{:S(2)}) collective-permute-start(bf16[1,32,3200]{2,1,0:T(8,128)(2,1)S(1)} %fusion.58), channel_id=1, source_target_pairs={{0,48},{8,24},{16,32},{24,8},{32,16},{40,56},{48,0},{56,40},{1,49}... | collective-permute-start | bytes 614408 | tf_op jit(solution)/shard_map/ppermute | solution.py:26
  75.8 8.4 %collective-permute-start.23 = (bf16[2,32,3200]{2,1,0:T(8,128)(2,1)S(1)}, bf16[2,32,3200]{2,1,0:T(8,128)(2,1)S(1)}, u32[]{:S(2)}, u32[]{:S(2)}) collective-permute-start(bf16[2,32,3200]{2,1,0:T(8,128)(2,1)S(1)} %pad_maximum_fusion.4), channel_id=1, source_target_pairs={{0,16},{8,56},{16,0},{24,40},{32,48},{40,24},{48,32},{56,8},{1,17}... | collective-permute-start | bytes 1228808 | tf_op jit(solution)/shard_map/ppermute | solution.py:26
  82.3 8.9 %slice-start.4 = ((s8[9437184]{0:T(1024)(128)(4,1)}), s8[4194304]{0:T(1024)(128)(4,1)S(1)}, s32[]{:S(2)}) async-start(s8[9437184]{0:T(1024)(128)(4,1)} %bitcast.75), calls=%async_computation.4 | async-start | bytes 8388608
  82.3 8.0 %collective-permute-start.27 = (bf16[2,32,3200]{2,1,0:T(8,128)(2,1)S(1)}, bf16[2,32,3200]{2,1,0:T(8,128)(2,1)S(1)}, u32[]{:S(2)}, u32[]{:S(2)}) collective-permute-start(bf16[2,32,3200]{2,1,0:T(8,128)(2,1)S(1)} %pad_maximum_fusion.5), channel_id=1, source_target_pairs={{0,16},{8,56},{16,0},{24,40},{32,48},{40,24},{48,32},{56,8},{1,17}... | collective-permute-start | bytes 1228808 | tf_op jit(solution)/shard_map/ppermute | solution.py:26
  84.3 6.7 %collective-permute-start.24 = (bf16[128,3200]{1,0:T(8,128)(2,1)S(1)}, bf16[128,3200]{1,0:T(8,128)(2,1)S(1)}, u32[]{:S(2)}, u32[]{:S(2)}) collective-permute-start(bf16[128,3200]{1,0:T(8,128)(2,1)S(1)} %bitcast.85), channel_id=1, source_target_pairs={{0,8},{8,0},{16,24},{24,16},{32,40},{40,32},{48,56},{56,48},{1,9},... | collective-permute-start | bytes 2457608 | tf_op jit(solution)/shard_map/ppermute | solution.py:17
  90.4 4.2 %collective-permute-start.28 = (bf16[128,3200]{1,0:T(8,128)(2,1)S(1)}, bf16[128,3200]{1,0:T(8,128)(2,1)S(1)}, u32[]{:S(2)}, u32[]{:S(2)}) collective-permute-start(bf16[128,3200]{1,0:T(8,128)(2,1)S(1)} %bitcast.88), channel_id=1, source_target_pairs={{0,8},{8,0},{16,24},{24,16},{32,40},{40,32},{48,56},{56,48},{1,9},... | collective-permute-start | bytes 2457608 | tf_op jit(solution)/shard_map/ppermute | solution.py:17
  98.4 3.9 %collective-permute-start.29 = (f32[1536]{0:T(1024)S(1)}, f32[1536]{0:T(1024)S(1)}, u32[]{:S(2)}, u32[]{:S(2)}) collective-permute-start(f32[1536]{0:T(1024)S(1)} %div.314), channel_id=1, source_target_pairs={{0,1},{1,0},{2,3},{3,2},{4,5},{5,4},{6,7},{7,6},{8,9},{9,8},{10,11... | collective-permute-start | bytes 18440 | tf_op jit(solution)/shard_map/ppermute | solution.py:17
  100.2 14.9 %collective-permute-start.30 = (bf16[4,32,1664]{2,1,0:T(8,128)(2,1)S(1)}, bf16[4,32,1664]{2,1,0:T(8,128)(2,1)S(1)}, u32[]{:S(2)}, u32[]{:S(2)}) collective-permute-start(bf16[4,32,1664]{2,1,0:T(8,128)(2,1)S(1)} %maximum_maximum_fusion.1), channel_id=1, source_target_pairs={{0,1},{1,0},{2,3},{3,2},{4,5},{5,4},{6,7},{7,6},{8,11},{9,10},{10,... | collective-permute-start | bytes 1277960 | tf_op jit(solution)/shard_map/ppermute | solution.py:36
  100.8 14.3 %collective-permute-start.31 = (bf16[4,32,1664]{2,1,0:T(8,128)(2,1)S(1)}, bf16[4,32,1664]{2,1,0:T(8,128)(2,1)S(1)}, u32[]{:S(2)}, u32[]{:S(2)}) collective-permute-start(bf16[4,32,1664]{2,1,0:T(8,128)(2,1)S(1)} %maximum_maximum_fusion), channel_id=1, source_target_pairs={{0,1},{1,0},{2,3},{3,2},{4,5},{5,4},{6,7},{7,6},{8,11},{9,10},{10,... | collective-permute-start | bytes 1277960 | tf_op jit(solution)/shard_map/ppermute | solution.py:36
  102.3 12.8 %collective-permute-start.36 = (f32[1536]{0:T(1024)S(1)}, f32[1536]{0:T(1024)S(1)}, u32[]{:S(2)}, u32[]{:S(2)}) collective-permute-start(f32[1536]{0:T(1024)S(1)} %add.697), channel_id=1, source_target_pairs={{0,2},{1,3},{2,0},{3,1},{4,6},{5,7},{6,4},{7,5},{8,10},{9,11},{10,... | collective-permute-start | bytes 18440 | tf_op jit(solution)/shard_map/ppermute | solution.py:17
  115.3 7.1 %collective-permute-start.34 = (bf16[2,32,1664]{2,1,0:T(8,128)(2,1)S(1)}, bf16[2,32,1664]{2,1,0:T(8,128)(2,1)S(1)}, u32[]{:S(2)}, u32[]{:S(2)}) collective-permute-start(bf16[2,32,1664]{2,1,0:T(8,128)(2,1)S(1)} %slice.425), channel_id=1, source_target_pairs={{0,3},{1,2},{2,1},{3,0},{4,7},{5,6},{6,5},{7,4},{8,9},{9,8},{10,11... | collective-permute-start | bytes 638984 | tf_op jit(solution)/shard_map/ppermute | solution.py:36
  116.3 8.4 %collective-permute-start.32 = (bf16[2,32,1664]{2,1,0:T(8,128)(2,1)S(1)}, bf16[2,32,1664]{2,1,0:T(8,128)(2,1)S(1)}, u32[]{:S(2)}, u32[]{:S(2)}) collective-permute-start(bf16[2,32,1664]{2,1,0:T(8,128)(2,1)S(1)} %slice.426), channel_id=1, source_target_pairs={{0,3},{1,2},{2,1},{3,0},{4,7},{5,6},{6,5},{7,4},{8,9},{9,8},{10,11... | collective-permute-start | bytes 638984 | tf_op jit(solution)/shard_map/ppermute | solution.py:36
  118.8 6.3 %collective-permute-start.37 = (f32[1536]{0:T(1024)S(1)}, f32[1536]{0:T(1024)S(1)}, u32[]{:S(2)}, u32[]{:S(2)}) collective-permute-start(f32[1536]{0:T(1024)S(1)} %add.703), channel_id=1, source_target_pairs={{0,4},{1,5},{2,6},{3,7},{4,0},{5,1},{6,2},{7,3},{8,12},{9,13},{10,... | collective-permute-start | bytes 18440 | tf_op jit(solution)/shard_map/ppermute | solution.py:17
  122.5 4.8 %collective-permute-start.35 = (bf16[32,1664]{1,0:T(8,128)(2,1)S(1)}, bf16[32,1664]{1,0:T(8,128)(2,1)S(1)}, u32[]{:S(2)}, u32[]{:S(2)}) collective-permute-start(bf16[32,1664]{1,0:T(8,128)(2,1)S(1)} %fusion.61), channel_id=1, source_target_pairs={{0,4},{1,5},{2,6},{3,7},{4,0},{5,1},{6,2},{7,3},{8,12},{9,13},{10,... | collective-permute-start | bytes 319496 | tf_op jit(solution)/shard_map/ppermute | solution.py:17
  124.7 4.8 %collective-permute-start.33 = (bf16[32,1664]{1,0:T(8,128)(2,1)S(1)}, bf16[32,1664]{1,0:T(8,128)(2,1)S(1)}, u32[]{:S(2)}, u32[]{:S(2)}) collective-permute-start(bf16[32,1664]{1,0:T(8,128)(2,1)S(1)} %fusion.60), channel_id=1, source_target_pairs={{0,4},{1,5},{2,6},{3,7},{4,0},{5,1},{6,2},{7,3},{8,12},{9,13},{10,... | collective-permute-start | bytes 319496 | tf_op jit(solution)/shard_map/ppermute | solution.py:17
  (6 other events, 16.6 us)
